TPU v7x, 128 devices: a whole 4x4x4 slice. The times are simulated.
128 devices in a mesh: region: 16 (over z, y), sub: 8 (over x, core).
Axes of the slice: x: 4, y: 4, z: 4, core: 2. Of those that a mesh axis runs over, the one named last changes fastest.
Arguments:
- mass_field: float32 [96, 393216], P(None, ('region', 'sub')), may hold values from -6 to 6
- normal_wind: float32 [96, 589824], P(None, ('region', 'sub')), may hold values from -6 to 6
- tracer_ratio: float32 [96, 393216], P(None, ('region', 'sub')), may hold values from 0.2 to 2
- gradient_weights: float32 [4608, 3, 128, 128], P(('region', 'sub')), may hold values from -0.3125 to 0.3125
- divergence_weights: float32 [3072, 4, 128, 128], P(('region', 'sub')), may hold values from -0.25 to 0.25
- vertical_inverse: float32 [3072, 96, 96], P(('region', 'sub')), may hold values from -1 to 1
- gradient_pattern: int32 [4608, 3], P(('region', 'sub')), may hold values from 0 to 39, as said below
- divergence_pattern: int32 [3072, 4], P(('region', 'sub')), may hold values from 0 to 51, as said below
- edge_cells: int32 [2, 851968], P(None, ('region', 'sub')), may hold values from 0 to 6143, as said below
- cell_sends: int32 [128, 16], P(('region', 'sub')), may hold values from -1 to 23, as said below
- edge_sends: int32 [128, 16], P(('region', 'sub')), may hold values from -1 to 35, as said below
- wide_sends: int32 [128, 24], P(('region', 'sub')), may hold values from -1 to 23, as said below
Outputs:
- mass_final: float32 [96, 393216], P(None, ('region', 'sub'))
- wind_final: float32 [96, 589824], P(None, ('region', 'sub'))
- tracer_final: float32 [96, 393216], P(None, ('region', 'sub'))
Inputs may be any that keep to these rules, and one draw needn't show every extreme that they name: `cell_sends`: -1 marks an empty slot, any other entry one of the device's own 24 blocks; every device sends nothing to its own sub-region nor past the first or last region, fills all slots for one other sub-region and for one neighbouring region, and at least one slot for every other peer that exists. `edge_sends`: as for cell_sends, with blocks of the device's own 36 edge blocks. `wide_sends`: as for cell_sends, with the tracer's 24 blocks. `gradient_pattern`: the first entry of each row is one of the device's own blocks; every block of the extended cell set appears somewhere on each device. `divergence_pattern`: every block of the extended edge set appears somewhere on each device. `edge_cells`: cell numbers within the device's extended tracer set; every such cell appears on each device.
All inputs are finite; a program needn't handle non-finite values.
Results may differ from a plain program's by a relative error of at most 0.0003.
Values sent between devices are 32-bit elements; how exact they have to be, the bound alone decides.
No kernel may reach another device: no remote copies, remote signals or barrier semaphores. Data moves between devices by JAX's collectives and lax.ppermute only.
A program may use at most 128 MiB of HBM per device.

v0:
```python
import jax
import jax.numpy as jnp
from jax import lax
from jax.sharding import PartitionSpec as P

BLOCK = 128
SS = 1
SR = 4
ES = 1
ER = 4
WS = 1
WR = 8
SUBSTEPS = 5


time_step = 0.25
tracer_step = 0.5


def shifted(value, axis, steps):
    count = lax.axis_size(axis)
    initial, last = (max(0, -steps), min(count, count - steps))
    return lax.ppermute(value, axis, [(source, source + steps) for source in range(initial, last)])


def to_blocks(field):
    levels = field.shape[0]
    return jnp.transpose(field.reshape(levels, -1, BLOCK), (1, 0, 2))


def from_blocks(blocks):
    levels = blocks.shape[1]
    return jnp.transpose(blocks, (1, 0, 2)).reshape(levels, -1)


def outgoing(blocks, send_list, per_peer, per_side):
    wanted = send_list[0]
    is_live = (wanted >= 0).astype(blocks.dtype)
    picked_blocks = jnp.take(blocks, jnp.maximum(wanted, 0), axis=0) * is_live[:, None, None]
    split_at = lax.axis_size("sub") * per_peer
    lateral = picked_blocks[:split_at]
    to_next = picked_blocks[split_at : split_at + per_side]
    to_prev = picked_blocks[split_at + per_side :]
    return (lateral, to_next, to_prev)


def joined(blocks, lateral_in, from_prev, from_next):
    return jnp.concatenate([blocks, lateral_in, from_prev, from_next], axis=0)


def cell_rim(blocks, send_list):
    lateral, to_next, to_prev = outgoing(blocks, send_list, SS, SR)
    lateral_in = lax.all_to_all(lateral, "sub", split_axis=0, concat_axis=0, tiled=True)
    from_prev = shifted(to_next, "region", 1)
    from_next = shifted(to_prev, "region", -1)
    return joined(blocks, lateral_in, from_prev, from_next)


def edge_rim(blocks, send_list):
    lateral, to_next, to_prev = outgoing(blocks, send_list, ES, ER)
    lateral_in = lax.all_to_all(lateral, "sub", split_axis=0, concat_axis=0, tiled=True)
    from_prev = shifted(to_next, "region", 1)
    from_next = shifted(to_prev, "region", -1)
    return joined(blocks, lateral_in, from_prev, from_next)


def tracer_rim(blocks, send_list):
    lateral, to_next, to_prev = outgoing(blocks, send_list, WS, WR)
    lateral_in = lax.all_to_all(lateral, "sub", split_axis=0, concat_axis=0, tiled=True)
    from_prev = shifted(to_next, "region", 1)
    from_next = shifted(to_prev, "region", -1)
    return joined(blocks, lateral_in, from_prev, from_next)


def block_product(rimmed, pattern, weights):
    gathered = jnp.take(rimmed, pattern, axis=0)
    return jnp.einsum("nklc,nkcj->nlj", gathered, weights, precision=lax.Precision.HIGHEST)


def vertical(pending, inverse):
    return jnp.einsum("blm,bmj->blj", inverse, pending, precision=lax.Precision.HIGHEST)


def body(
    mass_field,
    normal_wind,
    tracer_ratio,
    gradient_weights,
    divergence_weights,
    vertical_inverse,
    gradient_pattern,
    divergence_pattern,
    edge_cells,
    cell_sends,
    edge_sends,
    wide_sends,
):
    levels = mass_field.shape[0]
    mass_now = to_blocks(mass_field)
    wind_now = to_blocks(normal_wind)
    tracer_blocks = to_blocks(tracer_ratio)
    edge_blocks = wind_now.shape[0] + lax.axis_size("sub") * ES + 2 * ER
    wind_total = jnp.zeros((edge_blocks, levels, BLOCK), jnp.float32)
    cells_rimmed = cell_rim(mass_now, cell_sends)
    for substep in range(SUBSTEPS):
        if substep > 0:
            cells_rimmed = cell_rim(mass_now, cell_sends)
        wind_now = wind_now - time_step * block_product(
            cells_rimmed, gradient_pattern, gradient_weights
        )
        edges_rimmed = edge_rim(wind_now, edge_sends)
        wind_total = wind_total + edges_rimmed
        pending = mass_now - time_step * block_product(
            edges_rimmed, divergence_pattern, divergence_weights
        )
        mass_now = vertical(pending, vertical_inverse)
    tracer_rimmed = tracer_rim(tracer_blocks, wide_sends)
    tracer_cells = from_blocks(tracer_rimmed)
    edge_tracer = 0.5 * (
        jnp.take(tracer_cells, edge_cells[0], axis=1)
        + jnp.take(tracer_cells, edge_cells[1], axis=1)
    )
    tracer_flux = wind_total / SUBSTEPS * to_blocks(edge_tracer)
    tracer_final = tracer_blocks - tracer_step * block_product(
        tracer_flux, divergence_pattern, divergence_weights
    )
    return (from_blocks(mass_now), from_blocks(wind_now), from_blocks(tracer_final))


def solution(mesh):
    return jax.shard_map(
        body,
        mesh=mesh,
        in_specs=(
            P(None, ("region", "sub")),
            P(None, ("region", "sub")),
            P(None, ("region", "sub")),
            P(("region", "sub"), None, None, None),
            P(("region", "sub"), None, None, None),
            P(("region", "sub"), None, None),
            P(("region", "sub"), None),
            P(("region", "sub"), None),
            P(None, ("region", "sub")),
            P(("region", "sub"), None),
            P(("region", "sub"), None),
            P(("region", "sub"), None),
        ),
        out_specs=(
            P(None, ("region", "sub")),
            P(None, ("region", "sub")),
            P(None, ("region", "sub")),
        ),
        check_vma=False,
    )
```

profile of v0, /device:TPU:88, one launch (start us, length us, event | category | flops | bytes accessed | tf_op | source)
XLA Modules:
  0.0 524.4 jit_solution(7313727432194823143)
XLA Ops:
  42.9 10.0 %fusion.45 = (f32[36,96,128]{2,1,0:T(8,128)S(1)}, f32[36,96,128,1]{2,1,3,0:T(8,128)}) fusion(f32[36,3,128,128]{3,2,1,0:T(8,128)} %param.25, f32[36,3,96,128]{3,2,1,0:T(8,128)} %bitcast.243, pred[36,3]{1,0:T(8,128)(4,1)S(1)} %copy.73, f32[96,4608]{1,0:T(8,128)S(1)} %copy-done), kind=kOutput, calls=%fused_computation.85 | convolution fusion | flops 2040643584 | bytes 17694828 | tf_op jit(solution)/shard_map/nklc,nkcj->nlj/dot_general | solution.py:77
  66.0 6.2 %collective-permute-start.2 = (f32[4,96,128]{2,1,0:T(8,128)}, f32[4,96,128]{2,1,0:T(8,128)}, u32[]{:S(2)}, u32[]{:S(2)}) collective-permute-start(f32[4,96,128]{2,1,0:T(8,128)} %get-tuple-element.33), channel_id=1, source_target_pairs={{0,8},{8,16},{16,24},{24,32},{32,40},{40,48},{48,56},{56,64},{64,7... | collective-permute-start | bytes 589832 | tf_op jit(solution)/shard_map/ppermute | solution.py:23
  84.5 9.9 %fusion.112 = f32[24,96,128]{2,1,0:T(8,128)S(1)} fusion(f32[24,4,128,128]{3,2,1,0:T(8,128)} %param.26, f32[24,4,96,128]{3,2,1,0:T(8,128)} %bitcast.252, pred[24,4]{1,0:T(8,128)(4,1)} %copy.71, f32[96,3072]{1,0:T(8,128)} %param.22), kind=kOutput, calls=%fused_computation.124 | convolution fusion | flops 1813708800 | bytes 13369440 | tf_op jit(solution)/shard_map/nklc,nkcj->nlj/dot_general | solution.py:77
  110.0 6.9 %collective-permute-start.4 = (f32[4,96,128]{2,1,0:T(8,128)S(1)}, f32[4,96,128]{2,1,0:T(8,128)}, u32[]{:S(2)}, u32[]{:S(2)}) collective-permute-start(f32[4,96,128]{2,1,0:T(8,128)S(1)} %get-tuple-element.31), channel_id=1, source_target_pairs={{0,8},{8,16},{16,24},{24,32},{32,40},{40,48},{48,56},{56,64},{64,7... | collective-permute-start | bytes 589832 | tf_op jit(solution)/shard_map/ppermute | solution.py:23
  129.1 10.3 %fusion.51 = (f32[36,96,128]{2,1,0:T(8,128)}, f32[36,96,128,1]{2,1,3,0:T(8,128)}) fusion(f32[36,96,128]{2,1,0:T(8,128)S(1)} %get-tuple-element.39, f32[36,3,128,128]{3,2,1,0:T(8,128)} %param.25, f32[36,3,96,128]{3,2,1,0:T(8,128)} %bitcast.244, pred[36,3]{1,0:T(8,128)(4,1)S(1)} %copy.73), kind=kOutput, calls=%fused_computation.96 | convolution fusion | flops 2040643584 | bytes 17694828 | tf_op jit(solution)/shard_map/nklc,nkcj->nlj/dot_general | solution.py:77
  172.6 9.9 %fusion.106 = f32[24,96,128]{2,1,0:T(8,128)S(1)} fusion(f32[24,96,128]{2,1,0:T(8,128)} %convolution_bitcast_fusion.4, f32[24,4,128,128]{3,2,1,0:T(8,128)} %param.26, f32[24,4,96,128]{3,2,1,0:T(8,128)} %bitcast.248, pred[24,4]{1,0:T(8,128)(4,1)} %copy.71), kind=kOutput, calls=%fused_computation.122 | convolution fusion | flops 1813708800 | bytes 13369440 | tf_op jit(solution)/shard_map/nklc,nkcj->nlj/dot_general | solution.py:77
  193.0 6.0 %collective-permute-start.8 = (f32[4,96,128]{2,1,0:T(8,128)}, f32[4,96,128]{2,1,0:T(8,128)}, u32[]{:S(2)}, u32[]{:S(2)}) collective-permute-start(f32[4,96,128]{2,1,0:T(8,128)} %get-tuple-element.27), channel_id=1, source_target_pairs={{0,8},{8,16},{16,24},{24,32},{32,40},{40,48},{48,56},{56,64},{64,7... | collective-permute-start | bytes 589832 | tf_op jit(solution)/shard_map/ppermute | solution.py:23
  207.7 6.2 %collective-permute-start.20 = (f32[8,96,128]{2,1,0:T(8,128)}, f32[8,96,128]{2,1,0:T(8,128)}, u32[]{:S(2)}, u32[]{:S(2)}) collective-permute-start(f32[8,96,128]{2,1,0:T(8,128)} %get-tuple-element.16), channel_id=1, source_target_pairs={{0,8},{8,16},{16,24},{24,32},{32,40},{40,48},{48,56},{56,64},{64,7... | collective-permute-start | bytes 1179656 | tf_op jit(solution)/shard_map/ppermute | solution.py:23
  222.5 10.5 %fusion.52 = (f32[36,96,128]{2,1,0:T(8,128)}, f32[36,96,128,1]{2,1,3,0:T(8,128)}) fusion(f32[36,96,128]{2,1,0:T(8,128)} %get-tuple-element.41, f32[36,3,128,128]{3,2,1,0:T(8,128)} %param.25, f32[36,3,96,128]{3,2,1,0:T(8,128)} %bitcast.245, pred[36,3]{1,0:T(8,128)(4,1)S(1)} %copy.73), kind=kOutput, calls=%fused_computation.97 | convolution fusion | flops 2040643584 | bytes 17694828 | tf_op jit(solution)/shard_map/nklc,nkcj->nlj/dot_general | solution.py:77
  246.8 6.0 %collective-permute-start.10 = (f32[4,96,128]{2,1,0:T(8,128)S(1)}, f32[4,96,128]{2,1,0:T(8,128)}, u32[]{:S(2)}, u32[]{:S(2)}) collective-permute-start(f32[4,96,128]{2,1,0:T(8,128)S(1)} %get-tuple-element.25), channel_id=1, source_target_pairs={{0,8},{8,16},{16,24},{24,32},{32,40},{40,48},{48,56},{56,64},{64,7... | collective-permute-start | bytes 589832 | tf_op jit(solution)/shard_map/ppermute | solution.py:23
  265.6 9.9 %fusion.100 = f32[24,96,128]{2,1,0:T(8,128)S(1)} fusion(f32[24,96,128]{2,1,0:T(8,128)} %convolution_bitcast_fusion.3, f32[24,4,128,128]{3,2,1,0:T(8,128)} %param.26, f32[24,4,96,128]{3,2,1,0:T(8,128)} %bitcast.249, pred[24,4]{1,0:T(8,128)(4,1)} %copy.71), kind=kOutput, calls=%fused_computation.120 | convolution fusion | flops 1813708800 | bytes 13369440 | tf_op jit(solution)/shard_map/nklc,nkcj->nlj/dot_general | solution.py:77
  291.8 6.6 %collective-permute-start.12 = (f32[4,96,128]{2,1,0:T(8,128)}, f32[4,96,128]{2,1,0:T(8,128)}, u32[]{:S(2)}, u32[]{:S(2)}) collective-permute-start(f32[4,96,128]{2,1,0:T(8,128)} %get-tuple-element.23), channel_id=1, source_target_pairs={{0,8},{8,16},{16,24},{24,32},{32,40},{40,48},{48,56},{56,64},{64,7... | collective-permute-start | bytes 589832 | tf_op jit(solution)/shard_map/ppermute | solution.py:23
  312.9 10.6 %fusion.53 = (f32[36,96,128]{2,1,0:T(8,128)}, f32[36,96,128,1]{2,1,3,0:T(8,128)}) fusion(f32[36,96,128]{2,1,0:T(8,128)} %get-tuple-element.43, f32[36,3,128,128]{3,2,1,0:T(8,128)} %param.25, f32[36,3,96,128]{3,2,1,0:T(8,128)} %bitcast.246, pred[36,3]{1,0:T(8,128)(4,1)S(1)} %copy.73), kind=kOutput, calls=%fused_computation.98 | convolution fusion | flops 2040643584 | bytes 17694828 | tf_op jit(solution)/shard_map/nklc,nkcj->nlj/dot_general | solution.py:77
  338.1 6.0 %collective-permute-start.14 = (f32[4,96,128]{2,1,0:T(8,128)}, f32[4,96,128]{2,1,0:T(8,128)}, u32[]{:S(2)}, u32[]{:S(2)}) collective-permute-start(f32[4,96,128]{2,1,0:T(8,128)} %get-tuple-element.21), channel_id=1, source_target_pairs={{0,8},{8,16},{16,24},{24,32},{32,40},{40,48},{48,56},{56,64},{64,7... | collective-permute-start | bytes 589832 | tf_op jit(solution)/shard_map/ppermute | solution.py:23
  352.1 16.1 %gather_fusion.22 = f32[6656,96]{1,0:T(8,128)} fusion(f32[96,6144]{0,1:T(8,128)} %bitcast.240, s32[7168]{0:T(1024)} %pad_clamp_fusion), kind=kCustom, calls=%fused_computation.22.clone | custom fusion | bytes 5138432 | tf_op jit(solution)/shard_map/jit(_take)/gather | solution.py:121
  368.2 16.1 %gather_fusion.21 = f32[6656,96]{1,0:T(8,128)} fusion(f32[96,6144]{0,1:T(8,128)} %bitcast.241, s32[7168]{0:T(1024)} %pad_clamp_fusion.1), kind=kCustom, calls=%fused_computation.4.clone | custom fusion | bytes 5138432 | tf_op jit(solution)/shard_map/jit(_take)/gather | solution.py:120
  392.5 9.9 %fusion.94 = f32[24,96,128]{2,1,0:T(8,128)S(1)} fusion(f32[24,96,128]{2,1,0:T(8,128)} %convolution_bitcast_fusion.2, f32[24,4,128,128]{3,2,1,0:T(8,128)} %param.26, f32[24,4,96,128]{3,2,1,0:T(8,128)} %bitcast.250, pred[24,4]{1,0:T(8,128)(4,1)} %copy.71), kind=kOutput, calls=%fused_computation.118 | convolution fusion | flops 1813708800 | bytes 13369440 | tf_op jit(solution)/shard_map/nklc,nkcj->nlj/dot_general | solution.py:77
  412.2 6.0 %collective-permute-start.16 = (f32[4,96,128]{2,1,0:T(8,128)}, f32[4,96,128]{2,1,0:T(8,128)}, u32[]{:S(2)}, u32[]{:S(2)}) collective-permute-start(f32[4,96,128]{2,1,0:T(8,128)} %get-tuple-element.19), channel_id=1, source_target_pairs={{0,8},{8,16},{16,24},{24,32},{32,40},{40,48},{48,56},{56,64},{64,7... | collective-permute-start | bytes 589832 | tf_op jit(solution)/shard_map/ppermute | solution.py:23
  423.1 8.4 %fusion.22 = f32[96,6656]{0,1:T(8,128)} fusion(f32[6656,96]{1,0:T(8,128)} %gather_fusion.22, f32[6656,96]{1,0:T(8,128)} %gather_fusion.21, pred[6656]{0:T(1024)(128)(4,1)} %get-tuple-element.51, pred[6656]{0:T(1024)(128)(4,1)} %get-tuple-element.52), kind=kLoop, calls=%fused_computation.47 | loop fusion | flops 2555904 | bytes 7681024 | tf_op jit(solution)/shard_map/mul | solution.py:119
  442.9 10.5 %fusion.54 = (f32[36,96,128]{2,1,0:T(8,128)}, f32[36,96,128,1]{2,1,3,0:T(8,128)}) fusion(f32[36,96,128]{2,1,0:T(8,128)} %get-tuple-element.45, f32[36,3,128,128]{3,2,1,0:T(8,128)} %param.25, f32[36,3,96,128]{3,2,1,0:T(8,128)} %bitcast.242, pred[36,3]{1,0:T(8,128)(4,1)S(1)} %copy.73), kind=kOutput, calls=%fused_computation.99 | convolution fusion | flops 2040643584 | bytes 17694828 | tf_op jit(solution)/shard_map/nklc,nkcj->nlj/dot_general | solution.py:77
  461.3 6.0 %collective-permute-start.18 = (f32[4,96,128]{2,1,0:T(8,128)}, f32[4,96,128]{2,1,0:T(8,128)}, u32[]{:S(2)}, u32[]{:S(2)}) collective-permute-start(f32[4,96,128]{2,1,0:T(8,128)} %get-tuple-element.17), channel_id=1, source_target_pairs={{0,8},{8,16},{16,24},{24,32},{32,40},{40,48},{48,56},{56,64},{64,7... | collective-permute-start | bytes 589832 | tf_op jit(solution)/shard_map/ppermute | solution.py:23
  489.6 9.9 %fusion.88 = f32[24,96,128]{2,1,0:T(8,128)S(1)} fusion(f32[24,96,128]{2,1,0:T(8,128)} %convolution_bitcast_fusion.1, f32[24,4,128,128]{3,2,1,0:T(8,128)} %param.26, f32[24,4,96,128]{3,2,1,0:T(8,128)} %bitcast.251, pred[24,4]{1,0:T(8,128)(4,1)S(1)} %copy-done.19), kind=kOutput, calls=%fused_computation.116 | convolution fusion | flops 1813708800 | bytes 13369440 | tf_op jit(solution)/shard_map/nklc,nkcj->nlj/dot_general | solution.py:77
  502.8 7.2 %bitcast_multiply_fusion = f32[52,96,128]{2,1,0:T(8,128)} fusion(f32[96,52,128]{2,0,1:T(8,128)S(1)} %copy-done.10, f32[4,96,128]{2,1,0:T(8,128)} %collective-permute-done.19, f32[4,96,128]{2,1,0:T(8,128)} %collective-permute-done.18, f32[8,96,128]{2,1,0:T(8,128)} %all-to-all-done.9, f32[36,96,128]{2,1,0:T(8,128)S(1)} %copy-done.9, ...), kind=kLoop, calls=%fused_computation.63 | loop fusion | flops 13418496 | bytes 17891328 | tf_op jit(solution)/shard_map/mul | solution.py:123
  514.8 8.2 %fusion.82 = f32[24,12,8,128]{3,2,1,0:T(8,128)S(1)} fusion(f32[24,4,128,128]{3,2,1,0:T(8,128)} %param.26, f32[24,4,96,128]{3,2,1,0:T(8,128)} %bitcast.247, pred[24,4]{1,0:T(8,128)(4,1)S(1)} %copy-done.19, f32[96,3072]{1,0:T(8,128)S(1)} %copy-done.11), kind=kOutput, calls=%fused_computation.114 | convolution fusion | flops 1813708800 | bytes 13369440 | tf_op jit(solution)/shard_map/nklc,nkcj->nlj/dot_general | solution.py:77
  (216 shorter events, 309.5 us)
Async XLA Ops:
  7.1 28.6 %collective-permute-start.1 = (f32[4,96,128]{2,1,0:T(8,128)}, f32[4,96,128]{2,1,0:T(8,128)}, u32[]{:S(2)}, u32[]{:S(2)}) collective-permute-start(f32[4,96,128]{2,1,0:T(8,128)} %get-tuple-element.36), channel_id=1, source_target_pairs={{8,0},{16,8},{24,16},{32,24},{40,32},{48,40},{56,48},{64,56},{72,6... | collective-permute-start | bytes 589832 | tf_op jit(solution)/shard_map/ppermute | solution.py:23
  9.7 26.0 %collective-permute-start = (f32[4,96,128]{2,1,0:T(8,128)S(1)}, f32[4,96,128]{2,1,0:T(8,128)}, u32[]{:S(2)}, u32[]{:S(2)}) collective-permute-start(f32[4,96,128]{2,1,0:T(8,128)S(1)} %get-tuple-element.35), channel_id=1, source_target_pairs={{0,8},{8,16},{16,24},{24,32},{32,40},{40,48},{48,56},{56,64},{64,7... | collective-permute-start | bytes 589832 | tf_op jit(solution)/shard_map/ppermute | solution.py:23
  15.8 19.9 %all-to-all-start = ((f32[8,96,128]{2,1,0:T(8,128)}), f32[8,96,128]{2,1,0:T(8,128)S(1)}, u32[]{:S(2)}, u32[]{:S(2)}) async-start(f32[8,96,128]{2,1,0:T(8,128)} %slice.188), calls=%async_computation | async-start | bytes 786432 | tf_op jit(solution)/shard_map/all_to_all | solution.py:53
  57.5 19.4 %all-to-all-start.1 = ((f32[8,96,128]{2,1,0:T(8,128)}), f32[8,96,128]{2,1,0:T(8,128)}, u32[]{:S(2)}, u32[]{:S(2)}) async-start(f32[8,96,128]{2,1,0:T(8,128)} %slice.191), calls=%async_computation.1 | async-start | bytes 786432 | tf_op jit(solution)/shard_map/all_to_all | solution.py:61
  102.5 18.8 %all-to-all-start.2 = ((f32[8,96,128]{2,1,0:T(8,128)}), f32[8,96,128]{2,1,0:T(8,128)}, u32[]{:S(2)}, u32[]{:S(2)}) async-start(f32[8,96,128]{2,1,0:T(8,128)} %slice.194), calls=%async_computation.2 | async-start | bytes 786432 | tf_op jit(solution)/shard_map/all_to_all | solution.py:53
  145.5 18.9 %all-to-all-start.3 = ((f32[8,96,128]{2,1,0:T(8,128)}), f32[8,96,128]{2,1,0:T(8,128)}, u32[]{:S(2)}, u32[]{:S(2)}) async-start(f32[8,96,128]{2,1,0:T(8,128)} %slice.197), calls=%async_computation.3 | async-start | bytes 786432 | tf_op jit(solution)/shard_map/all_to_all | solution.py:61
  190.4 24.2 %collective-permute-start.9 = (f32[4,96,128]{2,1,0:T(8,128)}, f32[4,96,128]{2,1,0:T(8,128)}, u32[]{:S(2)}, u32[]{:S(2)}) collective-permute-start(f32[4,96,128]{2,1,0:T(8,128)} %get-tuple-element.28), channel_id=1, source_target_pairs={{8,0},{16,8},{24,16},{32,24},{40,32},{48,40},{56,48},{64,56},{72,6... | collective-permute-start | bytes 589832 | tf_op jit(solution)/shard_map/ppermute | solution.py:23
  193.0 21.7 %collective-permute-start.8 = (f32[4,96,128]{2,1,0:T(8,128)}, f32[4,96,128]{2,1,0:T(8,128)}, u32[]{:S(2)}, u32[]{:S(2)}) collective-permute-start(f32[4,96,128]{2,1,0:T(8,128)} %get-tuple-element.27), channel_id=1, source_target_pairs={{0,8},{8,16},{16,24},{24,32},{32,40},{40,48},{48,56},{56,64},{64,7... | collective-permute-start | bytes 589832 | tf_op jit(solution)/shard_map/ppermute | solution.py:23
  199.0 15.7 %all-to-all-start.4 = ((f32[8,96,128]{2,1,0:T(8,128)}), f32[8,96,128]{2,1,0:T(8,128)}, u32[]{:S(2)}, u32[]{:S(2)}) async-start(f32[8,96,128]{2,1,0:T(8,128)} %slice.200), calls=%async_computation.4 | async-start | bytes 786432 | tf_op jit(solution)/shard_map/all_to_all | solution.py:53
  205.7 139.7 %collective-permute-start.21 = (f32[8,96,128]{2,1,0:T(8,128)}, f32[8,96,128]{2,1,0:T(8,128)}, u32[]{:S(2)}, u32[]{:S(2)}) collective-permute-start(f32[8,96,128]{2,1,0:T(8,128)} %get-tuple-element.15), channel_id=1, source_target_pairs={{8,0},{16,8},{24,16},{32,24},{40,32},{48,40},{56,48},{64,56},{72,6... | collective-permute-start | bytes 1179656 | tf_op jit(solution)/shard_map/ppermute | solution.py:23
  207.7 137.8 %collective-permute-start.20 = (f32[8,96,128]{2,1,0:T(8,128)}, f32[8,96,128]{2,1,0:T(8,128)}, u32[]{:S(2)}, u32[]{:S(2)}) collective-permute-start(f32[8,96,128]{2,1,0:T(8,128)} %get-tuple-element.16), channel_id=1, source_target_pairs={{0,8},{8,16},{16,24},{24,32},{32,40},{40,48},{48,56},{56,64},{64,7... | collective-permute-start | bytes 1179656 | tf_op jit(solution)/shard_map/ppermute | solution.py:23
  239.0 18.3 %all-to-all-start.5 = ((f32[8,96,128]{2,1,0:T(8,128)}), f32[8,96,128]{2,1,0:T(8,128)}, u32[]{:S(2)}, u32[]{:S(2)}) async-start(f32[8,96,128]{2,1,0:T(8,128)} %slice.203), calls=%async_computation.5 | async-start | bytes 786432 | tf_op jit(solution)/shard_map/all_to_all | solution.py:61
  283.6 16.2 %all-to-all-start.6 = ((f32[8,96,128]{2,1,0:T(8,128)}), f32[8,96,128]{2,1,0:T(8,128)}, u32[]{:S(2)}, u32[]{:S(2)}) async-start(f32[8,96,128]{2,1,0:T(8,128)} %slice.206), calls=%async_computation.6 | async-start | bytes 786432 | tf_op jit(solution)/shard_map/all_to_all | solution.py:53
  289.8 15.2 %collective-permute-start.13 = (f32[4,96,128]{2,1,0:T(8,128)}, f32[4,96,128]{2,1,0:T(8,128)}, u32[]{:S(2)}, u32[]{:S(2)}) collective-permute-start(f32[4,96,128]{2,1,0:T(8,128)} %get-tuple-element.24), channel_id=1, source_target_pairs={{8,0},{16,8},{24,16},{32,24},{40,32},{48,40},{56,48},{64,56},{72,6... | collective-permute-start | bytes 589832 | tf_op jit(solution)/shard_map/ppermute | solution.py:23
  299.8 29.7 %all-to-all-start.10 = ((f32[8,96,128]{2,1,0:T(8,128)}), f32[8,96,128]{2,1,0:T(8,128)}, u32[]{:S(2)}, u32[]{:S(2)}) async-start(f32[8,96,128]{2,1,0:T(8,128)} %get-tuple-element.14), calls=%async_computation.10 | async-start | bytes 786432 | tf_op jit(solution)/shard_map/all_to_all | solution.py:69
  329.5 54.8 %all-to-all-start.7 = ((f32[8,96,128]{2,1,0:T(8,128)}), f32[8,96,128]{2,1,0:T(8,128)}, u32[]{:S(2)}, u32[]{:S(2)}) async-start(f32[8,96,128]{2,1,0:T(8,128)} %slice.209), calls=%async_computation.7 | async-start | bytes 786432 | tf_op jit(solution)/shard_map/all_to_all | solution.py:61
  336.2 48.1 %collective-permute-start.15 = (f32[4,96,128]{2,1,0:T(8,128)}, f32[4,96,128]{2,1,0:T(8,128)}, u32[]{:S(2)}, u32[]{:S(2)}) collective-permute-start(f32[4,96,128]{2,1,0:T(8,128)} %get-tuple-element.22), channel_id=1, source_target_pairs={{8,0},{16,8},{24,16},{32,24},{40,32},{48,40},{56,48},{64,56},{72,6... | collective-permute-start | bytes 589832 | tf_op jit(solution)/shard_map/ppermute | solution.py:23
  338.1 46.2 %collective-permute-start.14 = (f32[4,96,128]{2,1,0:T(8,128)}, f32[4,96,128]{2,1,0:T(8,128)}, u32[]{:S(2)}, u32[]{:S(2)}) collective-permute-start(f32[4,96,128]{2,1,0:T(8,128)} %get-tuple-element.21), channel_id=1, source_target_pairs={{0,8},{8,16},{16,24},{24,32},{32,40},{40,48},{48,56},{56,64},{64,7... | collective-permute-start | bytes 589832 | tf_op jit(solution)/shard_map/ppermute | solution.py:23
  410.3 24.8 %collective-permute-start.17 = (f32[4,96,128]{2,1,0:T(8,128)}, f32[4,96,128]{2,1,0:T(8,128)}, u32[]{:S(2)}, u32[]{:S(2)}) collective-permute-start(f32[4,96,128]{2,1,0:T(8,128)} %get-tuple-element.20), channel_id=1, source_target_pairs={{8,0},{16,8},{24,16},{32,24},{40,32},{48,40},{56,48},{64,56},{72,6... | collective-permute-start | bytes 589832 | tf_op jit(solution)/shard_map/ppermute | solution.py:23
  412.2 22.9 %collective-permute-start.16 = (f32[4,96,128]{2,1,0:T(8,128)}, f32[4,96,128]{2,1,0:T(8,128)}, u32[]{:S(2)}, u32[]{:S(2)}) collective-permute-start(f32[4,96,128]{2,1,0:T(8,128)} %get-tuple-element.19), channel_id=1, source_target_pairs={{0,8},{8,16},{16,24},{24,32},{32,40},{40,48},{48,56},{56,64},{64,7... | collective-permute-start | bytes 589832 | tf_op jit(solution)/shard_map/ppermute | solution.py:23
  418.3 16.9 %all-to-all-start.8 = ((f32[8,96,128]{2,1,0:T(8,128)}), f32[8,96,128]{2,1,0:T(8,128)}, u32[]{:S(2)}, u32[]{:S(2)}) async-start(f32[8,96,128]{2,1,0:T(8,128)} %slice.212), calls=%async_computation.8 | async-start | bytes 786432 | tf_op jit(solution)/shard_map/all_to_all | solution.py:53
  459.4 18.4 %collective-permute-start.19 = (f32[4,96,128]{2,1,0:T(8,128)}, f32[4,96,128]{2,1,0:T(8,128)}, u32[]{:S(2)}, u32[]{:S(2)}) collective-permute-start(f32[4,96,128]{2,1,0:T(8,128)} %get-tuple-element.18), channel_id=1, source_target_pairs={{8,0},{16,8},{24,16},{32,24},{40,32},{48,40},{56,48},{64,56},{72,6... | collective-permute-start | bytes 589832 | tf_op jit(solution)/shard_map/ppermute | solution.py:23
  461.3 16.4 %collective-permute-start.18 = (f32[4,96,128]{2,1,0:T(8,128)}, f32[4,96,128]{2,1,0:T(8,128)}, u32[]{:S(2)}, u32[]{:S(2)}) collective-permute-start(f32[4,96,128]{2,1,0:T(8,128)} %get-tuple-element.17), channel_id=1, source_target_pairs={{0,8},{8,16},{16,24},{24,32},{32,40},{40,48},{48,56},{56,64},{64,7... | collective-permute-start | bytes 589832 | tf_op jit(solution)/shard_map/ppermute | solution.py:23
  467.3 14.0 %all-to-all-start.9 = ((f32[8,96,128]{2,1,0:T(8,128)}), f32[8,96,128]{2,1,0:T(8,128)}, u32[]{:S(2)}, u32[]{:S(2)}) async-start(f32[8,96,128]{2,1,0:T(8,128)} %slice.215), calls=%async_computation.9 | async-start | bytes 786432 | tf_op jit(solution)/shard_map/all_to_all | solution.py:61
  (37 other events, 343.7 us)
where the time goes:
time: 534 us; the launch traced here: 524 us
  local copies, waits for them, and re-layouts  163 us (31%)
  starting transfers between devices  142 us (27%)
  matrix products  120 us (22%)
  other arithmetic  86.5 us (16%)
  waiting for transfers between devices  11.4 us (2%)
    dot_general x11, matrix products, block_product(): jnp.einsum('nklc,nkcj->nlj', gathered, weights, precision=lax.Precision.H...  110 us
    ppermute x22, starting transfers between devices, shifted(): lax.ppermute(value, axis, [(source, source + steps) for source in range(i...  90.4 us
    gather x11, local copies, waits for them, and re-layouts, block_product(): gathered = jnp.take(rimmed, pattern, axis=0)  52.4 us
    concatenate x10, other arithmetic, joined(): return jnp.concatenate([blocks, lateral_in, from_prev, from_next], axis=0)  31.3 us
    gather x11, local copies, waits for them, and re-layouts, outgoing(): jnp.take(blocks, jnp.maximum(wanted, 0), axis=0) * is_live[:, None, None]  29.8 us
    all_to_all x5, starting transfers between devices, edge_rim(): lax.all_to_all(lateral, 'sub', split_axis=0, concat_axis=0, tiled=True)  23.9 us
    all_to_all x5, starting transfers between devices, cell_rim(): lax.all_to_all(lateral, 'sub', split_axis=0, concat_axis=0, tiled=True)  22.5 us
    gather x1, local copies, waits for them, and re-layouts, body(): jnp.take(tracer_cells, edge_cells[0], axis=1)  16.1 us
  transfers between devices with their start and end apart: 33, of which 8 were waited for; matrix products, arithmetic and copies ran while one was open for 32% of the time, Pallas kernels for 0%

commit v1 on v0

v1 whole, which is shorter than its diff:
```python
import functools

import numpy as np
import jax
import jax.numpy as jnp
from jax import lax
from jax.experimental import pallas as pl
from jax.experimental.pallas import tpu as pltpu
from jax.sharding import PartitionSpec as P

BLOCK = 128
LEV = 96
NB = 24
NE = 36
KG = 3
KD = 4
SR = 4
ER = 4
WR = 8
SUBSTEPS = 5
N_REGION = 16
N_CHIP = 4
N_SUB = 8
LAT = 8

time_step = 0.25
tracer_step = 0.5

BF = jnp.bfloat16
F32 = jnp.float32

ALONG = [(2 * x + c, 2 * ((x + (1 if c == 0 else 3)) % 4) + c) for x in range(4) for c in range(2)]
ACROSS = [(2 * x + c, 2 * ((x + 2) % 4) + c) for x in range(4) for c in range(2)]
MATES = [(s, s ^ 1) for s in range(8)]


def send_order():
    rows = []
    for s in range(N_SUB):
        x, c = divmod(s, 2)
        mine = (x + (1 if c == 0 else 3)) % 4
        other = (x + (3 if c == 0 else 1)) % 4
        far = (x + 2) % 4
        o = 1 - c
        rows.append([2 * x + o, 2 * other + o, 2 * other + c, 2 * mine + c, 2 * mine + o, 2 * far + c, 2 * far + o])
    return np.array(rows, np.int32)


def lateral_place():
    rows = []
    for s in range(N_SUB):
        x, c = divmod(s, 2)
        back = 3 if c == 0 else 1
        row = []
        for p in range(N_SUB):
            px, pc = divmod(p, 2)
            d = (px - x) % 4
            same = pc == c
            if d == 0:
                row.append(7 if same else 0)
            elif d == back:
                row.append(1 if same else 2)
            elif d == 2:
                row.append(3 if same else 6)
            else:
                row.append(5 if same else 4)
        rows.append(row)
    return np.array(rows, np.int32)


def place_table(own, side):
    lat = lateral_place()
    rows = [
        np.concatenate([np.arange(own), own + lat[s], own + LAT + np.arange(2 * side)])
        for s in range(N_SUB)
    ]
    return np.stack(rows).astype(np.int32)


ORDER = send_order()


def row_of(table):
    sub = lax.axis_index("sub")
    return lax.dynamic_slice(jnp.asarray(table), (sub, 0), (1, table.shape[1]))[0]


def ring(v, step):
    return lax.ppermute(v, "region", [(s, (s + step) % N_REGION) for s in range(N_REGION)])


def exchange(sends):
    pre, along, across, to_next, to_prev = sends
    from_prev = ring(to_next, 1)
    from_next = ring(to_prev, -1)
    pre_in = lax.ppermute(pre, "sub", MATES)
    along_in = lax.ppermute(jnp.concatenate([along, pre_in[1:]], axis=0), "sub", ALONG)
    across_in = lax.ppermute(across, "sub", ACROSS)
    post = jnp.concatenate([along_in[1:2], along_in[3:4], across_in[1:2]], axis=0)
    post_in = lax.ppermute(post, "sub", MATES)
    return pre_in, along_in, across_in, post_in, from_prev, from_next


def two_parts(x):
    hi = x.astype(BF)
    lo = (x - hi.astype(F32)).astype(BF)
    return hi, lo


def split_kernel(w_ref, o_ref):
    hi, lo = two_parts(w_ref[...])
    o_ref[:, :, :BLOCK] = hi
    o_ref[:, :, BLOCK:] = lo


def split_weights(weights, per_step):
    n = weights.shape[0] * weights.shape[1]
    flat = weights.reshape(n, BLOCK, BLOCK)
    return pl.pallas_call(
        split_kernel,
        grid=(n // per_step,),
        in_specs=[pl.BlockSpec((per_step, BLOCK, BLOCK), lambda i: (i, 0, 0))],
        out_specs=pl.BlockSpec((per_step, BLOCK, 2 * BLOCK), lambda i: (i, 0, 0)),
        out_shape=jax.ShapeDtypeStruct((n, BLOCK, 2 * BLOCK), BF),
        compiler_params=pltpu.CompilerParams(vmem_limit_bytes=32 << 20),
        cost_estimate=pl.CostEstimate(flops=n * BLOCK * BLOCK * 4, bytes_accessed=n * BLOCK * BLOCK * 8, transcendentals=0),
        name="split_weights",
    )(flat)


RIM = (("pre", 0), ("along", 0), ("along", 2), ("across", 0), ("post", 0), ("post", 1), ("post", 2))


def rim_blocks(rim, side):
    pre, along, across, post, prev, nxt = rim
    by_name = dict(pre=pre, along=along, across=across, post=post)
    blocks = [(j, by_name[name], i) for j, (name, i) in enumerate(RIM)]
    blocks += [(LAT + i, prev, i) for i in range(side)]
    blocks += [(LAT + side + i, nxt, i) for i in range(side)]
    return blocks


def store_parts(ext, slot, x):
    hi, lo = two_parts(x)
    ext[slot, :LEV, :] = hi
    ext[slot, LEV:, :] = lo


def block_at(ref, b):
    return ref[:, pl.ds(pl.multiple_of(b * BLOCK, BLOCK), BLOCK)]


def fill_extended(ext, own_ref, own, rim, side):
    def one(b, _):
        store_parts(ext, b, block_at(own_ref, b))
        return 0

    lax.fori_loop(0, own, one, 0, unroll=4)
    for j, ref, i in rim_blocks(rim, side):
        store_parts(ext, own + j, ref[i])
    ext[own + LAT - 1] = jnp.zeros((2 * LEV, BLOCK), BF)


def target_product(ext, pattern, place, w_ref, base, local, width):
    xs = [ext[place[pattern[(base + local) * width + k]]] for k in range(width)]
    x = jnp.concatenate(xs, axis=1)
    w = w_ref[local * width : (local + 1) * width].reshape(width * BLOCK, 2 * BLOCK)
    y = jnp.dot(x, w, preferred_element_type=F32)
    return (y[:LEV, :BLOCK] + y[LEV:, :BLOCK]) + (y[:LEV, BLOCK:] + y[LEV:, BLOCK:])


def pick(source, entry):
    live = (entry >= 0).astype(F32)
    return source(jnp.maximum(entry, 0)) * live


def fill_sends(sends, send_list, order, source, side):
    pre, along, across, to_next, to_prev = sends
    for j in range(3):
        pre[j] = pick(source, send_list[order[j]])
    for j in range(2):
        along[j] = pick(source, send_list[order[3 + j]])
        across[j] = pick(source, send_list[order[5 + j]])
    for j in range(side):
        to_next[j] = pick(source, send_list[LAT + j])
        to_prev[j] = pick(source, send_list[LAT + side + j])


def send_shapes(side):
    return [jax.ShapeDtypeStruct((n, LEV, BLOCK), F32) for n in (3, 2, 2, side, side)]


def whole(shape):
    return pl.BlockSpec(shape, lambda *_: (0,) * len(shape))


def send_specs(side):
    return [whole((n, LEV, BLOCK)) for n in (3, 2, 2, side, side)]


def rim_specs(side):
    return [whole((n, LEV, BLOCK)) for n in (3, 4, 2, 3, side, side)]


def first_kernel(send_list, order, field_ref, *sends, side):
    fill_sends(sends, send_list, order, lambda b: block_at(field_ref, b), side)


def first_sends(field, send_list, order, side):
    return pl.pallas_call(
        functools.partial(first_kernel, side=side),
        grid_spec=pltpu.PrefetchScalarGridSpec(
            num_scalar_prefetch=2,
            grid=(1,),
            in_specs=[whole(field.shape)],
            out_specs=send_specs(side),
        ),
        out_shape=send_shapes(side),
        compiler_params=pltpu.CompilerParams(vmem_limit_bytes=32 << 20),
        name="first_sends",
    )(send_list, order, field)


G_STEP = 6


def gradient_kernel(pattern, place, send_list, order, mass_ref, wind_ref, w_ref, *refs):
    rim, out_ref, sends, ext, keep = refs[:6], refs[6], refs[7:12], refs[12], refs[13]
    step = pl.program_id(0)

    @pl.when(step == 0)
    def _():
        fill_extended(ext, mass_ref, NB, rim, SR)

    base = step * G_STEP
    for j in range(G_STEP):
        p = target_product(ext, pattern, place, w_ref, base, j, KG)
        new = wind_ref[:, j * BLOCK : (j + 1) * BLOCK] - time_step * p
        out_ref[:, j * BLOCK : (j + 1) * BLOCK] = new
        keep[base + j] = new

    @pl.when(step == NE // G_STEP - 1)
    def _():
        fill_sends(sends, send_list, order, lambda b: keep[b], ER)


def gradient(info, mass, wind, weights, rim):
    steps = NE // G_STEP
    out = pl.pallas_call(
        gradient_kernel,
        grid_spec=pltpu.PrefetchScalarGridSpec(
            num_scalar_prefetch=4,
            grid=(steps,),
            in_specs=[
                whole(mass.shape),
                pl.BlockSpec((LEV, G_STEP * BLOCK), lambda i, *_: (0, i)),
                pl.BlockSpec((G_STEP * KG, BLOCK, 2 * BLOCK), lambda i, *_: (i, 0, 0)),
                *rim_specs(SR),
            ],
            out_specs=[pl.BlockSpec((LEV, G_STEP * BLOCK), lambda i, *_: (0, i)), *send_specs(ER)],
            scratch_shapes=[
                pltpu.VMEM((NB + LAT + 2 * SR, 2 * LEV, BLOCK), BF),
                pltpu.VMEM((NE, LEV, BLOCK), F32),
            ],
        ),
        out_shape=[jax.ShapeDtypeStruct(wind.shape, F32), *send_shapes(ER)],
        compiler_params=pltpu.CompilerParams(vmem_limit_bytes=40 << 20),
        name="gradient",
    )(*info, mass, wind, weights, *rim)
    return out[0], out[1:]


D_STEP = 4


def divergence_kernel(pattern, place, send_list, order, wind_ref, mass_ref, w_ref, inv_ref, *refs):
    rim, out_ref, sends, ext, keep = refs[:6], refs[6], refs[7:12], refs[12], refs[13]
    step = pl.program_id(0)

    @pl.when(step == 0)
    def _():
        fill_extended(ext, wind_ref, NE, rim, ER)

    base = step * D_STEP
    for j in range(D_STEP):
        p = target_product(ext, pattern, place, w_ref, base, j, KD)
        pending = mass_ref[:, j * BLOCK : (j + 1) * BLOCK] - time_step * p
        v_hi, v_lo = two_parts(inv_ref[j])
        p_hi, p_lo = two_parts(pending)
        y = jnp.dot(jnp.concatenate([v_hi, v_lo], axis=0), jnp.concatenate([p_hi, p_lo], axis=1), preferred_element_type=F32)
        new = (y[:LEV, :BLOCK] + y[LEV:, :BLOCK]) + (y[:LEV, BLOCK:] + y[LEV:, BLOCK:])
        out_ref[:, j * BLOCK : (j + 1) * BLOCK] = new
        keep[base + j] = new

    @pl.when(step == NB // D_STEP - 1)
    def _():
        fill_sends(sends, send_list, order, lambda b: keep[b], SR)


def divergence(info, wind, mass, weights, inverse, rim):
    steps = NB // D_STEP
    out = pl.pallas_call(
        divergence_kernel,
        grid_spec=pltpu.PrefetchScalarGridSpec(
            num_scalar_prefetch=4,
            grid=(steps,),
            in_specs=[
                whole(wind.shape),
                pl.BlockSpec((LEV, D_STEP * BLOCK), lambda i, *_: (0, i)),
                pl.BlockSpec((D_STEP * KD, BLOCK, 2 * BLOCK), lambda i, *_: (i, 0, 0)),
                pl.BlockSpec((D_STEP, LEV, LEV), lambda i, *_: (i, 0, 0)),
                *rim_specs(ER),
            ],
            out_specs=[pl.BlockSpec((LEV, D_STEP * BLOCK), lambda i, *_: (0, i)), *send_specs(SR)],
            scratch_shapes=[
                pltpu.VMEM((NE + LAT + 2 * ER, 2 * LEV, BLOCK), BF),
                pltpu.VMEM((NB, LEV, BLOCK), F32),
            ],
        ),
        out_shape=[jax.ShapeDtypeStruct(mass.shape, F32), *send_shapes(SR)],
        compiler_params=pltpu.CompilerParams(vmem_limit_bytes=40 << 20),
        name="divergence",
    )(*info, wind, mass, weights, inverse, *rim)
    return out[0], out[1:]


T_STEP = 13
ROWS_AT_ONCE = 16


def turned(x):
    return jnp.transpose(x, (1, 0))


def table_kernel(tracer_ref, *refs):
    rim, table_ref = refs[:6], refs[6]

    def put(slot, x):
        padded = jnp.concatenate([x, jnp.zeros((BLOCK - LEV, BLOCK), F32)], axis=0)
        start = slot * BLOCK if isinstance(slot, int) else pl.multiple_of(slot * BLOCK, BLOCK)
        table_ref[pl.ds(start, BLOCK), :] = turned(padded)

    def one(b, _):
        put(b, block_at(tracer_ref, b))
        return 0

    lax.fori_loop(0, NB, one, 0, unroll=2)
    for j, ref, i in rim_blocks(rim, WR):
        put(NB + j, ref[i])
    put(NB + LAT - 1, jnp.zeros((LEV, BLOCK), F32))


def tracer_table(tracer, rim):
    cells = (NB + LAT + 2 * WR) * BLOCK
    return pl.pallas_call(
        table_kernel,
        grid=(1,),
        in_specs=[whole(tracer.shape), *rim_specs(WR)],
        out_specs=whole((cells, BLOCK)),
        out_shape=jax.ShapeDtypeStruct((cells, BLOCK), F32),
        compiler_params=pltpu.CompilerParams(vmem_limit_bytes=32 << 20),
        cost_estimate=pl.CostEstimate(flops=0, bytes_accessed=8 << 20, transcendentals=0),
        name="tracer_table",
    )(tracer, *rim)


def edge_tracer_kernel(cells, table_ref, out_ref, rows, *, first):
    count = T_STEP * BLOCK

    def block(e, _):
        def some(i, _):
            at = e * BLOCK + i * ROWS_AT_ONCE
            for j in range(ROWS_AT_ONCE):
                a = table_ref[pl.ds(cells[at + j], 1), :]
                b = table_ref[pl.ds(cells[count + at + j], 1), :]
                rows[pl.ds(i * ROWS_AT_ONCE + j, 1), :] = a + b
            return 0

        lax.fori_loop(0, BLOCK // ROWS_AT_ONCE, some, 0)
        out_ref[e] = 0.5 * turned(rows[...])[:LEV]
        return 0

    lax.fori_loop(0, T_STEP, block, 0)


def edge_tracer_part(table, cells, first):
    return pl.pallas_call(
        functools.partial(edge_tracer_kernel, first=first),
        grid_spec=pltpu.PrefetchScalarGridSpec(
            num_scalar_prefetch=1,
            grid=(1,),
            in_specs=[whole(table.shape)],
            out_specs=whole((T_STEP, LEV, BLOCK)),
            scratch_shapes=[pltpu.VMEM((BLOCK, BLOCK), F32)],
        ),
        out_shape=jax.ShapeDtypeStruct((T_STEP, LEV, BLOCK), F32),
        compiler_params=pltpu.CompilerParams(vmem_limit_bytes=32 << 20),
        cost_estimate=pl.CostEstimate(flops=0, bytes_accessed=16 << 20, transcendentals=0),
        name="edge_tracer",
    )(cells, table)


def transport_kernel(pattern, place, total_ref, tracer_ref, w_ref, edge_ref, *refs):
    rim, out_ref, ext = refs[:6], refs[6], refs[7]
    step = pl.program_id(0)

    @pl.when(step == 0)
    def _():
        def one(b, _):
            store_parts(ext, b, (block_at(total_ref, b) / SUBSTEPS) * edge_ref[b])
            return 0

        lax.fori_loop(0, NE, one, 0, unroll=4)
        for j, ref, i in rim_blocks(rim, ER):
            store_parts(ext, NE + j, (ref[i] / SUBSTEPS) * edge_ref[NE + j])
        ext[NE + LAT - 1] = jnp.zeros((2 * LEV, BLOCK), BF)

    base = step * D_STEP
    for j in range(D_STEP):
        p = target_product(ext, pattern, place, w_ref, base, j, KD)
        out_ref[:, j * BLOCK : (j + 1) * BLOCK] = tracer_ref[:, j * BLOCK : (j + 1) * BLOCK] - tracer_step * p


def transport(pattern, place, total, tracer, weights, edge_tracer, rim):
    steps = NB // D_STEP
    return pl.pallas_call(
        transport_kernel,
        grid_spec=pltpu.PrefetchScalarGridSpec(
            num_scalar_prefetch=2,
            grid=(steps,),
            in_specs=[
                whole(total.shape),
                pl.BlockSpec((LEV, D_STEP * BLOCK), lambda i, *_: (0, i)),
                pl.BlockSpec((D_STEP * KD, BLOCK, 2 * BLOCK), lambda i, *_: (i, 0, 0)),
                whole(edge_tracer.shape),
                *rim_specs(ER),
            ],
            out_specs=pl.BlockSpec((LEV, D_STEP * BLOCK), lambda i, *_: (0, i)),
            scratch_shapes=[pltpu.VMEM((NE + LAT + 2 * ER, 2 * LEV, BLOCK), BF)],
        ),
        out_shape=jax.ShapeDtypeStruct(tracer.shape, F32),
        compiler_params=pltpu.CompilerParams(vmem_limit_bytes=40 << 20),
        name="transport",
    )(pattern, place, total, tracer, weights, edge_tracer, *rim)


def edge_order():
    place = place_table(NE, ER)
    return np.argsort(place, axis=1).astype(np.int32)


def body(
    mass_field,
    normal_wind,
    tracer_ratio,
    gradient_weights,
    divergence_weights,
    vertical_inverse,
    gradient_pattern,
    divergence_pattern,
    edge_cells,
    cell_sends,
    edge_sends,
    wide_sends,
):
    order = row_of(ORDER)
    cell_place = row_of(place_table(NB, SR))
    edge_place = row_of(place_table(NE, ER))
    wide_place = row_of(place_table(NB, WR))
    cell_list, edge_list, wide_list = cell_sends[0], edge_sends[0], wide_sends[0]
    g_pattern = gradient_pattern.reshape(-1)
    d_pattern = divergence_pattern.reshape(-1)

    rim = exchange(first_sends(mass_field, cell_list, order, SR))
    g_weights = split_weights(gradient_weights, 18)
    d_weights = split_weights(divergence_weights, 16)

    held = row_of(edge_order())
    by_block = jnp.take(edge_cells.reshape(2, -1, BLOCK), held, axis=1)
    wanted = by_block // BLOCK
    lateral = (wanted >= NB) & (wanted < NB + LAT)
    place_lat = jnp.zeros_like(wanted)
    for p in range(LAT):
        place_lat = jnp.where(wanted == NB + p, wide_place[NB + p], place_lat)
    cells = jnp.where(lateral, place_lat * BLOCK + by_block % BLOCK, by_block)

    tracer_rim = exchange(first_sends(tracer_ratio, wide_list, order, WR))
    table = tracer_table(tracer_ratio, tracer_rim)
    parts = [
        edge_tracer_part(table, cells[:, i : i + T_STEP].reshape(-1), i)
        for i in range(0, NE + LAT + 2 * ER, T_STEP)
    ]
    edge_tracer = jnp.concatenate(parts, axis=0)

    g_info = (g_pattern, cell_place, edge_list, order)
    d_info = (d_pattern, edge_place, cell_list, order)
    mass, wind = mass_field, normal_wind
    winds, rims = [], []
    for substep in range(SUBSTEPS):
        if substep > 0:
            rim = exchange(sends)
        wind, sends = gradient(g_info, mass, wind, g_weights, rim)
        rim = exchange(sends)
        winds.append(wind)
        rims.append(rim)
        mass, sends = divergence(d_info, wind, mass, d_weights, vertical_inverse, rim)
    total = functools.reduce(jnp.add, winds)
    total_rim = [functools.reduce(jnp.add, parts) for parts in zip(*rims)]
    tracer_final = transport(d_pattern, edge_place, total, tracer_ratio, d_weights, edge_tracer, total_rim)
    return mass, wind, tracer_final


def solution(mesh):
    both = ("region", "sub")
    return jax.shard_map(
        body,
        mesh=mesh,
        in_specs=(
            P(None, both),
            P(None, both),
            P(None, both),
            P(both, None, None, None),
            P(both, None, None, None),
            P(both, None, None),
            P(both, None),
            P(both, None),
            P(None, both),
            P(both, None),
            P(both, None),
            P(both, None),
        ),
        out_specs=(P(None, both), P(None, both), P(None, both)),
        check_vma=False,
    )
```

time: 534 us -> 315 us (0.59)
  the two profiles are of different devices: /device:TPU:88 before, /device:TPU:1 now
where the time goes in v1:
time: 315 us; the launch traced here: 314 us
  starting transfers between devices  117 us (37%)
  Pallas kernels  97.5 us (31%)
  local copies, waits for them, and re-layouts  53.2 us (17%)
  waiting for transfers between devices  28.8 us (9%)
  other arithmetic  14.8 us (5%)
    ppermute x22, starting transfers between devices, ring(): lax.ppermute(v, 'region', [(s, (s + step) % N_REGION) for s in range(N_RE...  54.1 us
    unnamed x264, local copies, waits for them, and re-layouts  47.9 us
    pallas_call x5, Pallas kernels, divergence(): pl.pallas_call(divergence_kernel, grid_spec=pltpu.PrefetchScalarGridSpec(...  41.8 us
    pallas_call x5, Pallas kernels, gradient(): pl.pallas_call(gradient_kernel, grid_spec=pltpu.PrefetchScalarGridSpec(nu...  23.1 us
    pallas_call x4, Pallas kernels, edge_tracer_part(): pl.pallas_call(functools.partial(edge_tracer_kernel, first=first), grid_s...  20.5 us
    ppermute x11, starting transfers between devices, exchange(): post_in = lax.ppermute(post, 'sub', MATES)  19.6 us
    ppermute x11, starting transfers between devices, exchange(): lax.ppermute(jnp.concatenate([along, pre_in[1:]], axis=0), 'sub', ALONG)  16.2 us
    ppermute x11, starting transfers between devices, exchange(): pre_in = lax.ppermute(pre, 'sub', MATES)  15.9 us
  transfers between devices with their start and end apart: 66, of which 22 were waited for; matrix products, arithmetic and copies ran while one was open for 6% of the time, Pallas kernels for 13%

profile of v1, /device:TPU:1, one launch (start us, length us, event | category | flops | bytes accessed | tf_op | source)
XLA Modules:
  0.0 313.6 jit_solution(9579051087013983620)
XLA Ops:
  10.9 4.9 %collective-permute-start.5 = (f32[4,96,128]{2,1,0:T(8,128)S(1)}, f32[4,96,128]{2,1,0:T(8,128)S(1)}, u32[]{:S(2)}, u32[]{:S(2)}) collective-permute-start(f32[4,96,128]{2,1,0:T(8,128)S(1)} %get-tuple-element.72), channel_id=1, source_target_pairs={{0,120},{8,0},{16,8},{24,16},{32,24},{40,32},{48,40},{56,48},{64,5... | collective-permute-start | bytes 589832 | tf_op jit(solution)/shard_map/ppermute | solution.py:89
  28.9 4.9 %gradient.5 = (f32[96,4608]{1,0:T(8,128)S(1)}, f32[3,96,128]{2,1,0:T(8,128)S(1)}, f32[2,96,128]{2,1,0:T(8,128)S(1)}, f32[2,96,128]{2,1,0:T(8,128)S(1)}, f32[4,96,128]{2,1,0:T(8,128)}, /*index=5*/f32[4,96,128]{2,1,0:T(8,128)}) custom-call(s32[108]{0:T(128)S(1)} %reshape.84.pattern, s32[40]{0:T(128)S(1)} %fusion.4.place, s32[16]{0:T(128)S(1)} %bitcast.47, ...), custom_call_target="tpu_custom_call" | custom-call | tf_op jit(solution)/shard_map/gradient/pallas_call | solution.py:249
  37.3 4.9 %collective-permute-start.11 = (f32[4,96,128]{2,1,0:T(8,128)}, f32[4,96,128]{2,1,0:T(8,128)}, u32[]{:S(2)}, u32[]{:S(2)}) collective-permute-start(f32[4,96,128]{2,1,0:T(8,128)} %get-tuple-element.78), channel_id=1, source_target_pairs={{0,120},{8,0},{16,8},{24,16},{32,24},{40,32},{48,40},{56,48},{64,5... | collective-permute-start | bytes 589832 | tf_op jit(solution)/shard_map/ppermute | solution.py:89
  50.8 9.2 %divergence.5 = (f32[96,3072]{1,0:T(8,128)S(1)}, f32[3,96,128]{2,1,0:T(8,128)S(1)}, f32[2,96,128]{2,1,0:T(8,128)S(1)}, f32[2,96,128]{2,1,0:T(8,128)S(1)}, f32[4,...) custom-call(s32[96]{0:T(128)S(1)} %reshape.83.pattern, s32[52]{0:T(128)S(1)} %fusion.2.place, s32[16]{0:T(128)S(1)} %bitcast.42, ...), custom_call_target="tpu_custom_call" | custom-call | tf_op jit(solution)/shard_map/divergence/pallas_call | solution.py:302
  64.0 4.8 %collective-permute-start.17 = (f32[4,96,128]{2,1,0:T(8,128)S(1)}, f32[4,96,128]{2,1,0:T(8,128)S(1)}, u32[]{:S(2)}, u32[]{:S(2)}) collective-permute-start(f32[4,96,128]{2,1,0:T(8,128)S(1)} %get-tuple-element.84), channel_id=1, source_target_pairs={{0,120},{8,0},{16,8},{24,16},{32,24},{40,32},{48,40},{56,48},{64,5... | collective-permute-start | bytes 589832 | tf_op jit(solution)/shard_map/ppermute | solution.py:89
  86.1 5.1 %collective-permute-start.23 = (f32[4,96,128]{2,1,0:T(8,128)S(1)}, f32[4,96,128]{2,1,0:T(8,128)S(1)}, u32[]{:S(2)}, u32[]{:S(2)}) collective-permute-start(f32[4,96,128]{2,1,0:T(8,128)S(1)} %get-tuple-element.90), channel_id=1, source_target_pairs={{0,120},{8,0},{16,8},{24,16},{32,24},{40,32},{48,40},{56,48},{64,5... | collective-permute-start | bytes 589832 | tf_op jit(solution)/shard_map/ppermute | solution.py:89
  96.6 7.7 %divergence.6 = (f32[96,3072]{1,0:T(8,128)S(1)}, f32[3,96,128]{2,1,0:T(8,128)S(1)}, f32[2,96,128]{2,1,0:T(8,128)S(1)}, f32[2,96,128]{2,1,0:T(8,128)S(1)}, f32[4,...) custom-call(s32[96]{0:T(128)S(1)} %reshape.83.pattern, s32[52]{0:T(128)S(1)} %fusion.2.place, s32[16]{0:T(128)S(1)} %bitcast.43, ...), custom_call_target="tpu_custom_call" | custom-call | tf_op jit(solution)/shard_map/divergence/pallas_call | solution.py:302
  110.2 4.9 %collective-permute-start.29 = (f32[4,96,128]{2,1,0:T(8,128)S(1)}, f32[4,96,128]{2,1,0:T(8,128)S(1)}, u32[]{:S(2)}, u32[]{:S(2)}) collective-permute-start(f32[4,96,128]{2,1,0:T(8,128)S(1)} %get-tuple-element.96), channel_id=1, source_target_pairs={{0,120},{8,0},{16,8},{24,16},{32,24},{40,32},{48,40},{56,48},{64,5... | collective-permute-start | bytes 589832 | tf_op jit(solution)/shard_map/ppermute | solution.py:89
  133.4 4.8 %collective-permute-start.35 = (f32[4,96,128]{2,1,0:T(8,128)S(1)}, f32[4,96,128]{2,1,0:T(8,128)S(1)}, u32[]{:S(2)}, u32[]{:S(2)}) collective-permute-start(f32[4,96,128]{2,1,0:T(8,128)S(1)} %get-tuple-element.102), channel_id=1, source_target_pairs={{0,120},{8,0},{16,8},{24,16},{32,24},{40,32},{48,40},{56,48},{64,5... | collective-permute-start | bytes 589832 | tf_op jit(solution)/shard_map/ppermute | solution.py:89
  142.2 7.8 %divergence.7 = (f32[96,3072]{1,0:T(8,128)S(1)}, f32[3,96,128]{2,1,0:T(8,128)S(1)}, f32[2,96,128]{2,1,0:T(8,128)S(1)}, f32[2,96,128]{2,1,0:T(8,128)S(1)}, f32[4,...) custom-call(s32[96]{0:T(128)S(1)} %reshape.83.pattern, s32[52]{0:T(128)S(1)} %fusion.2.place, s32[16]{0:T(128)S(1)} %bitcast.44, ...), custom_call_target="tpu_custom_call" | custom-call | tf_op jit(solution)/shard_map/divergence/pallas_call | solution.py:302
  160.4 4.8 %collective-permute-start.41 = (f32[4,96,128]{2,1,0:T(8,128)S(1)}, f32[4,96,128]{2,1,0:T(8,128)S(1)}, u32[]{:S(2)}, u32[]{:S(2)}) collective-permute-start(f32[4,96,128]{2,1,0:T(8,128)S(1)} %get-tuple-element.108), channel_id=1, source_target_pairs={{0,120},{8,0},{16,8},{24,16},{32,24},{40,32},{48,40},{56,48},{64,5... | collective-permute-start | bytes 589832 | tf_op jit(solution)/shard_map/ppermute | solution.py:89
  171.8 4.8 %gradient.8 = (f32[96,4608]{1,0:T(8,128)S(1)}, f32[3,96,128]{2,1,0:T(8,128)}, f32[2,96,128]{2,1,0:T(8,128)S(1)}, f32[2,96,128]{2,1,0:T(8,128)S(1)}, f32[4,96,128...) custom-call(s32[108]{0:T(128)S(1)} %copy-done.106, s32[40]{0:T(128)S(1)} %copy-done.112, s32[16]{0:T(128)S(1)} %bitcast.50, ...), custom_call_target="tpu_custom_call" | custom-call | tf_op jit(solution)/shard_map/gradient/pallas_call | solution.py:249
  194.3 4.8 %collective-permute-start.47 = (f32[4,96,128]{2,1,0:T(8,128)}, f32[4,96,128]{2,1,0:T(8,128)S(1)}, u32[]{:S(2)}, u32[]{:S(2)}) collective-permute-start(f32[4,96,128]{2,1,0:T(8,128)} %copy-done.121), channel_id=1, source_target_pairs={{0,120},{8,0},{16,8},{24,16},{32,24},{40,32},{48,40},{56,48},{64,5... | collective-permute-start | bytes 589832 | tf_op jit(solution)/shard_map/ppermute | solution.py:89
  199.8 5.4 %and_select_fusion.1 = s32[2,52,128]{2,0,1:T(2,128)S(1)} fusion(s32[52,2,128]{2,1,0:T(2,128)S(1)} %copy-done.124, pred[52]{0:T(512)(128)(4,1)S(1)} %compare_and_fusion, s32[]{:T(128)} %bitcast.19, s32[]{:T(128)} %bitcast.18, s32[]{:T(128)} %bitcast.17, s32[]{:T(128)} %bitcast.16, s32[]{:T(128)} %bitcast.15, s32[]{:T(128)} %bitcast.14, s32[]{:T(128)} %bitcast.13, ...), kind=kLoop, calls=%fused_computation.39 | loop fusion | flops 559104 | bytes 106580 | tf_op jit(solution)/shard_map/jit(_where)/select_n | solution.py:485
  205.7 4.8 %collective-permute-start.65 = (f32[8,96,128]{2,1,0:T(8,128)}, f32[8,96,128]{2,1,0:T(8,128)}, u32[]{:S(2)}, u32[]{:S(2)}) collective-permute-start(f32[8,96,128]{2,1,0:T(8,128)} %copy-done.115), channel_id=1, source_target_pairs={{0,120},{8,0},{16,8},{24,16},{32,24},{40,32},{48,40},{56,48},{64,5... | collective-permute-start | bytes 1179656 | tf_op jit(solution)/shard_map/ppermute | solution.py:89
  215.3 8.4 %divergence.8 = (f32[96,3072]{1,0:T(8,128)S(1)}, f32[3,96,128]{2,1,0:T(8,128)S(1)}, f32[2,96,128]{2,1,0:T(8,128)S(1)}, f32[2,96,128]{2,1,0:T(8,128)}, f32[4,96,1...) custom-call(s32[96]{0:T(128)S(1)} %reshape.83.pattern, s32[52]{0:T(128)S(1)} %copy-done.103, s32[16]{0:T(128)S(1)} %bitcast.45, ...), custom_call_target="tpu_custom_call" | custom-call | tf_op jit(solution)/shard_map/divergence/pallas_call | solution.py:302
  236.6 5.1 %edge_tracer.4 = f32[13,96,128]{2,1,0:T(8,128)S(1)} custom-call(s32[3328]{0:T(1024)S(1)} %reshape.88.cells, f32[6144,128]{1,0:T(8,128)S(1)} %tracer_table.1.table_ref), custom_call_target="tpu_custom_call" | custom-call | bytes 16777216 | tf_op jit(solution)/shard_map/edge_tracer/pallas_call | solution.py:387
  241.7 5.1 %edge_tracer.5 = f32[13,96,128]{2,1,0:T(8,128)S(1)} custom-call(s32[3328]{0:T(1024)S(1)} %reshape.89.cells, f32[6144,128]{1,0:T(8,128)S(1)} %tracer_table.1.table_ref), custom_call_target="tpu_custom_call" | custom-call | bytes 16777216 | tf_op jit(solution)/shard_map/edge_tracer/pallas_call | solution.py:387
  246.8 5.1 %edge_tracer.6 = f32[13,96,128]{2,1,0:T(8,128)S(1)} custom-call(s32[3328]{0:T(1024)S(1)} %reshape.90.cells, f32[6144,128]{1,0:T(8,128)S(1)} %tracer_table.1.table_ref), custom_call_target="tpu_custom_call" | custom-call | bytes 16777216 | tf_op jit(solution)/shard_map/edge_tracer/pallas_call | solution.py:387
  252.0 5.1 %edge_tracer.7 = f32[13,96,128]{2,1,0:T(8,128)S(1)} custom-call(s32[3328]{0:T(1024)S(1)} %reshape.91.cells, f32[6144,128]{1,0:T(8,128)S(1)} %tracer_table.1.table_ref), custom_call_target="tpu_custom_call" | custom-call | bytes 16777216 | tf_op jit(solution)/shard_map/edge_tracer/pallas_call | solution.py:387
  257.3 4.8 %collective-permute-start.53 = (f32[4,96,128]{2,1,0:T(8,128)S(1)}, f32[4,96,128]{2,1,0:T(8,128)S(1)}, u32[]{:S(2)}, u32[]{:S(2)}) collective-permute-start(f32[4,96,128]{2,1,0:T(8,128)S(1)} %copy-done.118), channel_id=1, source_target_pairs={{0,120},{8,0},{16,8},{24,16},{32,24},{40,32},{48,40},{56,48},{64,5... | collective-permute-start | bytes 589832 | tf_op jit(solution)/shard_map/ppermute | solution.py:89
  272.4 5.1 %gradient.9 = (f32[96,4608]{1,0:T(8,128)}, f32[3,96,128]{2,1,0:T(8,128)S(1)}, f32[2,96,128]{2,1,0:T(8,128)S(1)}, f32[2,96,128]{2,1,0:T(8,128)S(1)}, f32[4,96,128...) custom-call(s32[108]{0:T(128)S(1)} %copy-done.107, s32[40]{0:T(128)S(1)} %copy-done.113, s32[16]{0:T(128)S(1)} %bitcast.51, ...), custom_call_target="tpu_custom_call" | custom-call | tf_op jit(solution)/shard_map/gradient/pallas_call | solution.py:249
  300.0 4.7 %transport.1 = f32[96,3072]{1,0:T(8,128)} custom-call(s32[96]{0:T(128)S(1)} %reshape.83.pattern, s32[52]{0:T(128)S(1)} %copy-done.104, f32[96,4608]{1,0:T(8,128)S(1)} %add_add_fusion.total_ref, f32[96,3072]{1,0:T(8,128)S(1)} %copy-done.23, bf16[96,128,256]{2,1,0:T(8,128)(2,1)S(1)} %bitcast.36, f32[52,96,128]{2,1,0:T(8,128)S(1)} %pad_maximum_fusion.edge_ref, ...), custom_call_target="tpu_custom_call" | custom-call | tf_op jit(solution)/shard_map/transport/pallas_call | solution.py:426
  304.8 8.7 %divergence.9 = (f32[96,3072]{1,0:T(8,128)}, f32[3,96,128]{2,1,0:T(8,128)}, f32[2,96,128]{2,1,0:T(8,128)}, f32[2,96,128]{2,1,0:T(8,128)}, f32[4,96,128]{2,1,0:T(8,128)}, /*index=5*/f32[4,96,128]{2,1,0:T(8,128)}) custom-call(s32[96]{0:T(128)S(1)} %reshape.83.pattern, s32[52]{0:T(128)S(1)} %copy-done.104, s32[16]{0:T(128)S(1)} %bitcast.46, s32[7]{0:T(128)S(1)} %fusion.3.order, ...), custom_call_target="tpu_custom_call" | custom-call | tf_op jit(solution)/shard_map/divergence/pallas_call | solution.py:302
  (478 shorter events, 175.2 us)
Async XLA Ops:
  6.5 9.4 %collective-permute-start.1 = (f32[4,96,128]{2,1,0:T(8,128)S(1)}, f32[4,96,128]{2,1,0:T(8,128)S(1)}, u32[]{:S(2)}, u32[]{:S(2)}) collective-permute-start(f32[4,96,128]{2,1,0:T(8,128)S(1)} %pad_maximum_fusion.1), channel_id=1, source_target_pairs={{0,2},{1,7},{2,4},{3,1},{4,6},{5,3},{6,0},{7,5},{8,10},{9,15},{10,... | collective-permute-start | bytes 589832 | tf_op jit(solution)/shard_map/ppermute | solution.py:97
  9.6 13.6 %collective-permute-start.4 = (f32[4,96,128]{2,1,0:T(8,128)S(1)}, f32[4,96,128]{2,1,0:T(8,128)S(1)}, u32[]{:S(2)}, u32[]{:S(2)}) collective-permute-start(f32[4,96,128]{2,1,0:T(8,128)S(1)} %get-tuple-element.71), channel_id=1, source_target_pairs={{0,8},{8,16},{16,24},{24,32},{32,40},{40,48},{48,56},{56,64},{64,7... | collective-permute-start | bytes 589832 | tf_op jit(solution)/shard_map/ppermute | solution.py:89
  10.9 13.4 %collective-permute-start.5 = (f32[4,96,128]{2,1,0:T(8,128)S(1)}, f32[4,96,128]{2,1,0:T(8,128)S(1)}, u32[]{:S(2)}, u32[]{:S(2)}) collective-permute-start(f32[4,96,128]{2,1,0:T(8,128)S(1)} %get-tuple-element.72), channel_id=1, source_target_pairs={{0,120},{8,0},{16,8},{24,16},{32,24},{40,32},{48,40},{56,48},{64,5... | collective-permute-start | bytes 589832 | tf_op jit(solution)/shard_map/ppermute | solution.py:89
  15.9 9.6 %collective-permute-start.3 = (f32[3,96,128]{2,1,0:T(8,128)S(1)}, f32[3,96,128]{2,1,0:T(8,128)S(1)}, u32[]{:S(2)}, u32[]{:S(2)}) collective-permute-start(f32[3,96,128]{2,1,0:T(8,128)S(1)} %pad_maximum_fusion.12), channel_id=1, source_target_pairs={{0,1},{1,0},{2,3},{3,2},{4,5},{5,4},{6,7},{7,6},{8,9},{9,8},{10,11... | collective-permute-start | bytes 442376 | tf_op jit(solution)/shard_map/ppermute | solution.py:100
  37.2 13.4 %collective-permute-start.10 = (f32[4,96,128]{2,1,0:T(8,128)}, f32[4,96,128]{2,1,0:T(8,128)S(1)}, u32[]{:S(2)}, u32[]{:S(2)}) collective-permute-start(f32[4,96,128]{2,1,0:T(8,128)} %get-tuple-element.77), channel_id=1, source_target_pairs={{0,8},{8,16},{16,24},{24,32},{32,40},{40,48},{48,56},{56,64},{64,7... | collective-permute-start | bytes 589832 | tf_op jit(solution)/shard_map/ppermute | solution.py:89
  37.3 13.4 %collective-permute-start.11 = (f32[4,96,128]{2,1,0:T(8,128)}, f32[4,96,128]{2,1,0:T(8,128)}, u32[]{:S(2)}, u32[]{:S(2)}) collective-permute-start(f32[4,96,128]{2,1,0:T(8,128)} %get-tuple-element.78), channel_id=1, source_target_pairs={{0,120},{8,0},{16,8},{24,16},{32,24},{40,32},{48,40},{56,48},{64,5... | collective-permute-start | bytes 589832 | tf_op jit(solution)/shard_map/ppermute | solution.py:89
  64.0 9.3 %collective-permute-start.16 = (f32[4,96,128]{2,1,0:T(8,128)S(1)}, f32[4,96,128]{2,1,0:T(8,128)S(1)}, u32[]{:S(2)}, u32[]{:S(2)}) collective-permute-start(f32[4,96,128]{2,1,0:T(8,128)S(1)} %get-tuple-element.83), channel_id=1, source_target_pairs={{0,8},{8,16},{16,24},{24,32},{32,40},{40,48},{48,56},{56,64},{64,7... | collective-permute-start | bytes 589832 | tf_op jit(solution)/shard_map/ppermute | solution.py:89
  64.0 9.3 %collective-permute-start.17 = (f32[4,96,128]{2,1,0:T(8,128)S(1)}, f32[4,96,128]{2,1,0:T(8,128)S(1)}, u32[]{:S(2)}, u32[]{:S(2)}) collective-permute-start(f32[4,96,128]{2,1,0:T(8,128)S(1)} %get-tuple-element.84), channel_id=1, source_target_pairs={{0,120},{8,0},{16,8},{24,16},{32,24},{40,32},{48,40},{56,48},{64,5... | collective-permute-start | bytes 589832 | tf_op jit(solution)/shard_map/ppermute | solution.py:89
  153.0 12.2 %collective-permute-start.37 = (f32[4,96,128]{2,1,0:T(8,128)S(1)}, f32[4,96,128]{2,1,0:T(8,128)S(1)}, u32[]{:S(2)}, u32[]{:S(2)}) collective-permute-start(f32[4,96,128]{2,1,0:T(8,128)S(1)} %pad_maximum_fusion.7), channel_id=1, source_target_pairs={{0,2},{1,7},{2,4},{3,1},{4,6},{5,3},{6,0},{7,5},{8,10},{9,15},{10,... | collective-permute-start | bytes 589832 | tf_op jit(solution)/shard_map/ppermute | solution.py:97
  157.5 30.3 %collective-permute-start.60 = (f32[3,96,128]{2,1,0:T(8,128)}, f32[3,96,128]{2,1,0:T(8,128)S(1)}, u32[]{:S(2)}, u32[]{:S(2)}) collective-permute-start(f32[3,96,128]{2,1,0:T(8,128)} %get-tuple-element.128), channel_id=1, source_target_pairs={{0,1},{1,0},{2,3},{3,2},{4,5},{5,4},{6,7},{7,6},{8,9},{9,8},{10,11... | collective-permute-start | bytes 442376 | tf_op jit(solution)/shard_map/ppermute | solution.py:96
  158.7 46.6 %collective-permute-start.62 = (f32[2,96,128]{2,1,0:T(8,128)}, f32[2,96,128]{2,1,0:T(8,128)S(1)}, u32[]{:S(2)}, u32[]{:S(2)}) collective-permute-start(f32[2,96,128]{2,1,0:T(8,128)} %get-tuple-element.130), channel_id=1, source_target_pairs={{0,4},{1,5},{2,6},{3,7},{4,0},{5,1},{6,2},{7,3},{8,12},{9,13},{10,... | collective-permute-start | bytes 294920 | tf_op jit(solution)/shard_map/ppermute | solution.py:98
  159.7 9.1 %collective-permute-start.40 = (f32[4,96,128]{2,1,0:T(8,128)S(1)}, f32[4,96,128]{2,1,0:T(8,128)S(1)}, u32[]{:S(2)}, u32[]{:S(2)}) collective-permute-start(f32[4,96,128]{2,1,0:T(8,128)S(1)} %get-tuple-element.107), channel_id=1, source_target_pairs={{0,8},{8,16},{16,24},{24,32},{32,40},{40,48},{48,56},{56,64},{64,7... | collective-permute-start | bytes 589832 | tf_op jit(solution)/shard_map/ppermute | solution.py:89
  185.2 13.9 %collective-permute-start.43 = (f32[4,96,128]{2,1,0:T(8,128)S(1)}, f32[4,96,128]{2,1,0:T(8,128)S(1)}, u32[]{:S(2)}, u32[]{:S(2)}) collective-permute-start(f32[4,96,128]{2,1,0:T(8,128)S(1)} %pad_maximum_fusion.8), channel_id=1, source_target_pairs={{0,2},{1,7},{2,4},{3,1},{4,6},{5,3},{6,0},{7,5},{8,10},{9,15},{10,... | collective-permute-start | bytes 589832 | tf_op jit(solution)/shard_map/ppermute | solution.py:97
  188.7 36.7 %collective-permute-start.61 = (f32[4,96,128]{2,1,0:T(8,128)S(1)}, f32[4,96,128]{2,1,0:T(8,128)S(1)}, u32[]{:S(2)}, u32[]{:S(2)}) collective-permute-start(f32[4,96,128]{2,1,0:T(8,128)S(1)} %pad_maximum_fusion.11), channel_id=1, source_target_pairs={{0,2},{1,7},{2,4},{3,1},{4,6},{5,3},{6,0},{7,5},{8,10},{9,15},{10,... | collective-permute-start | bytes 589832 | tf_op jit(solution)/shard_map/ppermute | solution.py:97
  190.0 15.6 %collective-permute-start.46 = (f32[4,96,128]{2,1,0:T(8,128)}, f32[4,96,128]{2,1,0:T(8,128)S(1)}, u32[]{:S(2)}, u32[]{:S(2)}) collective-permute-start(f32[4,96,128]{2,1,0:T(8,128)} %copy-done.122), channel_id=1, source_target_pairs={{0,8},{8,16},{16,24},{24,32},{32,40},{40,48},{48,56},{56,64},{64,7... | collective-permute-start | bytes 589832 | tf_op jit(solution)/shard_map/ppermute | solution.py:89
  194.3 16.2 %collective-permute-start.47 = (f32[4,96,128]{2,1,0:T(8,128)}, f32[4,96,128]{2,1,0:T(8,128)S(1)}, u32[]{:S(2)}, u32[]{:S(2)}) collective-permute-start(f32[4,96,128]{2,1,0:T(8,128)} %copy-done.121), channel_id=1, source_target_pairs={{0,120},{8,0},{16,8},{24,16},{32,24},{40,32},{48,40},{56,48},{64,5... | collective-permute-start | bytes 589832 | tf_op jit(solution)/shard_map/ppermute | solution.py:89
  199.2 11.3 %collective-permute-start.45 = (f32[3,96,128]{2,1,0:T(8,128)S(1)}, f32[3,96,128]{2,1,0:T(8,128)S(1)}, u32[]{:S(2)}, u32[]{:S(2)}) collective-permute-start(f32[3,96,128]{2,1,0:T(8,128)S(1)} %pad_maximum_fusion.19), channel_id=1, source_target_pairs={{0,1},{1,0},{2,3},{3,2},{4,5},{5,4},{6,7},{7,6},{8,9},{9,8},{10,11... | collective-permute-start | bytes 442376 | tf_op jit(solution)/shard_map/ppermute | solution.py:100
  205.3 25.3 %collective-permute-start.64 = (f32[8,96,128]{2,1,0:T(8,128)}, f32[8,96,128]{2,1,0:T(8,128)}, u32[]{:S(2)}, u32[]{:S(2)}) collective-permute-start(f32[8,96,128]{2,1,0:T(8,128)} %copy-done.116), channel_id=1, source_target_pairs={{0,8},{8,16},{16,24},{24,32},{32,40},{40,48},{48,56},{56,64},{64,7... | collective-permute-start | bytes 1179656 | tf_op jit(solution)/shard_map/ppermute | solution.py:89
  205.7 25.0 %collective-permute-start.65 = (f32[8,96,128]{2,1,0:T(8,128)}, f32[8,96,128]{2,1,0:T(8,128)}, u32[]{:S(2)}, u32[]{:S(2)}) collective-permute-start(f32[8,96,128]{2,1,0:T(8,128)} %copy-done.115), channel_id=1, source_target_pairs={{0,120},{8,0},{16,8},{24,16},{32,24},{40,32},{48,40},{56,48},{64,5... | collective-permute-start | bytes 1179656 | tf_op jit(solution)/shard_map/ppermute | solution.py:89
  226.1 35.9 %collective-permute-start.50 = (f32[2,96,128]{2,1,0:T(8,128)}, f32[2,96,128]{2,1,0:T(8,128)S(1)}, u32[]{:S(2)}, u32[]{:S(2)}) collective-permute-start(f32[2,96,128]{2,1,0:T(8,128)} %get-tuple-element.118), channel_id=1, source_target_pairs={{0,4},{1,5},{2,6},{3,7},{4,0},{5,1},{6,2},{7,3},{8,12},{9,13},{10,... | collective-permute-start | bytes 294920 | tf_op jit(solution)/shard_map/ppermute | solution.py:98
  228.8 33.3 %collective-permute-start.49 = (f32[4,96,128]{2,1,0:T(8,128)}, f32[4,96,128]{2,1,0:T(8,128)S(1)}, u32[]{:S(2)}, u32[]{:S(2)}) collective-permute-start(f32[4,96,128]{2,1,0:T(8,128)} %pad_maximum_fusion.9), channel_id=1, source_target_pairs={{0,2},{1,7},{2,4},{3,1},{4,6},{5,3},{6,0},{7,5},{8,10},{9,15},{10,... | collective-permute-start | bytes 589832 | tf_op jit(solution)/shard_map/ppermute | solution.py:97
  257.3 9.2 %collective-permute-start.53 = (f32[4,96,128]{2,1,0:T(8,128)S(1)}, f32[4,96,128]{2,1,0:T(8,128)S(1)}, u32[]{:S(2)}, u32[]{:S(2)}) collective-permute-start(f32[4,96,128]{2,1,0:T(8,128)S(1)} %copy-done.118), channel_id=1, source_target_pairs={{0,120},{8,0},{16,8},{24,16},{32,24},{40,32},{48,40},{56,48},{64,5... | collective-permute-start | bytes 589832 | tf_op jit(solution)/shard_map/ppermute | solution.py:89
  277.5 13.3 %collective-permute-start.59 = (f32[4,96,128]{2,1,0:T(8,128)S(1)}, f32[4,96,128]{2,1,0:T(8,128)S(1)}, u32[]{:S(2)}, u32[]{:S(2)}) collective-permute-start(f32[4,96,128]{2,1,0:T(8,128)S(1)} %get-tuple-element.126), channel_id=1, source_target_pairs={{0,120},{8,0},{16,8},{24,16},{32,24},{40,32},{48,40},{56,48},{64,5... | collective-permute-start | bytes 589832 | tf_op jit(solution)/shard_map/ppermute | solution.py:89
  281.4 10.5 %collective-permute-start.58 = (f32[4,96,128]{2,1,0:T(8,128)S(1)}, f32[4,96,128]{2,1,0:T(8,128)S(1)}, u32[]{:S(2)}, u32[]{:S(2)}) collective-permute-start(f32[4,96,128]{2,1,0:T(8,128)S(1)} %get-tuple-element.125), channel_id=1, source_target_pairs={{0,8},{8,16},{16,24},{24,32},{32,40},{40,48},{48,56},{56,64},{64,7... | collective-permute-start | bytes 589832 | tf_op jit(solution)/shard_map/ppermute | solution.py:89
  (173 other events, 1586.8 us)

commit v2 on v0

v2 whole, which is shorter than its diff:
```python
import functools

import numpy as np
import jax
import jax.numpy as jnp
from jax import lax
from jax.experimental import pallas as pl
from jax.experimental.pallas import tpu as pltpu
from jax.sharding import PartitionSpec as P

BLOCK = 128
LEV = 96
NB = 24
NE = 36
KG = 3
KD = 4
SR = 4
ER = 4
WR = 8
SUBSTEPS = 5
N_REGION = 16
N_CHIP = 4
N_SUB = 8
LAT = 8

time_step = 0.25
tracer_step = 0.5

BF = jnp.bfloat16
F32 = jnp.float32

ALONG = [(2 * x + c, 2 * ((x + (1 if c == 0 else 3)) % 4) + c) for x in range(4) for c in range(2)]
ACROSS = [(2 * x + c, 2 * ((x + 2) % 4) + c) for x in range(4) for c in range(2)]
MATES = [(s, s ^ 1) for s in range(8)]
REGIONS = [(r * 8 + s, (r + (1 if s % 2 == 0 else 15)) % 16 * 8 + s) for r in range(16) for s in range(8)]


def send_order(side):
    rows = []
    for s in range(N_SUB):
        x, c = divmod(s, 2)
        mine = (x + (1 if c == 0 else 3)) % 4
        other = (x + (3 if c == 0 else 1)) % 4
        far = (x + 2) % 4
        o = 1 - c
        to_next = [LAT + j for j in range(side)]
        to_prev = [LAT + side + j for j in range(side)]
        kept, given = (to_next, to_prev) if c == 0 else (to_prev, to_next)
        rows.append(
            [2 * x + o, 2 * other + o, 2 * other + c, *given]
            + [2 * mine + c, 2 * mine + o, 2 * far + c, 2 * far + o, *kept]
        )
    return np.array(rows, np.int32)


def lateral_place():
    rows = []
    for s in range(N_SUB):
        x, c = divmod(s, 2)
        back = 3 if c == 0 else 1
        row = []
        for p in range(N_SUB):
            px, pc = divmod(p, 2)
            d = (px - x) % 4
            same = pc == c
            if d == 0:
                row.append(7 if same else 0)
            elif d == back:
                row.append(1 if same else 2)
            elif d == 2:
                row.append(3 if same else 6)
            else:
                row.append(5 if same else 4)
        rows.append(row)
    return np.array(rows, np.int32)


def place_table(own, side):
    lat = lateral_place()
    rows = []
    for s in range(N_SUB):
        first, second = np.arange(side), side + np.arange(side)
        prev, nxt = (first, second) if s % 2 == 0 else (second, first)
        rows.append(np.concatenate([np.arange(own), own + lat[s], own + LAT + prev, own + LAT + nxt]))
    return np.stack(rows).astype(np.int32)


def row_of(table):
    sub = lax.axis_index("sub")
    return lax.dynamic_slice(jnp.asarray(table), (sub, 0), (1, table.shape[1]))[0]


def exchange(sends, work, *given):
    pre, along, across, region = sends
    pre_in = lax.ppermute(pre, "sub", MATES)
    pre_in, *given = together(pre_in, *given)
    region_in = lax.ppermute(jnp.concatenate([region, pre_in[3:]], axis=0), ("region", "sub"), REGIONS)
    along_in = lax.ppermute(jnp.concatenate([along, pre_in[1:3]], axis=0), "sub", ALONG)
    across_in = lax.ppermute(across, "sub", ACROSS)
    side = region.shape[0]
    done, along_in, across_in, region_in = together(work(*given), along_in, across_in, region_in)
    post = jnp.concatenate([along_in[1:2], along_in[3:4], across_in[1:2], region_in[side:]], axis=0)
    post_in = lax.ppermute(post, "sub", MATES)
    return done, (pre_in, along_in, across_in, region_in, post_in)


def two_parts(x):
    hi = x.astype(BF)
    lo = (x - hi.astype(F32)).astype(BF)
    return hi, lo


VMEM = pl.BlockSpec(memory_space=pltpu.VMEM)
SMEM = pl.BlockSpec(memory_space=pltpu.SMEM)
HBM = pl.BlockSpec(memory_space=pltpu.HBM)
PARAMS = pltpu.CompilerParams(vmem_limit_bytes=16 << 20)
BIG = pltpu.CompilerParams(vmem_limit_bytes=40 << 20)
BIGGEST = pltpu.CompilerParams(vmem_limit_bytes=58 << 20)


def cost(flops, moved):
    return pl.CostEstimate(flops=flops, bytes_accessed=moved, transcendentals=0)


GROUP = 6
CUT = 12
READS = 6
G_TERMS = NE * KG
D_TERMS = NB * KD
G_RIM = NE * (KG - 1) + GROUP
D_RIM = D_TERMS + GROUP
G_AT = G_TERMS + D_TERMS
D_AT = G_AT + G_RIM
ALL_TERMS = D_AT + D_RIM


def split_kernel(g_pattern, d_pattern, g_ref, d_ref, out_ref, raw, cut, rim, in_sem, out_sem, rim_sem):
    g_steps, d_steps = G_TERMS // CUT, D_TERMS // CUT
    steps = g_steps + d_steps

    def read(i):
        ref, j = (g_ref, i) if i < g_steps else (d_ref, i - g_steps)
        return pltpu.make_async_copy(ref.at[pl.ds(j * CUT, CUT)], raw.at[i % READS], in_sem.at[i])

    def write(i):
        return pltpu.make_async_copy(cut.at[i], out_ref.at[pl.ds(i * CUT, CUT)], out_sem.at[i])

    def write_rim(at, g):
        rows = pl.ds(at + g * GROUP, GROUP)
        return pltpu.make_async_copy(rim.at[rows], out_ref.at[pl.ds(at + G_AT + g * GROUP, GROUP)], rim_sem.at[at // GROUP + g])

    def finish(at, n):
        for j in range(GROUP):
            rim[n + j] = jnp.zeros((BLOCK, 2 * BLOCK), BF)
        groups = (n - at + GROUP - 1) // GROUP

        def one(g, _):
            write_rim(at, g).start()
            return 0

        lax.fori_loop(0, groups, one, 0)
        return groups

    for i in range(READS):
        read(i).start()
    n = jnp.int32(0)
    for i in range(steps):
        read(i).wait()
        pattern, own, start = (g_pattern, NB, i * CUT) if i < g_steps else (d_pattern, NE, (i - g_steps) * CUT)
        if i == g_steps:
            g_groups = finish(0, n)
            n = jnp.int32(G_RIM)

        def one(j, n):
            hi, lo = two_parts(raw[i % READS, j])
            both = jnp.concatenate([hi, lo], axis=1)
            cut[i, j] = both
            rim[n] = both
            return n + (pattern[start + j] >= own).astype(jnp.int32)

        n = lax.fori_loop(0, CUT, one, n, unroll=4)
        write(i).start()
        if i + READS < steps:
            read(i + READS).start()
    d_groups = finish(G_RIM, n)
    for i in range(steps):
        write(i).wait()
    for at, groups in ((0, g_groups), (G_RIM, d_groups)):

        def done(g, _, at=at):
            write_rim(at, g).wait()
            return 0

        lax.fori_loop(0, groups, done, 0)


def split_weights(g_pattern, d_pattern, g, d):
    steps = (G_TERMS + D_TERMS) // CUT
    return pl.pallas_call(
        split_kernel,
        in_specs=[SMEM, SMEM, HBM, HBM],
        out_specs=HBM,
        out_shape=jax.ShapeDtypeStruct((ALL_TERMS, BLOCK, 2 * BLOCK), BF),
        scratch_shapes=[
            pltpu.VMEM((READS, CUT, BLOCK, BLOCK), F32),
            pltpu.VMEM((steps, CUT, BLOCK, 2 * BLOCK), BF),
            pltpu.VMEM((G_RIM + D_RIM, BLOCK, 2 * BLOCK), BF),
            pltpu.SemaphoreType.DMA((steps,)),
            pltpu.SemaphoreType.DMA((steps,)),
            pltpu.SemaphoreType.DMA(((G_RIM + D_RIM) // GROUP,)),
        ],
        compiler_params=BIGGEST,
        cost_estimate=cost(0, 30 << 20),
        name="split_weights",
    )(g_pattern, d_pattern, g.reshape(-1, BLOCK, BLOCK), d.reshape(-1, BLOCK, BLOCK))


def split_inverse_kernel(v_ref, o_ref):
    hi, lo = two_parts(v_ref[...])
    o_ref[:, :LEV] = hi
    o_ref[:, LEV:] = lo


def split_inverse(inverse):
    return pl.pallas_call(
        split_inverse_kernel,
        grid=(4,),
        in_specs=[pl.BlockSpec((NB // 4, LEV, LEV), lambda i: (i, 0, 0))],
        out_specs=pl.BlockSpec((NB // 4, 2 * LEV, LEV), lambda i: (i, 0, 0)),
        out_shape=jax.ShapeDtypeStruct((NB, 2 * LEV, LEV), BF),
        compiler_params=PARAMS,
        cost_estimate=cost(NB * LEV * LEV * 4, NB * LEV * LEV * 8),
        name="split_inverse",
    )(inverse)


ROOM = 128


def list_kernel(pattern, place, slot, target, count, *, own, targets, width):
    def one(t, n):
        for k in range(width):
            e = pattern[t * width + k]
            slot[n] = place[e] - own
            target[n] = t
            n = n + (e >= own).astype(jnp.int32)
        return n

    n = lax.fori_loop(0, targets, one, jnp.int32(0))
    for j in range(GROUP):
        slot[n + j] = LAT - 1
        target[n + j] = 0
    count[0] = (n + GROUP - 1) // GROUP


def rim_list(pattern, place, own, targets, width):
    room = jax.ShapeDtypeStruct((ROOM,), jnp.int32)
    return pl.pallas_call(
        functools.partial(list_kernel, own=own, targets=targets, width=width),
        in_specs=[SMEM] * 2,
        out_specs=[SMEM] * 3,
        out_shape=[room] * 2 + [jax.ShapeDtypeStruct((1,), jnp.int32)],
        compiler_params=PARAMS,
        name="rim_list",
    )(pattern, place)


RIM = ((0, 0), (1, 0), (1, 2), (2, 0), (4, 0), (4, 1), (4, 2))


def rim_blocks(rim, side):
    blocks = [(j, rim[which], i) for j, (which, i) in enumerate(RIM)]
    blocks += [(LAT + i, rim[3], i) for i in range(side)]
    blocks += [(LAT + side + i, rim[4], 3 + i) for i in range(side)]
    return blocks


def store_parts(ext, slot, x):
    hi, lo = two_parts(x)
    ext[slot, :LEV, :] = hi
    ext[slot, LEV:, :] = lo


def columns(b):
    return pl.ds(b * BLOCK if isinstance(b, int) else pl.multiple_of(b * BLOCK, BLOCK), BLOCK)


def block_at(ref, b):
    return ref[:, columns(b)]


def summed(y):
    return (y[:LEV, :BLOCK] + y[LEV:, :BLOCK]) + (y[:LEV, BLOCK:] + y[LEV:, BLOCK:])


def pick(source, entry):
    live = (entry >= 0).astype(F32)
    return source(jnp.maximum(entry, 0)) * live


def fill_sends(sends, send_list, order, source, side):
    at = 0
    for ref, n in zip(sends, (3 + side, 2, 2, side)):
        for j in range(n):
            ref[j] = pick(source, send_list[order[at + j]])
        at += n


def send_shapes(side):
    return [jax.ShapeDtypeStruct((n, LEV, BLOCK), F32) for n in (3 + side, 2, 2, side)]


def first_kernel(send_list, order, field_ref, *sends, side):
    fill_sends(sends, send_list, order, lambda b: block_at(field_ref, b), side)


def first_sends(field, send_list, order, side):
    return pl.pallas_call(
        functools.partial(first_kernel, side=side),
        in_specs=[SMEM, SMEM, VMEM],
        out_specs=[VMEM] * 4,
        out_shape=send_shapes(side),
        compiler_params=PARAMS,
        name="first_sends",
    )(send_list, order, field)


UNROLL = 6
SOLVED = 8


def own_kernel(pattern, *refs, own, targets, width, first, scale, flux):
    if flux:
        source_ref, edge_ref, start_ref, w_ref, out_ref, ext, wbuf, sems = refs
    else:
        source_ref, start_ref, w_ref, out_ref, ext, wbuf, sems = refs
    groups, size = targets // UNROLL, UNROLL * width

    def fetch(i):
        return pltpu.make_async_copy(w_ref.at[pl.ds(first + i * size, size)], wbuf.at[i], sems.at[i])

    for i in range(groups):
        fetch(i).start()

    def fill(b, _):
        x = block_at(source_ref, b)
        if flux:
            x = (x / SUBSTEPS) * edge_ref[b]
        store_parts(ext, b, x)
        return 0

    lax.fori_loop(0, own, fill, 0, unroll=4)
    ext[own] = jnp.zeros((2 * LEV, BLOCK), BF)

    def some(i, _):
        fetch(i).wait()
        for j in range(UNROLL):
            t = i * UNROLL + j
            x = jnp.concatenate([ext[jnp.minimum(pattern[t * width + k], own)] for k in range(width)], axis=1)
            w = wbuf[i, j * width : (j + 1) * width].reshape(width * BLOCK, 2 * BLOCK)
            y = jnp.dot(x, w, preferred_element_type=F32)
            out_ref[:, columns(t)] = block_at(start_ref, t) - scale * summed(y)
        return 0

    lax.fori_loop(0, groups, some, 0)


def own_product(pattern, source, start, weights, own, targets, width, first, scale, edge=None):
    ins = [source] + ([] if edge is None else [edge]) + [start, weights]
    return pl.pallas_call(
        functools.partial(own_kernel, own=own, targets=targets, width=width, first=first, scale=scale, flux=edge is not None),
        in_specs=[SMEM] + [VMEM] * (len(ins) - 1) + [HBM],
        out_specs=VMEM,
        out_shape=jax.ShapeDtypeStruct(start.shape, F32),
        scratch_shapes=[
            pltpu.VMEM((own + 1, 2 * LEV, BLOCK), BF),
            pltpu.VMEM((targets // UNROLL, UNROLL * width, BLOCK, 2 * BLOCK), BF),
            pltpu.SemaphoreType.DMA((targets // UNROLL,)),
        ],
        compiler_params=BIG,
        cost_estimate=cost(4 << 30, 8 << 20),
        name="own_product",
    )(pattern, *ins)


def rim_kernel(slot, target, count, *refs, targets, side, next_side, first, scale, flux, solve):
    refs = list(refs)
    held = refs.pop(0) if flux else None
    if next_side:
        send_list, order = refs.pop(0), refs.pop(0)
    partial_ref, w_ref = refs.pop(0), refs.pop(0)
    rim, refs = refs[:5], refs[5:]
    edge_ref = refs.pop(0) if flux else None
    inv_ref = refs.pop(0) if solve else None
    out_ref = refs.pop(0)
    sends, refs = (refs[:4], refs[4:]) if next_side else ((), refs)
    ext, wbuf, sems = refs.pop(0), refs.pop(0), refs.pop(0)
    acc = refs.pop(0) if solve else out_ref

    def fetch(g):
        return pltpu.make_async_copy(w_ref.at[pl.ds(first + g * GROUP, GROUP)], wbuf.at[pl.ds(g * GROUP, GROUP)], sems.at[g])

    def begin(g, _):
        fetch(g).start()
        return 0

    lax.fori_loop(0, count[0], begin, 0)
    for j, ref, i in rim_blocks(rim, side):
        x = ref[i]
        if flux:
            x = (x / SUBSTEPS) * edge_ref[held[NE + j]]
        store_parts(ext, j, x)
    ext[LAT - 1] = jnp.zeros((2 * LEV, BLOCK), BF)
    acc[...] = partial_ref[...]

    def some(i, _):
        at = i * GROUP
        parts = []
        fetch(i).wait()
        for j in range(GROUP):
            y = jnp.dot(ext[slot[at + j]], wbuf[at + j], preferred_element_type=F32)
            parts.append(scale * summed(y))
        for j in range(GROUP):
            t = target[at + j]
            acc[:, columns(t)] = block_at(acc, t) - parts[j]
        return 0

    lax.fori_loop(0, count[0], some, 0)

    if solve:
        def solved(i, _):
            for j in range(SOLVED):
                b = i * SOLVED + j
                p_hi, p_lo = two_parts(block_at(acc, b))
                y = jnp.dot(inv_ref[b], jnp.concatenate([p_hi, p_lo], axis=1), preferred_element_type=F32)
                out_ref[:, columns(b)] = summed(y)
            return 0

        lax.fori_loop(0, targets // SOLVED, solved, 0)
    if next_side:
        fill_sends(sends, send_list, order, lambda b: block_at(out_ref, b), next_side)


def rim_product(lists, partial, weights, rim, targets, side, scale, sends=None, next_side=0, edge=None, held=None, inverse=None):
    ins = [partial, weights, *rim]
    if edge is not None:
        ins.append(edge)
    if inverse is not None:
        ins.append(inverse)
    scalars = [*lists] + ([] if edge is None else [held]) + ([] if sends is None else [*sends])
    out_shape = [jax.ShapeDtypeStruct(partial.shape, F32)] + (send_shapes(next_side) if next_side else [])
    rim_terms = G_RIM if targets == NE else D_RIM
    scratch = [
        pltpu.VMEM((LAT + 2 * side, 2 * LEV, BLOCK), BF),
        pltpu.VMEM((rim_terms, BLOCK, 2 * BLOCK), BF),
        pltpu.SemaphoreType.DMA((rim_terms // GROUP,)),
    ]
    if inverse is not None:
        scratch.append(pltpu.VMEM(partial.shape, F32))
    out = pl.pallas_call(
        functools.partial(
            rim_kernel, targets=targets, side=side, next_side=next_side, first=G_AT if targets == NE else D_AT, scale=scale, flux=edge is not None, solve=inverse is not None
        ),
        in_specs=[SMEM] * len(scalars) + [VMEM, HBM] + [VMEM] * (len(ins) - 2),
        out_specs=[VMEM] * len(out_shape),
        out_shape=out_shape,
        scratch_shapes=scratch,
        compiler_params=BIG,
        cost_estimate=cost(1 << 30, 4 << 20),
        name="rim_product",
    )(*scalars, *ins)
    return out[0], out[1:]


ROWS_AT_ONCE = 32
PARTS = (8, 8, 8, 8, 8, 8, 4)


def turned(x):
    return jnp.transpose(x, (1, 0))


def table_kernel(held, tracer_ref, *refs):
    rim, table_ref = refs[:5], refs[5]

    def put(slot, x):
        padded = jnp.concatenate([x, jnp.zeros((BLOCK - LEV, BLOCK), F32)], axis=0)
        table_ref[columns(slot), :] = turned(padded)

    def one(b, _):
        put(b, block_at(tracer_ref, b))
        return 0

    lax.fori_loop(0, NB, one, 0, unroll=2)
    for j, ref, i in rim_blocks(rim, WR):
        put(held[NB + j], ref[i])
    put(held[NB + LAT - 1], jnp.zeros((LEV, BLOCK), F32))


def tracer_table(held, tracer, rim):
    cells = (NB + LAT + 2 * WR) * BLOCK
    return pl.pallas_call(
        table_kernel,
        in_specs=[SMEM] + [VMEM] * 6,
        out_specs=VMEM,
        out_shape=jax.ShapeDtypeStruct((cells, BLOCK), F32),
        compiler_params=PARAMS,
        cost_estimate=cost(0, 8 << 20),
        name="tracer_table",
    )(held, tracer, *rim)


def edge_tracer_kernel(cells_ref, table_ref, out_ref, rows, cells, sem, *, start, blocks):
    fetch = pltpu.make_async_copy(cells_ref.at[:, pl.ds(start * BLOCK, blocks * BLOCK)], cells, sem)
    fetch.start()
    fetch.wait()

    def block(e, _):
        def some(i, _):
            at = e * BLOCK + i * ROWS_AT_ONCE
            sums = []
            for j in range(ROWS_AT_ONCE):
                a = table_ref[pl.ds(cells[0, at + j], 1), :]
                b = table_ref[pl.ds(cells[1, at + j], 1), :]
                sums.append(a + b)
            for j in range(ROWS_AT_ONCE):
                rows[pl.ds(i * ROWS_AT_ONCE + j, 1), :] = sums[j]
            return 0

        lax.fori_loop(0, BLOCK // ROWS_AT_ONCE, some, 0)
        out_ref[e] = 0.5 * turned(rows[...])[:LEV]
        return 0

    lax.fori_loop(0, blocks, block, 0)


def edge_tracer_part(table, cells, start, blocks):
    return pl.pallas_call(
        functools.partial(edge_tracer_kernel, start=start, blocks=blocks),
        in_specs=[HBM, VMEM],
        out_specs=VMEM,
        out_shape=jax.ShapeDtypeStruct((blocks, LEV, BLOCK), F32),
        scratch_shapes=[
            pltpu.VMEM((BLOCK, BLOCK), F32),
            pltpu.SMEM((2, blocks * BLOCK), jnp.int32),
            pltpu.SemaphoreType.DMA,
        ],
        compiler_params=PARAMS,
        cost_estimate=cost(0, 8 << 20),
        name="edge_tracer",
    )(cells, table)


def held_table(own, side):
    return np.argsort(place_table(own, side), axis=1).astype(np.int32)


def together(*xs):
    return lax.optimization_barrier(xs)


def body(
    mass_field,
    normal_wind,
    tracer_ratio,
    gradient_weights,
    divergence_weights,
    vertical_inverse,
    gradient_pattern,
    divergence_pattern,
    edge_cells,
    cell_sends,
    edge_sends,
    wide_sends,
):
    order = row_of(send_order(SR))
    wide_order = row_of(send_order(WR))
    cell_place = row_of(place_table(NB, SR))
    edge_place = row_of(place_table(NE, ER))
    cell_list, edge_list, wide_list = cell_sends[0], edge_sends[0], wide_sends[0]
    g_pattern = gradient_pattern.reshape(-1)
    d_pattern = divergence_pattern.reshape(-1)

    wide_held = row_of(held_table(NB, WR))
    edge_held = row_of(held_table(NE, ER))

    def g_own(mass, wind):
        return own_product(g_pattern, mass, wind, weights, NB, NE, KG, 0, time_step)

    def d_own(source, start, scale, edge=None):
        return own_product(d_pattern, source, start, weights, NE, NB, KD, G_TERMS, scale, edge)

    def prepared():
        nonlocal weights
        weights = split_weights(g_pattern, d_pattern, gradient_weights, divergence_weights)
        v = split_inverse(vertical_inverse)
        g_terms = rim_list(g_pattern, cell_place, NB, NE, KG)
        d_terms = rim_list(d_pattern, edge_place, NE, NB, KD)
        return together(g_own(mass_field, normal_wind), v, *g_terms, *d_terms)

    weights = None
    first = first_sends(mass_field, cell_list, order, SR)
    wide = first_sends(tracer_ratio, wide_list, wide_order, WR)
    done, rim = exchange(first, prepared)
    partial, inverse, g_terms, d_terms = done[0], done[1], done[2:5], done[5:]
    tracer_rim = exchange(wide, lambda: ())[1]
    edge_parts = []
    table = None

    def tracer_work(window, partial):
        nonlocal table
        if window == 1:
            partial, *rim = together(partial, *tracer_rim)
            table = tracer_table(wide_held, tracer_ratio, rim)
            partial, table = together(partial, table)
        elif window - 2 < len(PARTS):
            blocks, start = PARTS[window - 2], sum(PARTS[: window - 2])
            partial, now = together(partial, table)
            part = edge_tracer_part(now, edge_cells, start, blocks)
            partial, part = together(partial, part)
            edge_parts.append(part)
        return partial

    mass, wind = mass_field, normal_wind
    winds, rims = [], []
    for substep in range(SUBSTEPS):
        if substep > 0:
            partial, rim = exchange(sends, lambda m, w: tracer_work(2 * substep, g_own(m, w)), mass, wind)
        wind, sends = rim_product(g_terms, partial, weights, rim, NE, SR, time_step, (edge_list, order), ER)
        winds.append(wind)
        if substep < SUBSTEPS - 1:
            partial, rim = exchange(sends, lambda w, m: tracer_work(2 * substep + 1, d_own(w, m, time_step)), wind, mass)
        else:

            def last_work(w, m, *earlier):
                edge_tracer = jnp.concatenate(edge_parts, axis=0)
                total = functools.reduce(jnp.add, (*earlier, w))
                partial, total, tracer = together(d_own(w, m, time_step), total, tracer_ratio)
                return partial, d_own(total, tracer, tracer_step, edge_tracer), edge_tracer

            (partial, t_partial, edge_tracer), rim = exchange(sends, last_work, wind, mass, *winds[:-1])
        rims.append(rim)
        if substep < SUBSTEPS - 1:
            mass, sends = rim_product(d_terms, partial, weights, rim, NB, ER, time_step, (cell_list, order), SR, inverse=inverse)
        else:
            mass, _ = rim_product(d_terms, partial, weights, rim, NB, ER, time_step, inverse=inverse)
    total_rim = [functools.reduce(jnp.add, parts) for parts in zip(*rims)]
    tracer_final, _ = rim_product(d_terms, t_partial, weights, total_rim, NB, ER, tracer_step, edge=edge_tracer, held=edge_held)
    return mass, wind, tracer_final


def solution(mesh):
    both = ("region", "sub")
    return jax.shard_map(
        body,
        mesh=mesh,
        in_specs=(
            P(None, both),
            P(None, both),
            P(None, both),
            P(both, None, None, None),
            P(both, None, None, None),
            P(both, None, None),
            P(both, None),
            P(both, None),
            P(None, both),
            P(both, None),
            P(both, None),
            P(both, None),
        ),
        out_specs=(P(None, both), P(None, both), P(None, both)),
        check_vma=False,
    )
```

time: 534 us -> 261 us (0.49)
  the two profiles are of different devices: /device:TPU:88 before, /device:TPU:1 now
where the time goes in v2:
time: 261 us; the launch traced here: 260 us
  Pallas kernels  149 us (57%)
  starting transfers between devices  75.8 us (29%)
  local copies, waits for them, and re-layouts  16.3 us (6%)
  waiting for transfers between devices  15.1 us (6%)
    pallas_call x11, Pallas kernels, rim_product(): pl.pallas_call(functools.partial(rim_kernel, targets=targets, side=side,...  50.1 us
    pallas_call x11, Pallas kernels, own_product(): pl.pallas_call(functools.partial(own_kernel, own=own, targets=targets, wi...  47.5 us
    pallas_call x7, Pallas kernels, edge_tracer_part(): pl.pallas_call(functools.partial(edge_tracer_kernel, start=start, blocks=...  29.9 us
    ppermute x11, starting transfers between devices, exchange(): lax.ppermute(jnp.concatenate([region, pre_in[3:]], axis=0), ('region', 's...  29.1 us
    ppermute x11, starting transfers between devices, exchange(): across_in = lax.ppermute(across, 'sub', ACROSS)  17.2 us
    ppermute x11, starting transfers between devices, exchange(): lax.ppermute(jnp.concatenate([along, pre_in[1:3]], axis=0), 'sub', ALONG)  14.4 us
    pallas_call x1, Pallas kernels, split_weights(): pl.pallas_call(split_kernel, in_specs=[SMEM, SMEM, HBM, HBM], out_specs=H...  12.3 us
    ppermute x11, waiting for transfers between devices, exchange(): post_in = lax.ppermute(post, 'sub', MATES)  12 us
  transfers between devices with their start and end apart: 55, of which 15 were waited for; matrix products, arithmetic and copies ran while one was open for 4% of the time, Pallas kernels for 39%

profile of v2, /device:TPU:1, one launch (start us, length us, event | category | flops | bytes accessed | tf_op | source)
XLA Modules:
  0.0 260.1 jit_solution(6363798276086770346)
XLA Ops:
  16.9 12.3 %split_weights.1.refs_2_.refs_3_.refs_1_ = bf16[384,128,256]{2,1,0:T(8,128)(2,1)} custom-call(s32[108]{0:T(128)} %reshape.18.g_pattern.pattern, s32[96]{0:T(128)} %reshape.19.d_pattern.pattern, f32[108,128,128]{2,1,0:T(8,128)} %bitcast.28, f32[96,128,128]{2,1,0:T(8,128)} %bitcast.29), custom_call_target="tpu_custom_call" | custom-call | bytes 31457280 | tf_op jit(solution)/shard_map/split_weights/pallas_call | solution.py:199
  29.3 4.8 %own_product.11.refs_2_ = f32[96,4608]{1,0:T(8,128)S(1)} custom-call(s32[108]{0:T(128)S(1)} %copy-done.46, f32[96,3072]{1,0:T(8,128)S(1)} %copy-done.2, f32[96,4608]{1,0:T(8,128)S(1)} %copy-done.13, bf16[384,128,256]{2,1,0:T(8,128)(2,1)} %split_weights.1.refs_2_.refs_3_.refs_1_), custom_call_target="tpu_custom_call" | custom-call | flops 4294967296 | bytes 8388608 | tf_op jit(solution)/shard_map/own_product/pallas_call | solution.py:370
  35.2 6.3 %collective-permute-start.3 = (f32[8,96,128]{2,1,0:T(8,128)S(1)}, f32[8,96,128]{2,1,0:T(8,128)S(1)}, u32[]{:S(2)}, u32[]{:S(2)}) collective-permute-start(f32[8,96,128]{2,1,0:T(8,128)S(1)} %pad_maximum_fusion.2), channel_id=1, source_target_pairs={{0,8},{1,121},{2,10},{3,123},{4,12},{5,125},{6,14},{7,127},{8,16},... | collective-permute-start | bytes 1179656 | tf_op jit(solution)/shard_map/ppermute | solution.py:97
  54.1 4.2 %rim_product.11 = (f32[96,4608]{1,0:T(8,128)S(1)}, f32[7,96,128]{2,1,0:T(8,128)S(1)}, f32[2,96,128]{2,1,0:T(8,128)S(1)}, f32[2,96,128]{2,1,0:T(8,128)S(1)}, f32[4,96,128]{2,1,0:T(8,128)S(1)}) custom-call(s32[128]{0:T(128)S(1)} %get-tuple-element.213.slot, s32[128]{0:T(128)S(1)} %get-tuple-element.214.target, s32[1]{0:T(128)} %get-tuple-element.215.count, ...), custom_call_target="tpu_custom_call" | custom-call | flops 1073741824 | bytes 4194304 | tf_op jit(solution)/shard_map/rim_product/pallas_call | solution.py:460
  74.5 4.9 %rim_product.12 = (f32[96,3072]{1,0:T(8,128)S(1)}, f32[7,96,128]{2,1,0:T(8,128)S(1)}, f32[2,96,128]{2,1,0:T(8,128)S(1)}, f32[2,96,128]{2,1,0:T(8,128)S(1)}, f32[4,96,128]{2,1,0:T(8,128)S(1)}) custom-call(s32[128]{0:T(128)S(1)} %get-tuple-element.210.slot, s32[128]{0:T(128)S(1)} %get-tuple-element.211.target, s32[1]{0:T(128)} %get-tuple-element.212.count, ...), custom_call_target="tpu_custom_call" | custom-call | flops 1073741824 | bytes 4194304 | tf_op jit(solution)/shard_map/rim_product/pallas_call | solution.py:460
  84.8 4.7 %own_product.13.refs_2_ = f32[96,4608]{1,0:T(8,128)S(1)} custom-call(s32[108]{0:T(128)S(1)} %copy-done.46, f32[96,3072]{1,0:T(8,128)S(1)} %get-tuple-element.266.refs_0_.refs_1_, f32[96,4608]{1,0:T(8,128)S(1)} %get-tuple-element.357.refs_0_.refs_1_, bf16[384,128,256]{2,1,0:T(8,128)(2,1)} %split_weights.1.refs_2_.refs_3_.refs_1_), custom_call_target="tpu_custom_call" | custom-call | flops 4294967296 | bytes 8388608 | tf_op jit(solution)/shard_map/own_product/pallas_call | solution.py:370
  89.5 4.6 %edge_tracer.7 = f32[8,96,128]{2,1,0:T(8,128)S(1)} custom-call(s32[2,6656]{1,0:T(2,128)S(1)} %copy-done.4, f32[6144,128]{1,0:T(8,128)S(1)} %tracer_table.1.table_ref), custom_call_target="tpu_custom_call" | custom-call | bytes 8388608 | tf_op jit(solution)/shard_map/edge_tracer/pallas_call | solution.py:538
  107.3 4.0 %own_product.14.refs_2_ = f32[96,3072]{1,0:T(8,128)S(1)} custom-call(s32[96]{0:T(128)S(1)} %copy-done.45, f32[96,4608]{1,0:T(8,128)S(1)} %get-tuple-element.358.refs_0_.refs_1_, f32[96,3072]{1,0:T(8,128)S(1)} %get-tuple-element.266.refs_0_.refs_1_, bf16[384,128,256]{2,1,0:T(8,128)(2,1)} %split_weights.1.refs_2_.refs_3_.refs_1_), custom_call_target="tpu_custom_call" | custom-call | flops 4294967296 | bytes 8388608 | tf_op jit(solution)/shard_map/own_product/pallas_call | solution.py:370
  111.3 4.6 %edge_tracer.8 = f32[8,96,128]{2,1,0:T(8,128)S(1)} custom-call(s32[2,6656]{1,0:T(2,128)S(1)} %copy-done.4, f32[6144,128]{1,0:T(8,128)S(1)} %tracer_table.1.table_ref), custom_call_target="tpu_custom_call" | custom-call | bytes 8388608 | tf_op jit(solution)/shard_map/edge_tracer/pallas_call | solution.py:538
  117.7 4.9 %rim_product.14 = (f32[96,3072]{1,0:T(8,128)S(1)}, f32[7,96,128]{2,1,0:T(8,128)S(1)}, f32[2,96,128]{2,1,0:T(8,128)S(1)}, f32[2,96,128]{2,1,0:T(8,128)S(1)}, f32[4,96,128]{2,1,0:T(8,128)S(1)}) custom-call(s32[128]{0:T(128)S(1)} %get-tuple-element.210.slot, s32[128]{0:T(128)S(1)} %get-tuple-element.211.target, s32[1]{0:T(128)} %get-tuple-element.212.count, ...), custom_call_target="tpu_custom_call" | custom-call | flops 1073741824 | bytes 4194304 | tf_op jit(solution)/shard_map/rim_product/pallas_call | solution.py:460
  128.1 4.8 %own_product.15.refs_2_ = f32[96,4608]{1,0:T(8,128)S(1)} custom-call(s32[108]{0:T(128)S(1)} %copy-done.46, f32[96,3072]{1,0:T(8,128)S(1)} %get-tuple-element.296.refs_0_.refs_1_, f32[96,4608]{1,0:T(8,128)S(1)} %get-tuple-element.358.refs_0_.refs_1_, bf16[384,128,256]{2,1,0:T(8,128)(2,1)} %split_weights.1.refs_2_.refs_3_.refs_1_), custom_call_target="tpu_custom_call" | custom-call | flops 4294967296 | bytes 8388608 | tf_op jit(solution)/shard_map/own_product/pallas_call | solution.py:370
  132.9 4.6 %edge_tracer.9 = f32[8,96,128]{2,1,0:T(8,128)S(1)} custom-call(s32[2,6656]{1,0:T(2,128)S(1)} %copy-done.4, f32[6144,128]{1,0:T(8,128)S(1)} %tracer_table.1.table_ref), custom_call_target="tpu_custom_call" | custom-call | bytes 8388608 | tf_op jit(solution)/shard_map/edge_tracer/pallas_call | solution.py:538
  153.3 4.6 %edge_tracer.10 = f32[8,96,128]{2,1,0:T(8,128)S(1)} custom-call(s32[2,6656]{1,0:T(2,128)S(1)} %copy-done.4, f32[6144,128]{1,0:T(8,128)S(1)} %tracer_table.1.table_ref), custom_call_target="tpu_custom_call" | custom-call | bytes 8388608 | tf_op jit(solution)/shard_map/edge_tracer/pallas_call | solution.py:538
  159.7 4.9 %rim_product.16 = (f32[96,3072]{1,0:T(8,128)S(1)}, f32[7,96,128]{2,1,0:T(8,128)S(1)}, f32[2,96,128]{2,1,0:T(8,128)S(1)}, f32[2,96,128]{2,1,0:T(8,128)S(1)}, f32[4,96,128]{2,1,0:T(8,128)S(1)}) custom-call(s32[128]{0:T(128)S(1)} %get-tuple-element.210.slot, s32[128]{0:T(128)S(1)} %get-tuple-element.211.target, s32[1]{0:T(128)} %get-tuple-element.212.count, ...), custom_call_target="tpu_custom_call" | custom-call | flops 1073741824 | bytes 4194304 | tf_op jit(solution)/shard_map/rim_product/pallas_call | solution.py:460
  170.1 4.7 %own_product.17.refs_2_ = f32[96,4608]{1,0:T(8,128)S(1)} custom-call(s32[108]{0:T(128)S(1)} %copy-done.46, f32[96,3072]{1,0:T(8,128)S(1)} %get-tuple-element.326.refs_0_.refs_1_, f32[96,4608]{1,0:T(8,128)S(1)} %get-tuple-element.359.refs_0_.refs_1_, bf16[384,128,256]{2,1,0:T(8,128)(2,1)} %split_weights.1.refs_2_.refs_3_.refs_1_), custom_call_target="tpu_custom_call" | custom-call | flops 4294967296 | bytes 8388608 | tf_op jit(solution)/shard_map/own_product/pallas_call | solution.py:370
  174.9 4.6 %edge_tracer.11 = f32[8,96,128]{2,1,0:T(8,128)S(1)} custom-call(s32[2,6656]{1,0:T(2,128)S(1)} %copy-done.4, f32[6144,128]{1,0:T(8,128)S(1)} %tracer_table.1.table_ref), custom_call_target="tpu_custom_call" | custom-call | bytes 8388608 | tf_op jit(solution)/shard_map/edge_tracer/pallas_call | solution.py:538
  195.3 4.6 %edge_tracer.12 = f32[8,96,128]{2,1,0:T(8,128)S(1)} custom-call(s32[2,6656]{1,0:T(2,128)S(1)} %copy-done.4, f32[6144,128]{1,0:T(8,128)S(1)} %tracer_table.1.table_ref), custom_call_target="tpu_custom_call" | custom-call | bytes 8388608 | tf_op jit(solution)/shard_map/edge_tracer/pallas_call | solution.py:538
  201.7 4.9 %rim_product.18 = (f32[96,3072]{1,0:T(8,128)S(1)}, f32[7,96,128]{2,1,0:T(8,128)S(1)}, f32[2,96,128]{2,1,0:T(8,128)S(1)}, f32[2,96,128]{2,1,0:T(8,128)S(1)}, f32[4,96,128]{2,1,0:T(8,128)S(1)}) custom-call(s32[128]{0:T(128)S(1)} %get-tuple-element.210.slot, s32[128]{0:T(128)S(1)} %get-tuple-element.211.target, s32[1]{0:T(128)} %get-tuple-element.212.count, ...), custom_call_target="tpu_custom_call" | custom-call | flops 1073741824 | bytes 4194304 | tf_op jit(solution)/shard_map/rim_product/pallas_call | solution.py:460
  212.9 4.8 %own_product.19.refs_2_ = f32[96,4608]{1,0:T(8,128)S(1)} custom-call(s32[108]{0:T(128)S(1)} %copy-done.46, f32[96,3072]{1,0:T(8,128)S(1)} %get-tuple-element.356.refs_0_.refs_1_, f32[96,4608]{1,0:T(8,128)S(1)} %get-tuple-element.360.refs_0_.refs_1_, bf16[384,128,256]{2,1,0:T(8,128)(2,1)} %split_weights.1.refs_2_.refs_3_.refs_1_), custom_call_target="tpu_custom_call" | custom-call | flops 4294967296 | bytes 8388608 | tf_op jit(solution)/shard_map/own_product/pallas_call | solution.py:370
  222.9 4.9 %rim_product.19 = (f32[96,4608]{1,0:T(8,128)}, f32[7,96,128]{2,1,0:T(8,128)S(1)}, f32[2,96,128]{2,1,0:T(8,128)S(1)}, f32[2,96,128]{2,1,0:T(8,128)S(1)}, f32[4,96,128]{2,1,0:T(8,128)S(1)}) custom-call(s32[128]{0:T(128)S(1)} %get-tuple-element.213.slot, s32[128]{0:T(128)S(1)} %get-tuple-element.214.target, s32[1]{0:T(128)} %get-tuple-element.215.count, ...), custom_call_target="tpu_custom_call" | custom-call | flops 1073741824 | bytes 4194304 | tf_op jit(solution)/shard_map/rim_product/pallas_call | solution.py:460
  230.8 4.0 %own_product.20.refs_0_ = f32[96,3072]{1,0:T(8,128)S(1)} custom-call(s32[96]{0:T(128)S(1)} %copy-done.45, f32[96,4608]{1,0:T(8,128)S(1)} %copy-done.3, f32[96,3072]{1,0:T(8,128)S(1)} %get-tuple-element.356.refs_0_.refs_1_, bf16[384,128,256]{2,1,0:T(8,128)(2,1)} %split_weights.1.refs_2_.refs_3_.refs_1_), custom_call_target="tpu_custom_call" | custom-call | flops 4294967296 | bytes 8388608 | tf_op jit(solution)/shard_map/own_product/pallas_call | solution.py:370
  243.8 4.3 %collective-permute-start.54 = (f32[7,96,128]{2,1,0:T(8,128)S(1)}, f32[7,96,128]{2,1,0:T(8,128)S(1)}, u32[]{:S(2)}, u32[]{:S(2)}) collective-permute-start(f32[7,96,128]{2,1,0:T(8,128)S(1)} %pad_maximum_fusion.21), channel_id=1, source_target_pairs={{0,1},{1,0},{2,3},{3,2},{4,5},{5,4},{6,7},{7,6},{8,9},{9,8},{10,11... | collective-permute-start | bytes 1032200 | tf_op jit(solution)/shard_map/ppermute | solution.py:103
  249.5 4.7 %rim_product.21 = f32[96,3072]{1,0:T(8,128)} custom-call(s32[128]{0:T(128)S(1)} %get-tuple-element.210.slot, s32[128]{0:T(128)S(1)} %get-tuple-element.211.target, s32[1]{0:T(128)} %get-tuple-element.212.count, s32[52]{0:T(128)S(1)} %fusion.5.refs_0_, f32[96,3072]{1,0:T(8,128)S(1)} %own_product.21.refs_1_, ...), custom_call_target="tpu_custom_call" | custom-call | flops 1073741824 | bytes 4194304 | tf_op jit(solution)/shard_map/rim_product/pallas_call | solution.py:460
  254.2 5.8 %rim_product.20 = f32[96,3072]{1,0:T(8,128)} custom-call(s32[128]{0:T(128)S(1)} %get-tuple-element.210.slot, s32[128]{0:T(128)S(1)} %get-tuple-element.211.target, s32[1]{0:T(128)} %get-tuple-element.212.count, f32[96,3072]{1,0:T(8,128)S(1)} %own_product.20.refs_0_, bf16[384,128,256]{2,1,0:T(8,128)(2,1)} %split_weights.1.refs_2_.refs_3_.refs_1_, ...), custom_call_target="tpu_custom_call" | custom-call | flops 1073741824 | bytes 4194304 | tf_op jit(solution)/shard_map/rim_product/pallas_call | solution.py:460
  (343 shorter events, 136.7 us)
Async XLA Ops:
  6.1 28.0 %collective-permute-start = (f32[7,96,128]{2,1,0:T(8,128)}, f32[7,96,128]{2,1,0:T(8,128)}, u32[]{:S(2)}, u32[]{:S(2)}) collective-permute-start(f32[7,96,128]{2,1,0:T(8,128)} %get-tuple-element.207), channel_id=1, source_target_pairs={{0,1},{1,0},{2,3},{3,2},{4,5},{5,4},{6,7},{7,6},{8,9},{9,8},{10,11... | collective-permute-start | bytes 1032200 | tf_op jit(solution)/shard_map/ppermute | solution.py:95
  7.5 41.7 %collective-permute-start.2 = (f32[2,96,128]{2,1,0:T(8,128)}, f32[2,96,128]{2,1,0:T(8,128)}, u32[]{:S(2)}, u32[]{:S(2)}) collective-permute-start(f32[2,96,128]{2,1,0:T(8,128)} %get-tuple-element.208), channel_id=1, source_target_pairs={{0,4},{1,5},{2,6},{3,7},{4,0},{5,1},{6,2},{7,3},{8,12},{9,13},{10,... | collective-permute-start | bytes 294920 | tf_op jit(solution)/shard_map/ppermute | solution.py:99
  15.2 33.3 %collective-permute-start.6 = (f32[11,96,128]{2,1,0:T(8,128)}, f32[11,96,128]{2,1,0:T(8,128)S(1)}, u32[]{:S(2)}, u32[]{:S(2)}) collective-permute-start(f32[11,96,128]{2,1,0:T(8,128)} %get-tuple-element.224), channel_id=1, source_target_pairs={{0,1},{1,0},{2,3},{3,2},{4,5},{5,4},{6,7},{7,6},{8,9},{9,8},{10,11... | collective-permute-start | bytes 1622024 | tf_op jit(solution)/shard_map/ppermute | solution.py:95
  35.2 14.3 %collective-permute-start.3 = (f32[8,96,128]{2,1,0:T(8,128)S(1)}, f32[8,96,128]{2,1,0:T(8,128)S(1)}, u32[]{:S(2)}, u32[]{:S(2)}) collective-permute-start(f32[8,96,128]{2,1,0:T(8,128)S(1)} %pad_maximum_fusion.2), channel_id=1, source_target_pairs={{0,8},{1,121},{2,10},{3,123},{4,12},{5,125},{6,14},{7,127},{8,16},... | collective-permute-start | bytes 1179656 | tf_op jit(solution)/shard_map/ppermute | solution.py:97
  48.7 11.8 %collective-permute-start.9 = (f32[16,96,128]{2,1,0:T(8,128)S(1)}, f32[16,96,128]{2,1,0:T(8,128)S(1)}, u32[]{:S(2)}, u32[]{:S(2)}) collective-permute-start(f32[16,96,128]{2,1,0:T(8,128)S(1)} %pad_maximum_fusion), channel_id=1, source_target_pairs={{0,8},{1,121},{2,10},{3,123},{4,12},{5,125},{6,14},{7,127},{8,16},... | collective-permute-start | bytes 2359304 | tf_op jit(solution)/shard_map/ppermute | solution.py:97
  79.9 14.2 %collective-permute-start.17 = (f32[2,96,128]{2,1,0:T(8,128)S(1)}, f32[2,96,128]{2,1,0:T(8,128)S(1)}, u32[]{:S(2)}, u32[]{:S(2)}) collective-permute-start(f32[2,96,128]{2,1,0:T(8,128)S(1)} %get-tuple-element.257), channel_id=1, source_target_pairs={{0,4},{1,5},{2,6},{3,7},{4,0},{5,1},{6,2},{7,3},{8,12},{9,13},{10,... | collective-permute-start | bytes 294920 | tf_op jit(solution)/shard_map/ppermute | solution.py:99
  82.0 12.1 %collective-permute-start.16 = (f32[4,96,128]{2,1,0:T(8,128)S(1)}, f32[4,96,128]{2,1,0:T(8,128)S(1)}, u32[]{:S(2)}, u32[]{:S(2)}) collective-permute-start(f32[4,96,128]{2,1,0:T(8,128)S(1)} %pad_maximum_fusion.25), channel_id=1, source_target_pairs={{0,2},{1,7},{2,4},{3,1},{4,6},{5,3},{6,0},{7,5},{8,10},{9,15},{10,... | collective-permute-start | bytes 589832 | tf_op jit(solution)/shard_map/ppermute | solution.py:98
  100.7 15.1 %collective-permute-start.22 = (f32[2,96,128]{2,1,0:T(8,128)S(1)}, f32[2,96,128]{2,1,0:T(8,128)S(1)}, u32[]{:S(2)}, u32[]{:S(2)}) collective-permute-start(f32[2,96,128]{2,1,0:T(8,128)S(1)} %get-tuple-element.272), channel_id=1, source_target_pairs={{0,4},{1,5},{2,6},{3,7},{4,0},{5,1},{6,2},{7,3},{8,12},{9,13},{10,... | collective-permute-start | bytes 294920 | tf_op jit(solution)/shard_map/ppermute | solution.py:99
  102.6 13.3 %collective-permute-start.21 = (f32[4,96,128]{2,1,0:T(8,128)S(1)}, f32[4,96,128]{2,1,0:T(8,128)S(1)}, u32[]{:S(2)}, u32[]{:S(2)}) collective-permute-start(f32[4,96,128]{2,1,0:T(8,128)S(1)} %pad_maximum_fusion.26), channel_id=1, source_target_pairs={{0,2},{1,7},{2,4},{3,1},{4,6},{5,3},{6,0},{7,5},{8,10},{9,15},{10,... | collective-permute-start | bytes 589832 | tf_op jit(solution)/shard_map/ppermute | solution.py:98
  103.9 12.0 %collective-permute-start.23 = (f32[8,96,128]{2,1,0:T(8,128)S(1)}, f32[8,96,128]{2,1,0:T(8,128)S(1)}, u32[]{:S(2)}, u32[]{:S(2)}) collective-permute-start(f32[8,96,128]{2,1,0:T(8,128)S(1)} %pad_maximum_fusion.5), channel_id=1, source_target_pairs={{0,8},{1,121},{2,10},{3,123},{4,12},{5,125},{6,14},{7,127},{8,16},... | collective-permute-start | bytes 1179656 | tf_op jit(solution)/shard_map/ppermute | solution.py:97
  122.8 14.6 %collective-permute-start.27 = (f32[2,96,128]{2,1,0:T(8,128)S(1)}, f32[2,96,128]{2,1,0:T(8,128)S(1)}, u32[]{:S(2)}, u32[]{:S(2)}) collective-permute-start(f32[2,96,128]{2,1,0:T(8,128)S(1)} %get-tuple-element.287), channel_id=1, source_target_pairs={{0,4},{1,5},{2,6},{3,7},{4,0},{5,1},{6,2},{7,3},{8,12},{9,13},{10,... | collective-permute-start | bytes 294920 | tf_op jit(solution)/shard_map/ppermute | solution.py:99
  124.4 13.0 %collective-permute-start.26 = (f32[4,96,128]{2,1,0:T(8,128)S(1)}, f32[4,96,128]{2,1,0:T(8,128)S(1)}, u32[]{:S(2)}, u32[]{:S(2)}) collective-permute-start(f32[4,96,128]{2,1,0:T(8,128)S(1)} %pad_maximum_fusion.27), channel_id=1, source_target_pairs={{0,2},{1,7},{2,4},{3,1},{4,6},{5,3},{6,0},{7,5},{8,10},{9,15},{10,... | collective-permute-start | bytes 589832 | tf_op jit(solution)/shard_map/ppermute | solution.py:98
  125.6 11.8 %collective-permute-start.28 = (f32[8,96,128]{2,1,0:T(8,128)S(1)}, f32[8,96,128]{2,1,0:T(8,128)S(1)}, u32[]{:S(2)}, u32[]{:S(2)}) collective-permute-start(f32[8,96,128]{2,1,0:T(8,128)S(1)} %pad_maximum_fusion.6), channel_id=1, source_target_pairs={{0,8},{1,121},{2,10},{3,123},{4,12},{5,125},{6,14},{7,127},{8,16},... | collective-permute-start | bytes 1179656 | tf_op jit(solution)/shard_map/ppermute | solution.py:97
  143.2 14.6 %collective-permute-start.32 = (f32[2,96,128]{2,1,0:T(8,128)S(1)}, f32[2,96,128]{2,1,0:T(8,128)S(1)}, u32[]{:S(2)}, u32[]{:S(2)}) collective-permute-start(f32[2,96,128]{2,1,0:T(8,128)S(1)} %get-tuple-element.302), channel_id=1, source_target_pairs={{0,4},{1,5},{2,6},{3,7},{4,0},{5,1},{6,2},{7,3},{8,12},{9,13},{10,... | collective-permute-start | bytes 294920 | tf_op jit(solution)/shard_map/ppermute | solution.py:99
  144.8 13.0 %collective-permute-start.31 = (f32[4,96,128]{2,1,0:T(8,128)S(1)}, f32[4,96,128]{2,1,0:T(8,128)S(1)}, u32[]{:S(2)}, u32[]{:S(2)}) collective-permute-start(f32[4,96,128]{2,1,0:T(8,128)S(1)} %pad_maximum_fusion.28), channel_id=1, source_target_pairs={{0,2},{1,7},{2,4},{3,1},{4,6},{5,3},{6,0},{7,5},{8,10},{9,15},{10,... | collective-permute-start | bytes 589832 | tf_op jit(solution)/shard_map/ppermute | solution.py:98
  145.9 11.9 %collective-permute-start.33 = (f32[8,96,128]{2,1,0:T(8,128)S(1)}, f32[8,96,128]{2,1,0:T(8,128)S(1)}, u32[]{:S(2)}, u32[]{:S(2)}) collective-permute-start(f32[8,96,128]{2,1,0:T(8,128)S(1)} %pad_maximum_fusion.7), channel_id=1, source_target_pairs={{0,8},{1,121},{2,10},{3,123},{4,12},{5,125},{6,14},{7,127},{8,16},... | collective-permute-start | bytes 1179656 | tf_op jit(solution)/shard_map/ppermute | solution.py:97
  164.8 14.6 %collective-permute-start.37 = (f32[2,96,128]{2,1,0:T(8,128)S(1)}, f32[2,96,128]{2,1,0:T(8,128)S(1)}, u32[]{:S(2)}, u32[]{:S(2)}) collective-permute-start(f32[2,96,128]{2,1,0:T(8,128)S(1)} %get-tuple-element.317), channel_id=1, source_target_pairs={{0,4},{1,5},{2,6},{3,7},{4,0},{5,1},{6,2},{7,3},{8,12},{9,13},{10,... | collective-permute-start | bytes 294920 | tf_op jit(solution)/shard_map/ppermute | solution.py:99
  166.4 13.1 %collective-permute-start.36 = (f32[4,96,128]{2,1,0:T(8,128)S(1)}, f32[4,96,128]{2,1,0:T(8,128)S(1)}, u32[]{:S(2)}, u32[]{:S(2)}) collective-permute-start(f32[4,96,128]{2,1,0:T(8,128)S(1)} %pad_maximum_fusion.29), channel_id=1, source_target_pairs={{0,2},{1,7},{2,4},{3,1},{4,6},{5,3},{6,0},{7,5},{8,10},{9,15},{10,... | collective-permute-start | bytes 589832 | tf_op jit(solution)/shard_map/ppermute | solution.py:98
  167.6 11.8 %collective-permute-start.38 = (f32[8,96,128]{2,1,0:T(8,128)S(1)}, f32[8,96,128]{2,1,0:T(8,128)S(1)}, u32[]{:S(2)}, u32[]{:S(2)}) collective-permute-start(f32[8,96,128]{2,1,0:T(8,128)S(1)} %pad_maximum_fusion.8), channel_id=1, source_target_pairs={{0,8},{1,121},{2,10},{3,123},{4,12},{5,125},{6,14},{7,127},{8,16},... | collective-permute-start | bytes 1179656 | tf_op jit(solution)/shard_map/ppermute | solution.py:97
  185.2 14.6 %collective-permute-start.42 = (f32[2,96,128]{2,1,0:T(8,128)S(1)}, f32[2,96,128]{2,1,0:T(8,128)S(1)}, u32[]{:S(2)}, u32[]{:S(2)}) collective-permute-start(f32[2,96,128]{2,1,0:T(8,128)S(1)} %get-tuple-element.332), channel_id=1, source_target_pairs={{0,4},{1,5},{2,6},{3,7},{4,0},{5,1},{6,2},{7,3},{8,12},{9,13},{10,... | collective-permute-start | bytes 294920 | tf_op jit(solution)/shard_map/ppermute | solution.py:99
  186.8 13.0 %collective-permute-start.41 = (f32[4,96,128]{2,1,0:T(8,128)S(1)}, f32[4,96,128]{2,1,0:T(8,128)S(1)}, u32[]{:S(2)}, u32[]{:S(2)}) collective-permute-start(f32[4,96,128]{2,1,0:T(8,128)S(1)} %pad_maximum_fusion.30), channel_id=1, source_target_pairs={{0,2},{1,7},{2,4},{3,1},{4,6},{5,3},{6,0},{7,5},{8,10},{9,15},{10,... | collective-permute-start | bytes 589832 | tf_op jit(solution)/shard_map/ppermute | solution.py:98
  187.9 12.0 %collective-permute-start.43 = (f32[8,96,128]{2,1,0:T(8,128)S(1)}, f32[8,96,128]{2,1,0:T(8,128)S(1)}, u32[]{:S(2)}, u32[]{:S(2)}) collective-permute-start(f32[8,96,128]{2,1,0:T(8,128)S(1)} %pad_maximum_fusion.9), channel_id=1, source_target_pairs={{0,8},{1,121},{2,10},{3,123},{4,12},{5,125},{6,14},{7,127},{8,16},... | collective-permute-start | bytes 1179656 | tf_op jit(solution)/shard_map/ppermute | solution.py:97
  207.6 12.7 %collective-permute-start.47 = (f32[2,96,128]{2,1,0:T(8,128)S(1)}, f32[2,96,128]{2,1,0:T(8,128)S(1)}, u32[]{:S(2)}, u32[]{:S(2)}) collective-permute-start(f32[2,96,128]{2,1,0:T(8,128)S(1)} %get-tuple-element.347), channel_id=1, source_target_pairs={{0,4},{1,5},{2,6},{3,7},{4,0},{5,1},{6,2},{7,3},{8,12},{9,13},{10,... | collective-permute-start | bytes 294920 | tf_op jit(solution)/shard_map/ppermute | solution.py:99
  228.4 13.8 %collective-permute-start.52 = (f32[2,96,128]{2,1,0:T(8,128)S(1)}, f32[2,96,128]{2,1,0:T(8,128)S(1)}, u32[]{:S(2)}, u32[]{:S(2)}) collective-permute-start(f32[2,96,128]{2,1,0:T(8,128)S(1)} %get-tuple-element.373), channel_id=1, source_target_pairs={{0,4},{1,5},{2,6},{3,7},{4,0},{5,1},{6,2},{7,3},{8,12},{9,13},{10,... | collective-permute-start | bytes 294920 | tf_op jit(solution)/shard_map/ppermute | solution.py:99
  (86 other events, 467.1 us)

commit v3 on v2

--- a/solution.py
+++ b/solution.py
@@ -85,15 +85,53 @@
     return np.stack(rows).astype(np.int32)
 
 
-def row_of(table):
+def held_table(own, side):
+    return np.argsort(place_table(own, side), axis=1).astype(np.int32)
+
+
+class At:
+    def __init__(self, ref, start):
+        self.ref, self.start = ref, start
+
+    def __getitem__(self, i):
+        return self.ref[self.start + i]
+
+
+def all_tables():
+    tables = dict(
+        order=send_order(SR),
+        wide_order=send_order(WR),
+        cell_place=place_table(NB, SR),
+        edge_place=place_table(NE, ER),
+        wide_held=held_table(NB, WR),
+        edge_held=held_table(NE, ER),
+    )
+    starts, at = {}, 0
+    for name, table in tables.items():
+        starts[name] = at
+        at += table.shape[1]
+    return np.concatenate(list(tables.values()), axis=1), starts
+
+
+TABLES, STARTS = all_tables()
+
+
+def row_of_tables():
     sub = lax.axis_index("sub")
-    return lax.dynamic_slice(jnp.asarray(table), (sub, 0), (1, table.shape[1]))[0]
+    return lax.dynamic_slice(jnp.asarray(TABLES), (sub, 0), (1, TABLES.shape[1]))[0]
+
+
+def hand_over(sends):
+    return lax.ppermute(sends[0], "sub", MATES)
 
 
 def exchange(sends, work, *given):
-    pre, along, across, region = sends
-    pre_in = lax.ppermute(pre, "sub", MATES)
-    pre_in, *given = together(pre_in, *given)
+    pre_in, *given = together(hand_over(sends), *given)
+    return travel(sends, pre_in, work, *given)
+
+
+def travel(sends, pre_in, work, *given):
+    _, along, across, region = sends
     region_in = lax.ppermute(jnp.concatenate([region, pre_in[3:]], axis=0), ("region", "sub"), REGIONS)
     along_in = lax.ppermute(jnp.concatenate([along, pre_in[1:3]], axis=0), "sub", ALONG)
     across_in = lax.ppermute(across, "sub", ACROSS)
@@ -123,6 +161,7 @@
 
 
 GROUP = 6
+ROOM = 128
 CUT = 12
 READS = 6
 G_TERMS = NE * KG
@@ -134,7 +173,7 @@
 ALL_TERMS = D_AT + D_RIM
 
 
-def split_kernel(g_pattern, d_pattern, g_ref, d_ref, out_ref, raw, cut, rim, in_sem, out_sem, rim_sem):
+def split_kernel(g_pattern, d_pattern, info, g_ref, d_ref, out_ref, g_slot, g_target, g_count, d_slot, d_target, d_count, raw, cut, rim, in_sem, out_sem, rim_sem):
     g_steps, d_steps = G_TERMS // CUT, D_TERMS // CUT
     steps = g_steps + d_steps
 
@@ -149,10 +188,13 @@
         rows = pl.ds(at + g * GROUP, GROUP)
         return pltpu.make_async_copy(rim.at[rows], out_ref.at[pl.ds(at + G_AT + g * GROUP, GROUP)], rim_sem.at[at // GROUP + g])
 
-    def finish(at, n):
+    def finish(at, n, slot, target, count):
         for j in range(GROUP):
             rim[n + j] = jnp.zeros((BLOCK, 2 * BLOCK), BF)
+            slot[n - at + j] = LAT - 1
+            target[n - at + j] = 0
         groups = (n - at + GROUP - 1) // GROUP
+        count[0] = groups
 
         def one(g, _):
             write_rim(at, g).start()
@@ -166,9 +208,14 @@
     n = jnp.int32(0)
     for i in range(steps):
         read(i).wait()
-        pattern, own, start = (g_pattern, NB, i * CUT) if i < g_steps else (d_pattern, NE, (i - g_steps) * CUT)
+        if i < g_steps:
+            pattern, own, start, at, width, lists = g_pattern, NB, i * CUT, 0, KG, (g_slot, g_target)
+            place = At(info, STARTS["cell_place"])
+        else:
+            pattern, own, start, at, width, lists = d_pattern, NE, (i - g_steps) * CUT, G_RIM, KD, (d_slot, d_target)
+            place = At(info, STARTS["edge_place"])
         if i == g_steps:
-            g_groups = finish(0, n)
+            g_groups = finish(0, n, g_slot, g_target, g_count)
             n = jnp.int32(G_RIM)
 
         def one(j, n):
@@ -176,13 +223,17 @@
             both = jnp.concatenate([hi, lo], axis=1)
             cut[i, j] = both
             rim[n] = both
-            return n + (pattern[start + j] >= own).astype(jnp.int32)
+            e = pattern[start + j]
+            slot, target = lists
+            slot[n - at] = place[e] - own
+            target[n - at] = start // width + (j * 43 >> 7 if width == 3 else j >> 2)
+            return n + (e >= own).astype(jnp.int32)
 
         n = lax.fori_loop(0, CUT, one, n, unroll=4)
         write(i).start()
         if i + READS < steps:
             read(i + READS).start()
-    d_groups = finish(G_RIM, n)
+    d_groups = finish(G_RIM, n, d_slot, d_target, d_count)
     for i in range(steps):
         write(i).wait()
     for at, groups in ((0, g_groups), (G_RIM, d_groups)):
@@ -194,13 +245,14 @@
         lax.fori_loop(0, groups, done, 0)
 
 
-def split_weights(g_pattern, d_pattern, g, d):
+def split_weights(g_pattern, d_pattern, info, g, d):
     steps = (G_TERMS + D_TERMS) // CUT
     return pl.pallas_call(
         split_kernel,
-        in_specs=[SMEM, SMEM, HBM, HBM],
-        out_specs=HBM,
-        out_shape=jax.ShapeDtypeStruct((ALL_TERMS, BLOCK, 2 * BLOCK), BF),
+        in_specs=[SMEM] * 3 + [HBM] * 2,
+        out_specs=[HBM] + [SMEM] * 6,
+        out_shape=[jax.ShapeDtypeStruct((ALL_TERMS, BLOCK, 2 * BLOCK), BF)]
+        + [jax.ShapeDtypeStruct((n,), jnp.int32) for n in (ROOM, ROOM, 1)] * 2,
         scratch_shapes=[
             pltpu.VMEM((READS, CUT, BLOCK, BLOCK), F32),
             pltpu.VMEM((steps, CUT, BLOCK, 2 * BLOCK), BF),
@@ -212,7 +264,7 @@
         compiler_params=BIGGEST,
         cost_estimate=cost(0, 30 << 20),
         name="split_weights",
-    )(g_pattern, d_pattern, g.reshape(-1, BLOCK, BLOCK), d.reshape(-1, BLOCK, BLOCK))
+    )(g_pattern, d_pattern, info, g.reshape(-1, BLOCK, BLOCK), d.reshape(-1, BLOCK, BLOCK))
 
 
 def split_inverse_kernel(v_ref, o_ref):
@@ -234,37 +286,6 @@
     )(inverse)
 
 
-ROOM = 128
-
-
-def list_kernel(pattern, place, slot, target, count, *, own, targets, width):
-    def one(t, n):
-        for k in range(width):
-            e = pattern[t * width + k]
-            slot[n] = place[e] - own
-            target[n] = t
-            n = n + (e >= own).astype(jnp.int32)
-        return n
-
-    n = lax.fori_loop(0, targets, one, jnp.int32(0))
-    for j in range(GROUP):
-        slot[n + j] = LAT - 1
-        target[n + j] = 0
-    count[0] = (n + GROUP - 1) // GROUP
-
-
-def rim_list(pattern, place, own, targets, width):
-    room = jax.ShapeDtypeStruct((ROOM,), jnp.int32)
-    return pl.pallas_call(
-        functools.partial(list_kernel, own=own, targets=targets, width=width),
-        in_specs=[SMEM] * 2,
-        out_specs=[SMEM] * 3,
-        out_shape=[room] * 2 + [jax.ShapeDtypeStruct((1,), jnp.int32)],
-        compiler_params=PARAMS,
-        name="rim_list",
-    )(pattern, place)
-
-
 RIM = ((0, 0), (1, 0), (1, 2), (2, 0), (4, 0), (4, 1), (4, 2))
 
 
@@ -298,7 +319,8 @@
     return source(jnp.maximum(entry, 0)) * live
 
 
-def fill_sends(sends, send_list, order, source, side):
+def fill_sends(sends, send_list, info, source, side):
+    order = At(info, STARTS["order" if side == SR else "wide_order"])
     at = 0
     for ref, n in zip(sends, (3 + side, 2, 2, side)):
         for j in range(n):
@@ -378,14 +400,14 @@
             pltpu.SemaphoreType.DMA((targets // UNROLL,)),
         ],
         compiler_params=BIG,
-        cost_estimate=cost(4 << 30, 8 << 20),
+        cost_estimate=cost(0, 1 << 18),
         name="own_product",
     )(pattern, *ins)
 
 
 def rim_kernel(slot, target, count, *refs, targets, side, next_side, first, scale, flux, solve):
     refs = list(refs)
-    held = refs.pop(0) if flux else None
+    held = At(refs.pop(0), STARTS["edge_held"]) if flux else None
     if next_side:
         send_list, order = refs.pop(0), refs.pop(0)
     partial_ref, w_ref = refs.pop(0), refs.pop(0)
@@ -480,7 +502,8 @@
     return jnp.transpose(x, (1, 0))
 
 
-def table_kernel(held, tracer_ref, *refs):
+def table_kernel(info, tracer_ref, *refs):
+    held = At(info, STARTS["wide_held"])
     rim, table_ref = refs[:5], refs[5]
 
     def put(slot, x):
@@ -505,13 +528,22 @@
         out_specs=VMEM,
         out_shape=jax.ShapeDtypeStruct((cells, BLOCK), F32),
         compiler_params=PARAMS,
-        cost_estimate=cost(0, 8 << 20),
+        cost_estimate=cost(0, 1 << 18),
         name="tracer_table",
     )(held, tracer, *rim)
 
 
+def cells_by_part(edge_cells):
+    at, parts = 0, []
+    for blocks in PARTS:
+        parts.append(edge_cells[:, at * BLOCK : (at + blocks) * BLOCK].reshape(-1))
+        at += blocks
+    return jnp.concatenate(parts)
+
+
 def edge_tracer_kernel(cells_ref, table_ref, out_ref, rows, cells, sem, *, start, blocks):
-    fetch = pltpu.make_async_copy(cells_ref.at[:, pl.ds(start * BLOCK, blocks * BLOCK)], cells, sem)
+    count = blocks * BLOCK
+    fetch = pltpu.make_async_copy(cells_ref.at[pl.ds(2 * start * BLOCK, 2 * count)], cells, sem)
     fetch.start()
     fetch.wait()
 
@@ -520,8 +552,8 @@
             at = e * BLOCK + i * ROWS_AT_ONCE
             sums = []
             for j in range(ROWS_AT_ONCE):
-                a = table_ref[pl.ds(cells[0, at + j], 1), :]
-                b = table_ref[pl.ds(cells[1, at + j], 1), :]
+                a = table_ref[pl.ds(cells[at + j], 1), :]
+                b = table_ref[pl.ds(cells[count + at + j], 1), :]
                 sums.append(a + b)
             for j in range(ROWS_AT_ONCE):
                 rows[pl.ds(i * ROWS_AT_ONCE + j, 1), :] = sums[j]
@@ -542,17 +574,13 @@
         out_shape=jax.ShapeDtypeStruct((blocks, LEV, BLOCK), F32),
         scratch_shapes=[
             pltpu.VMEM((BLOCK, BLOCK), F32),
-            pltpu.SMEM((2, blocks * BLOCK), jnp.int32),
+            pltpu.SMEM((2 * blocks * BLOCK,), jnp.int32),
             pltpu.SemaphoreType.DMA,
         ],
         compiler_params=PARAMS,
-        cost_estimate=cost(0, 8 << 20),
+        cost_estimate=cost(0, 1 << 18),
         name="edge_tracer",
     )(cells, table)
-
-
-def held_table(own, side):
-    return np.argsort(place_table(own, side), axis=1).astype(np.int32)
 
 
 def together(*xs):
@@ -573,16 +601,11 @@
     edge_sends,
     wide_sends,
 ):
-    order = row_of(send_order(SR))
-    wide_order = row_of(send_order(WR))
-    cell_place = row_of(place_table(NB, SR))
-    edge_place = row_of(place_table(NE, ER))
+    info = row_of_tables()
     cell_list, edge_list, wide_list = cell_sends[0], edge_sends[0], wide_sends[0]
     g_pattern = gradient_pattern.reshape(-1)
     d_pattern = divergence_pattern.reshape(-1)
 
-    wide_held = row_of(held_table(NB, WR))
-    edge_held = row_of(held_table(NE, ER))
 
     def g_own(mass, wind):
         return own_product(g_pattern, mass, wind, weights, NB, NE, KG, 0, time_step)
@@ -590,20 +613,18 @@
     def d_own(source, start, scale, edge=None):
         return own_product(d_pattern, source, start, weights, NE, NB, KD, G_TERMS, scale, edge)
 
-    def prepared():
+    def prepared(g_weights):
         nonlocal weights
-        weights = split_weights(g_pattern, d_pattern, gradient_weights, divergence_weights)
-        v = split_inverse(vertical_inverse)
-        g_terms = rim_list(g_pattern, cell_place, NB, NE, KG)
-        d_terms = rim_list(d_pattern, edge_place, NE, NB, KD)
-        return together(g_own(mass_field, normal_wind), v, *g_terms, *d_terms)
+        weights, *lists = split_weights(g_pattern, d_pattern, info, g_weights, divergence_weights)
+        return g_own(mass_field, normal_wind), split_inverse(vertical_inverse), lists, cells_by_part(edge_cells)
 
     weights = None
-    first = first_sends(mass_field, cell_list, order, SR)
-    wide = first_sends(tracer_ratio, wide_list, wide_order, WR)
-    done, rim = exchange(first, prepared)
-    partial, inverse, g_terms, d_terms = done[0], done[1], done[2:5], done[5:]
-    tracer_rim = exchange(wide, lambda: ())[1]
+    first = first_sends(mass_field, cell_list, info, SR)
+    wide = first_sends(tracer_ratio, wide_list, info, WR)
+    pre_in, wide_pre_in, g_weights = together(hand_over(first), hand_over(wide), gradient_weights)
+    (partial, inverse, lists, cells), rim = travel(first, pre_in, prepared, g_weights)
+    g_terms, d_terms = lists[:3], lists[3:]
+    tracer_rim = travel(wide, wide_pre_in, lambda: ())[1]
     edge_parts = []
     table = None
 
@@ -611,12 +632,12 @@
         nonlocal table
         if window == 1:
             partial, *rim = together(partial, *tracer_rim)
-            table = tracer_table(wide_held, tracer_ratio, rim)
+            table = tracer_table(info, tracer_ratio, rim)
             partial, table = together(partial, table)
         elif window - 2 < len(PARTS):
             blocks, start = PARTS[window - 2], sum(PARTS[: window - 2])
             partial, now = together(partial, table)
-            part = edge_tracer_part(now, edge_cells, start, blocks)
+            part = edge_tracer_part(now, cells, start, blocks)
             partial, part = together(partial, part)
             edge_parts.append(part)
         return partial
@@ -626,7 +647,7 @@
     for substep in range(SUBSTEPS):
         if substep > 0:
             partial, rim = exchange(sends, lambda m, w: tracer_work(2 * substep, g_own(m, w)), mass, wind)
-        wind, sends = rim_product(g_terms, partial, weights, rim, NE, SR, time_step, (edge_list, order), ER)
+        wind, sends = rim_product(g_terms, partial, weights, rim, NE, SR, time_step, (edge_list, info), ER)
         winds.append(wind)
         if substep < SUBSTEPS - 1:
             partial, rim = exchange(sends, lambda w, m: tracer_work(2 * substep + 1, d_own(w, m, time_step)), wind, mass)
@@ -641,11 +662,11 @@
             (partial, t_partial, edge_tracer), rim = exchange(sends, last_work, wind, mass, *winds[:-1])
         rims.append(rim)
         if substep < SUBSTEPS - 1:
-            mass, sends = rim_product(d_terms, partial, weights, rim, NB, ER, time_step, (cell_list, order), SR, inverse=inverse)
+            mass, sends = rim_product(d_terms, partial, weights, rim, NB, ER, time_step, (cell_list, info), SR, inverse=inverse)
         else:
             mass, _ = rim_product(d_terms, partial, weights, rim, NB, ER, time_step, inverse=inverse)
     total_rim = [functools.reduce(jnp.add, parts) for parts in zip(*rims)]
-    tracer_final, _ = rim_product(d_terms, t_partial, weights, total_rim, NB, ER, tracer_step, edge=edge_tracer, held=edge_held)
+    tracer_final, _ = rim_product(d_terms, t_partial, weights, total_rim, NB, ER, tracer_step, edge=edge_tracer, held=info)
     return mass, wind, tracer_final
 
 

time: 261 us -> 249 us (0.954)
  Pallas kernels: 149 us -> 135 us
  waiting for transfers between devices: 15.1 us -> 23.3 us
  starting transfers between devices: 75.8 us -> 68.9 us
    pallas_call x7, Pallas kernels: 29.9 us -> 21 us  [edge_tracer_part(): pl.pallas_call(functools.partial(edge_tracer_kernel, start=start, blocks=...]
    ppermute x55, waiting for transfers between devices: 15.1 us -> 23.3 us  [the longest x11 12.4 us: travel(): post_in = lax.ppermute(post, 'sub', MATES)]
    ppermute x55, starting transfers between devices: 75.8 us -> 68.9 us  [the longest x11 26.1 us: travel(): lax.ppermute(jnp.concatenate([region, pre_in[3:]], axis=0), ('region', 's...]
    unnamed x118 -> x129, local copies, waits for them, and re-layouts: 7.49 us -> 12.3 us
    squeeze x6 -> x0, local copies, waits for them, and re-layouts: 4.25 us -> none  [row_of(): lax.dynamic_slice(jnp.asarray(table), (sub, 0), (1, table.shape[1]))[0]]
    pallas_call x3 -> x1, Pallas kernels: 15.7 us -> 12.8 us  [split_weights(): pl.pallas_call(split_kernel, in_specs=[SMEM] * 3 + [HBM] * 2, out_specs=[...]
    slice x55, local copies, waits for them, and re-layouts: 3.3 us -> 0.58 us  [the longest x11 0.17 us: travel(): region_in[side:]]
  transfers between devices with their start and end apart: 55 -> 55, of which waited for: 15 -> 18; matrix products, arithmetic and copies ran while one was open for 4% -> 3% of each run, Pallas kernels for 39% -> 35%
where the time goes in v3:
time: 249 us
  Pallas kernels  135 us (54%)
  starting transfers between devices  68.9 us (28%)
  waiting for transfers between devices  23.3 us (9%)
  local copies, waits for them, and re-layouts  15 us (6%)
  other arithmetic  4.03 us (2%)
  between operations  2.58 us (1%)
    pallas_call x11, Pallas kernels, rim_product(): pl.pallas_call(functools.partial(rim_kernel, targets=targets, side=side,...  48.9 us
    pallas_call x11, Pallas kernels, own_product(): pl.pallas_call(functools.partial(own_kernel, own=own, targets=targets, wi...  47.5 us
    ppermute x11, starting transfers between devices, travel(): lax.ppermute(jnp.concatenate([region, pre_in[3:]], axis=0), ('region', 's...  26.1 us
    pallas_call x7, Pallas kernels, edge_tracer_part(): pl.pallas_call(functools.partial(edge_tracer_kernel, start=start, blocks=...  21 us
    ppermute x11, starting transfers between devices, travel(): across_in = lax.ppermute(across, 'sub', ACROSS)  20.3 us
    pallas_call x1, Pallas kernels, split_weights(): pl.pallas_call(split_kernel, in_specs=[SMEM] * 3 + [HBM] * 2, out_specs=[...  12.8 us
    ppermute x11, waiting for transfers between devices, travel(): post_in = lax.ppermute(post, 'sub', MATES)  12.4 us
    unnamed x129, local copies, waits for them, and re-layouts  12.3 us
  transfers between devices with their start and end apart: 55, of which 18 were waited for; matrix products, arithmetic and copies ran while one was open for 3% of the time, Pallas kernels for 35%

profile of v3, /device:TPU:1, one launch (start us, length us, event | category | flops | bytes accessed | tf_op | source)
XLA Modules:
  0.0 248.6 jit_solution(18240743418514466549)
XLA Ops:
  12.1 6.2 %collective-permute-start.4 = (f32[8,96,128]{2,1,0:T(8,128)}, f32[8,96,128]{2,1,0:T(8,128)S(1)}, u32[]{:S(2)}, u32[]{:S(2)}) collective-permute-start(f32[8,96,128]{2,1,0:T(8,128)} %pad_maximum_fusion.2), channel_id=1, source_target_pairs={{0,8},{1,121},{2,10},{3,123},{4,12},{5,125},{6,14},{7,127},{8,16},... | collective-permute-start | bytes 1179656 | tf_op jit(solution)/shard_map/ppermute | solution.py:135
  25.1 12.8 %split_weights.1 = (bf16[384,128,256]{2,1,0:T(8,128)(2,1)}, s32[128]{0:T(128)}, s32[128]{0:T(128)}, s32[1]{0:T(128)}, s32[128]{0:T(128)}, /*index=5*/s32[128]{0:T(128)}, s32[1]{0:T(128)}) custom-call(s32[108]{0:T(128)} %reshape.39.g_pattern.pattern, s32[96]{0:T(128)} %reshape.40.d_pattern.pattern, s32[230]{0:T(256)} %bitcast.35, f32[108,128,128]{2,1,0:T(8,128)} %bitcast.58, ...), custom_call_target="tpu_custom_call" | custom-call | bytes 31457280 | tf_op jit(solution)/shard_map/split_weights/pallas_call | solution.py:250
  39.5 4.8 %own_product.11.refs_2_ = f32[96,4608]{1,0:T(8,128)S(1)} custom-call(s32[108]{0:T(128)S(1)} %copy-done.43, f32[96,3072]{1,0:T(8,128)S(1)} %copy-done.2, f32[96,4608]{1,0:T(8,128)S(1)} %copy-done.6, bf16[384,128,256]{2,1,0:T(8,128)(2,1)} %get-tuple-element.192.refs_2_.refs_3_.refs_1_), custom_call_target="tpu_custom_call" | custom-call | bytes 262144 | tf_op jit(solution)/shard_map/own_product/pallas_call | solution.py:392
  47.0 3.7 %rim_product.11 = (f32[96,4608]{1,0:T(8,128)S(1)}, f32[7,96,128]{2,1,0:T(8,128)S(1)}, f32[2,96,128]{2,1,0:T(8,128)S(1)}, f32[2,96,128]{2,1,0:T(8,128)S(1)}, f32[4,96,128]{2,1,0:T(8,128)S(1)}) custom-call(s32[128]{0:T(128)S(1)} %copy-done.49, s32[128]{0:T(128)S(1)} %copy-done.50, s32[1]{0:T(128)} %get-tuple-element.208.count, s32[16]{0:T(128)S(1)} %bitcast.52, ...), custom_call_target="tpu_custom_call" | custom-call | flops 1073741824 | bytes 4194304 | tf_op jit(solution)/shard_map/rim_product/pallas_call | solution.py:482
  56.1 3.9 %own_product.12.refs_2_ = f32[96,3072]{1,0:T(8,128)S(1)} custom-call(s32[96]{0:T(128)S(1)} %copy-done.42, f32[96,4608]{1,0:T(8,128)S(1)} %get-tuple-element.351.refs_0_.refs_1_, f32[96,3072]{1,0:T(8,128)S(1)} %copy-done.2, bf16[384,128,256]{2,1,0:T(8,128)(2,1)} %get-tuple-element.192.refs_2_.refs_3_.refs_1_), custom_call_target="tpu_custom_call" | custom-call | bytes 262144 | tf_op jit(solution)/shard_map/own_product/pallas_call | solution.py:392
  66.9 4.7 %rim_product.12 = (f32[96,3072]{1,0:T(8,128)S(1)}, f32[7,96,128]{2,1,0:T(8,128)S(1)}, f32[2,96,128]{2,1,0:T(8,128)S(1)}, f32[2,96,128]{2,1,0:T(8,128)S(1)}, f32[4,96,128]{2,1,0:T(8,128)S(1)}) custom-call(s32[128]{0:T(128)S(1)} %copy-done.44, s32[128]{0:T(128)S(1)} %copy-done.45, s32[1]{0:T(128)} %get-tuple-element.205.count, s32[16]{0:T(128)S(1)} %bitcast.48, ...), custom_call_target="tpu_custom_call" | custom-call | flops 1073741824 | bytes 4194304 | tf_op jit(solution)/shard_map/rim_product/pallas_call | solution.py:482
  79.5 4.8 %own_product.13.refs_2_ = f32[96,4608]{1,0:T(8,128)S(1)} custom-call(s32[108]{0:T(128)S(1)} %copy-done.43, f32[96,3072]{1,0:T(8,128)S(1)} %get-tuple-element.260.refs_0_.refs_1_, f32[96,4608]{1,0:T(8,128)S(1)} %get-tuple-element.351.refs_0_.refs_1_, bf16[384,128,256]{2,1,0:T(8,128)(2,1)} %get-tuple-element.192.refs_2_.refs_3_.refs_1_), custom_call_target="tpu_custom_call" | custom-call | bytes 262144 | tf_op jit(solution)/shard_map/own_product/pallas_call | solution.py:392
  89.3 3.8 %rim_product.13 = (f32[96,4608]{1,0:T(8,128)S(1)}, f32[7,96,128]{2,1,0:T(8,128)S(1)}, f32[2,96,128]{2,1,0:T(8,128)S(1)}, f32[2,96,128]{2,1,0:T(8,128)S(1)}, f32[4,96,128]{2,1,0:T(8,128)S(1)}) custom-call(s32[128]{0:T(128)S(1)} %copy-done.49, s32[128]{0:T(128)S(1)} %copy-done.50, s32[1]{0:T(128)} %get-tuple-element.208.count, s32[16]{0:T(128)S(1)} %bitcast.53, ...), custom_call_target="tpu_custom_call" | custom-call | flops 1073741824 | bytes 4194304 | tf_op jit(solution)/shard_map/rim_product/pallas_call | solution.py:482
  99.9 3.9 %own_product.14.refs_2_ = f32[96,3072]{1,0:T(8,128)S(1)} custom-call(s32[96]{0:T(128)S(1)} %copy-done.42, f32[96,4608]{1,0:T(8,128)S(1)} %get-tuple-element.352.refs_0_.refs_1_, f32[96,3072]{1,0:T(8,128)S(1)} %get-tuple-element.260.refs_0_.refs_1_, bf16[384,128,256]{2,1,0:T(8,128)(2,1)} %get-tuple-element.192.refs_2_.refs_3_.refs_1_), custom_call_target="tpu_custom_call" | custom-call | bytes 262144 | tf_op jit(solution)/shard_map/own_product/pallas_call | solution.py:392
  108.9 4.7 %rim_product.14 = (f32[96,3072]{1,0:T(8,128)S(1)}, f32[7,96,128]{2,1,0:T(8,128)S(1)}, f32[2,96,128]{2,1,0:T(8,128)S(1)}, f32[2,96,128]{2,1,0:T(8,128)S(1)}, f32[4,96,128]{2,1,0:T(8,128)S(1)}) custom-call(s32[128]{0:T(128)S(1)} %copy-done.44, s32[128]{0:T(128)S(1)} %copy-done.45, s32[1]{0:T(128)} %get-tuple-element.205.count, s32[16]{0:T(128)S(1)} %bitcast.49, ...), custom_call_target="tpu_custom_call" | custom-call | flops 1073741824 | bytes 4194304 | tf_op jit(solution)/shard_map/rim_product/pallas_call | solution.py:482
  121.3 4.8 %own_product.15.refs_2_ = f32[96,4608]{1,0:T(8,128)S(1)} custom-call(s32[108]{0:T(128)S(1)} %copy-done.43, f32[96,3072]{1,0:T(8,128)S(1)} %get-tuple-element.290.refs_0_.refs_1_, f32[96,4608]{1,0:T(8,128)S(1)} %get-tuple-element.352.refs_0_.refs_1_, bf16[384,128,256]{2,1,0:T(8,128)(2,1)} %get-tuple-element.192.refs_2_.refs_3_.refs_1_), custom_call_target="tpu_custom_call" | custom-call | bytes 262144 | tf_op jit(solution)/shard_map/own_product/pallas_call | solution.py:392
  131.1 3.7 %rim_product.15 = (f32[96,4608]{1,0:T(8,128)S(1)}, f32[7,96,128]{2,1,0:T(8,128)S(1)}, f32[2,96,128]{2,1,0:T(8,128)S(1)}, f32[2,96,128]{2,1,0:T(8,128)S(1)}, f32[4,96,128]{2,1,0:T(8,128)S(1)}) custom-call(s32[128]{0:T(128)S(1)} %copy-done.49, s32[128]{0:T(128)S(1)} %copy-done.50, s32[1]{0:T(128)} %get-tuple-element.208.count, s32[16]{0:T(128)S(1)} %bitcast.54, ...), custom_call_target="tpu_custom_call" | custom-call | flops 1073741824 | bytes 4194304 | tf_op jit(solution)/shard_map/rim_product/pallas_call | solution.py:482
  141.5 3.9 %own_product.16.refs_2_ = f32[96,3072]{1,0:T(8,128)S(1)} custom-call(s32[96]{0:T(128)S(1)} %copy-done.42, f32[96,4608]{1,0:T(8,128)S(1)} %get-tuple-element.353.refs_0_.refs_1_, f32[96,3072]{1,0:T(8,128)S(1)} %get-tuple-element.290.refs_0_.refs_1_, bf16[384,128,256]{2,1,0:T(8,128)(2,1)} %get-tuple-element.192.refs_2_.refs_3_.refs_1_), custom_call_target="tpu_custom_call" | custom-call | bytes 262144 | tf_op jit(solution)/shard_map/own_product/pallas_call | solution.py:392
  150.6 4.7 %rim_product.16 = (f32[96,3072]{1,0:T(8,128)S(1)}, f32[7,96,128]{2,1,0:T(8,128)S(1)}, f32[2,96,128]{2,1,0:T(8,128)S(1)}, f32[2,96,128]{2,1,0:T(8,128)S(1)}, f32[4,96,128]{2,1,0:T(8,128)S(1)}) custom-call(s32[128]{0:T(128)S(1)} %copy-done.44, s32[128]{0:T(128)S(1)} %copy-done.45, s32[1]{0:T(128)} %get-tuple-element.205.count, s32[16]{0:T(128)S(1)} %bitcast.50, ...), custom_call_target="tpu_custom_call" | custom-call | flops 1073741824 | bytes 4194304 | tf_op jit(solution)/shard_map/rim_product/pallas_call | solution.py:482
  163.0 4.7 %own_product.17.refs_2_ = f32[96,4608]{1,0:T(8,128)S(1)} custom-call(s32[108]{0:T(128)S(1)} %copy-done.43, f32[96,3072]{1,0:T(8,128)S(1)} %get-tuple-element.320.refs_0_.refs_1_, f32[96,4608]{1,0:T(8,128)S(1)} %get-tuple-element.353.refs_0_.refs_1_, bf16[384,128,256]{2,1,0:T(8,128)(2,1)} %get-tuple-element.192.refs_2_.refs_3_.refs_1_), custom_call_target="tpu_custom_call" | custom-call | bytes 262144 | tf_op jit(solution)/shard_map/own_product/pallas_call | solution.py:392
  172.8 3.7 %rim_product.17 = (f32[96,4608]{1,0:T(8,128)S(1)}, f32[7,96,128]{2,1,0:T(8,128)S(1)}, f32[2,96,128]{2,1,0:T(8,128)S(1)}, f32[2,96,128]{2,1,0:T(8,128)S(1)}, f32[4,96,128]{2,1,0:T(8,128)S(1)}) custom-call(s32[128]{0:T(128)S(1)} %copy-done.49, s32[128]{0:T(128)S(1)} %copy-done.50, s32[1]{0:T(128)} %get-tuple-element.208.count, s32[16]{0:T(128)S(1)} %bitcast.55, ...), custom_call_target="tpu_custom_call" | custom-call | flops 1073741824 | bytes 4194304 | tf_op jit(solution)/shard_map/rim_product/pallas_call | solution.py:482
  183.2 3.9 %own_product.18.refs_2_ = f32[96,3072]{1,0:T(8,128)S(1)} custom-call(s32[96]{0:T(128)S(1)} %copy-done.42, f32[96,4608]{1,0:T(8,128)S(1)} %get-tuple-element.354.refs_0_.refs_1_, f32[96,3072]{1,0:T(8,128)S(1)} %get-tuple-element.320.refs_0_.refs_1_, bf16[384,128,256]{2,1,0:T(8,128)(2,1)} %get-tuple-element.192.refs_2_.refs_3_.refs_1_), custom_call_target="tpu_custom_call" | custom-call | bytes 262144 | tf_op jit(solution)/shard_map/own_product/pallas_call | solution.py:392
  192.2 4.7 %rim_product.18 = (f32[96,3072]{1,0:T(8,128)S(1)}, f32[7,96,128]{2,1,0:T(8,128)S(1)}, f32[2,96,128]{2,1,0:T(8,128)S(1)}, f32[2,96,128]{2,1,0:T(8,128)S(1)}, f32[4,96,128]{2,1,0:T(8,128)S(1)}) custom-call(s32[128]{0:T(128)S(1)} %copy-done.44, s32[128]{0:T(128)S(1)} %copy-done.45, s32[1]{0:T(128)} %get-tuple-element.205.count, s32[16]{0:T(128)S(1)} %bitcast.51, ...), custom_call_target="tpu_custom_call" | custom-call | flops 1073741824 | bytes 4194304 | tf_op jit(solution)/shard_map/rim_product/pallas_call | solution.py:482
  204.6 4.8 %own_product.19.refs_2_ = f32[96,4608]{1,0:T(8,128)S(1)} custom-call(s32[108]{0:T(128)S(1)} %copy-done.43, f32[96,3072]{1,0:T(8,128)S(1)} %get-tuple-element.350.refs_0_.refs_1_, f32[96,4608]{1,0:T(8,128)S(1)} %get-tuple-element.354.refs_0_.refs_1_, bf16[384,128,256]{2,1,0:T(8,128)(2,1)} %get-tuple-element.192.refs_2_.refs_3_.refs_1_), custom_call_target="tpu_custom_call" | custom-call | bytes 262144 | tf_op jit(solution)/shard_map/own_product/pallas_call | solution.py:392
  215.8 4.9 %rim_product.19 = (f32[96,4608]{1,0:T(8,128)}, f32[7,96,128]{2,1,0:T(8,128)S(1)}, f32[2,96,128]{2,1,0:T(8,128)S(1)}, f32[2,96,128]{2,1,0:T(8,128)S(1)}, f32[4,96,128]{2,1,0:T(8,128)S(1)}) custom-call(s32[128]{0:T(128)S(1)} %copy-done.49, s32[128]{0:T(128)S(1)} %copy-done.50, s32[1]{0:T(128)} %get-tuple-element.208.count, s32[16]{0:T(128)S(1)} %bitcast.56, ...), custom_call_target="tpu_custom_call" | custom-call | flops 1073741824 | bytes 4194304 | tf_op jit(solution)/shard_map/rim_product/pallas_call | solution.py:482
  227.6 4.0 %own_product.20.refs_0_ = f32[96,3072]{1,0:T(8,128)S(1)} custom-call(s32[96]{0:T(128)S(1)} %copy-done.42, f32[96,4608]{1,0:T(8,128)S(1)} %copy-done.3, f32[96,3072]{1,0:T(8,128)S(1)} %get-tuple-element.350.refs_0_.refs_1_, bf16[384,128,256]{2,1,0:T(8,128)(2,1)} %get-tuple-element.192.refs_2_.refs_3_.refs_1_), custom_call_target="tpu_custom_call" | custom-call | bytes 262144 | tf_op jit(solution)/shard_map/own_product/pallas_call | solution.py:392
  231.6 4.0 %own_product.21.refs_1_ = f32[96,3072]{1,0:T(8,128)S(1)} custom-call(s32[96]{0:T(128)S(1)} %copy-done.42, f32[96,4608]{1,0:T(8,128)S(1)} %add_add_fusion.refs_0_, f32[52,96,128]{2,1,0:T(8,128)S(1)} %constant_dynamic-update-slice_fusion.1.refs_1_.refs_8_, f32[96,3072]{1,0:T(8,128)S(1)} %copy-done, ...), custom_call_target="tpu_custom_call" | custom-call | bytes 262144 | tf_op jit(solution)/shard_map/own_product/pallas_call | solution.py:392
  238.2 4.6 %rim_product.21 = f32[96,3072]{1,0:T(8,128)} custom-call(s32[128]{0:T(128)S(1)} %copy-done.44, s32[128]{0:T(128)S(1)} %copy-done.45, s32[1]{0:T(128)} %get-tuple-element.205.count, s32[230]{0:T(256)S(1)} %bitcast.46, f32[96,3072]{1,0:T(8,128)S(1)} %own_product.21.refs_1_, bf16[384,128,256]{2,1,0:T(8,128)(2,1)} %get-tuple-element.192.refs_2_.refs_3_.refs_1_, ...), custom_call_target="tpu_custom_call" | custom-call | flops 1073741824 | bytes 4194304 | tf_op jit(solution)/shard_map/rim_product/pallas_call | solution.py:482
  242.8 5.6 %rim_product.20 = f32[96,3072]{1,0:T(8,128)} custom-call(s32[128]{0:T(128)S(1)} %copy-done.44, s32[128]{0:T(128)S(1)} %copy-done.45, s32[1]{0:T(128)} %get-tuple-element.205.count, f32[96,3072]{1,0:T(8,128)S(1)} %own_product.20.refs_0_, bf16[384,128,256]{2,1,0:T(8,128)(2,1)} %get-tuple-element.192.refs_2_.refs_3_.refs_1_, ...), custom_call_target="tpu_custom_call" | custom-call | flops 1073741824 | bytes 4194304 | tf_op jit(solution)/shard_map/rim_product/pallas_call | solution.py:482
  (348 shorter events, 130.6 us)
Async XLA Ops:
  7.6 36.7 %collective-permute-start.3 = (f32[2,96,128]{2,1,0:T(8,128)}, f32[2,96,128]{2,1,0:T(8,128)S(1)}, u32[]{:S(2)}, u32[]{:S(2)}) collective-permute-start(f32[2,96,128]{2,1,0:T(8,128)} %get-tuple-element.201), channel_id=1, source_target_pairs={{0,4},{1,5},{2,6},{3,7},{4,0},{5,1},{6,2},{7,3},{8,12},{9,13},{10,... | collective-permute-start | bytes 294920 | tf_op jit(solution)/shard_map/ppermute | solution.py:137
  12.1 32.2 %collective-permute-start.4 = (f32[8,96,128]{2,1,0:T(8,128)}, f32[8,96,128]{2,1,0:T(8,128)S(1)}, u32[]{:S(2)}, u32[]{:S(2)}) collective-permute-start(f32[8,96,128]{2,1,0:T(8,128)} %pad_maximum_fusion.2), channel_id=1, source_target_pairs={{0,8},{1,121},{2,10},{3,123},{4,12},{5,125},{6,14},{7,127},{8,16},... | collective-permute-start | bytes 1179656 | tf_op jit(solution)/shard_map/ppermute | solution.py:135
  22.8 21.5 %collective-permute-start.2 = (f32[4,96,128]{2,1,0:T(8,128)}, f32[4,96,128]{2,1,0:T(8,128)S(1)}, u32[]{:S(2)}, u32[]{:S(2)}) collective-permute-start(f32[4,96,128]{2,1,0:T(8,128)} %pad_maximum_fusion.22), channel_id=1, source_target_pairs={{0,2},{1,7},{2,4},{3,1},{4,6},{5,3},{6,0},{7,5},{8,10},{9,15},{10,... | collective-permute-start | bytes 589832 | tf_op jit(solution)/shard_map/ppermute | solution.py:136
  24.7 26.5 %collective-permute-start.9 = (f32[16,96,128]{2,1,0:T(8,128)}, f32[16,96,128]{2,1,0:T(8,128)S(1)}, u32[]{:S(2)}, u32[]{:S(2)}) collective-permute-start(f32[16,96,128]{2,1,0:T(8,128)} %pad_maximum_fusion), channel_id=1, source_target_pairs={{0,8},{1,121},{2,10},{3,123},{4,12},{5,125},{6,14},{7,127},{8,16},... | collective-permute-start | bytes 2359304 | tf_op jit(solution)/shard_map/ppermute | solution.py:135
  73.5 14.0 %collective-permute-start.18 = (f32[8,96,128]{2,1,0:T(8,128)S(1)}, f32[8,96,128]{2,1,0:T(8,128)S(1)}, u32[]{:S(2)}, u32[]{:S(2)}) collective-permute-start(f32[8,96,128]{2,1,0:T(8,128)S(1)} %pad_maximum_fusion.4), channel_id=1, source_target_pairs={{0,8},{1,121},{2,10},{3,123},{4,12},{5,125},{6,14},{7,127},{8,16},... | collective-permute-start | bytes 1179656 | tf_op jit(solution)/shard_map/ppermute | solution.py:135
  75.9 11.6 %collective-permute-start.16 = (f32[4,96,128]{2,1,0:T(8,128)S(1)}, f32[4,96,128]{2,1,0:T(8,128)S(1)}, u32[]{:S(2)}, u32[]{:S(2)}) collective-permute-start(f32[4,96,128]{2,1,0:T(8,128)S(1)} %pad_maximum_fusion.25), channel_id=1, source_target_pairs={{0,2},{1,7},{2,4},{3,1},{4,6},{5,3},{6,0},{7,5},{8,10},{9,15},{10,... | collective-permute-start | bytes 589832 | tf_op jit(solution)/shard_map/ppermute | solution.py:136
  77.5 10.0 %collective-permute-start.17 = (f32[2,96,128]{2,1,0:T(8,128)S(1)}, f32[2,96,128]{2,1,0:T(8,128)S(1)}, u32[]{:S(2)}, u32[]{:S(2)}) collective-permute-start(f32[2,96,128]{2,1,0:T(8,128)S(1)} %get-tuple-element.251), channel_id=1, source_target_pairs={{0,4},{1,5},{2,6},{3,7},{4,0},{5,1},{6,2},{7,3},{8,12},{9,13},{10,... | collective-permute-start | bytes 294920 | tf_op jit(solution)/shard_map/ppermute | solution.py:137
  95.0 12.1 %collective-permute-start.23 = (f32[8,96,128]{2,1,0:T(8,128)S(1)}, f32[8,96,128]{2,1,0:T(8,128)S(1)}, u32[]{:S(2)}, u32[]{:S(2)}) collective-permute-start(f32[8,96,128]{2,1,0:T(8,128)S(1)} %pad_maximum_fusion.5), channel_id=1, source_target_pairs={{0,8},{1,121},{2,10},{3,123},{4,12},{5,125},{6,14},{7,127},{8,16},... | collective-permute-start | bytes 1179656 | tf_op jit(solution)/shard_map/ppermute | solution.py:135
  96.3 10.8 %collective-permute-start.21 = (f32[4,96,128]{2,1,0:T(8,128)S(1)}, f32[4,96,128]{2,1,0:T(8,128)S(1)}, u32[]{:S(2)}, u32[]{:S(2)}) collective-permute-start(f32[4,96,128]{2,1,0:T(8,128)S(1)} %pad_maximum_fusion.26), channel_id=1, source_target_pairs={{0,2},{1,7},{2,4},{3,1},{4,6},{5,3},{6,0},{7,5},{8,10},{9,15},{10,... | collective-permute-start | bytes 589832 | tf_op jit(solution)/shard_map/ppermute | solution.py:136
  115.5 13.8 %collective-permute-start.28 = (f32[8,96,128]{2,1,0:T(8,128)S(1)}, f32[8,96,128]{2,1,0:T(8,128)S(1)}, u32[]{:S(2)}, u32[]{:S(2)}) collective-permute-start(f32[8,96,128]{2,1,0:T(8,128)S(1)} %pad_maximum_fusion.6), channel_id=1, source_target_pairs={{0,8},{1,121},{2,10},{3,123},{4,12},{5,125},{6,14},{7,127},{8,16},... | collective-permute-start | bytes 1179656 | tf_op jit(solution)/shard_map/ppermute | solution.py:135
  118.1 11.2 %collective-permute-start.26 = (f32[4,96,128]{2,1,0:T(8,128)S(1)}, f32[4,96,128]{2,1,0:T(8,128)S(1)}, u32[]{:S(2)}, u32[]{:S(2)}) collective-permute-start(f32[4,96,128]{2,1,0:T(8,128)S(1)} %pad_maximum_fusion.27), channel_id=1, source_target_pairs={{0,2},{1,7},{2,4},{3,1},{4,6},{5,3},{6,0},{7,5},{8,10},{9,15},{10,... | collective-permute-start | bytes 589832 | tf_op jit(solution)/shard_map/ppermute | solution.py:136
  119.3 10.0 %collective-permute-start.27 = (f32[2,96,128]{2,1,0:T(8,128)S(1)}, f32[2,96,128]{2,1,0:T(8,128)S(1)}, u32[]{:S(2)}, u32[]{:S(2)}) collective-permute-start(f32[2,96,128]{2,1,0:T(8,128)S(1)} %get-tuple-element.281), channel_id=1, source_target_pairs={{0,4},{1,5},{2,6},{3,7},{4,0},{5,1},{6,2},{7,3},{8,12},{9,13},{10,... | collective-permute-start | bytes 294920 | tf_op jit(solution)/shard_map/ppermute | solution.py:137
  136.6 12.1 %collective-permute-start.33 = (f32[8,96,128]{2,1,0:T(8,128)S(1)}, f32[8,96,128]{2,1,0:T(8,128)S(1)}, u32[]{:S(2)}, u32[]{:S(2)}) collective-permute-start(f32[8,96,128]{2,1,0:T(8,128)S(1)} %pad_maximum_fusion.7), channel_id=1, source_target_pairs={{0,8},{1,121},{2,10},{3,123},{4,12},{5,125},{6,14},{7,127},{8,16},... | collective-permute-start | bytes 1179656 | tf_op jit(solution)/shard_map/ppermute | solution.py:135
  138.3 10.4 %collective-permute-start.31 = (f32[4,96,128]{2,1,0:T(8,128)S(1)}, f32[4,96,128]{2,1,0:T(8,128)S(1)}, u32[]{:S(2)}, u32[]{:S(2)}) collective-permute-start(f32[4,96,128]{2,1,0:T(8,128)S(1)} %pad_maximum_fusion.28), channel_id=1, source_target_pairs={{0,2},{1,7},{2,4},{3,1},{4,6},{5,3},{6,0},{7,5},{8,10},{9,15},{10,... | collective-permute-start | bytes 589832 | tf_op jit(solution)/shard_map/ppermute | solution.py:136
  157.1 13.8 %collective-permute-start.38 = (f32[8,96,128]{2,1,0:T(8,128)S(1)}, f32[8,96,128]{2,1,0:T(8,128)S(1)}, u32[]{:S(2)}, u32[]{:S(2)}) collective-permute-start(f32[8,96,128]{2,1,0:T(8,128)S(1)} %pad_maximum_fusion.8), channel_id=1, source_target_pairs={{0,8},{1,121},{2,10},{3,123},{4,12},{5,125},{6,14},{7,127},{8,16},... | collective-permute-start | bytes 1179656 | tf_op jit(solution)/shard_map/ppermute | solution.py:135
  159.7 11.2 %collective-permute-start.36 = (f32[4,96,128]{2,1,0:T(8,128)S(1)}, f32[4,96,128]{2,1,0:T(8,128)S(1)}, u32[]{:S(2)}, u32[]{:S(2)}) collective-permute-start(f32[4,96,128]{2,1,0:T(8,128)S(1)} %pad_maximum_fusion.29), channel_id=1, source_target_pairs={{0,2},{1,7},{2,4},{3,1},{4,6},{5,3},{6,0},{7,5},{8,10},{9,15},{10,... | collective-permute-start | bytes 589832 | tf_op jit(solution)/shard_map/ppermute | solution.py:136
  161.0 10.0 %collective-permute-start.37 = (f32[2,96,128]{2,1,0:T(8,128)S(1)}, f32[2,96,128]{2,1,0:T(8,128)S(1)}, u32[]{:S(2)}, u32[]{:S(2)}) collective-permute-start(f32[2,96,128]{2,1,0:T(8,128)S(1)} %get-tuple-element.311), channel_id=1, source_target_pairs={{0,4},{1,5},{2,6},{3,7},{4,0},{5,1},{6,2},{7,3},{8,12},{9,13},{10,... | collective-permute-start | bytes 294920 | tf_op jit(solution)/shard_map/ppermute | solution.py:137
  178.3 12.1 %collective-permute-start.43 = (f32[8,96,128]{2,1,0:T(8,128)S(1)}, f32[8,96,128]{2,1,0:T(8,128)S(1)}, u32[]{:S(2)}, u32[]{:S(2)}) collective-permute-start(f32[8,96,128]{2,1,0:T(8,128)S(1)} %pad_maximum_fusion.9), channel_id=1, source_target_pairs={{0,8},{1,121},{2,10},{3,123},{4,12},{5,125},{6,14},{7,127},{8,16},... | collective-permute-start | bytes 1179656 | tf_op jit(solution)/shard_map/ppermute | solution.py:135
  180.0 10.4 %collective-permute-start.41 = (f32[4,96,128]{2,1,0:T(8,128)S(1)}, f32[4,96,128]{2,1,0:T(8,128)S(1)}, u32[]{:S(2)}, u32[]{:S(2)}) collective-permute-start(f32[4,96,128]{2,1,0:T(8,128)S(1)} %pad_maximum_fusion.30), channel_id=1, source_target_pairs={{0,2},{1,7},{2,4},{3,1},{4,6},{5,3},{6,0},{7,5},{8,10},{9,15},{10,... | collective-permute-start | bytes 589832 | tf_op jit(solution)/shard_map/ppermute | solution.py:136
  198.8 13.2 %collective-permute-start.48 = (f32[8,96,128]{2,1,0:T(8,128)S(1)}, f32[8,96,128]{2,1,0:T(8,128)S(1)}, u32[]{:S(2)}, u32[]{:S(2)}) collective-permute-start(f32[8,96,128]{2,1,0:T(8,128)S(1)} %pad_maximum_fusion.10), channel_id=1, source_target_pairs={{0,8},{1,121},{2,10},{3,123},{4,12},{5,125},{6,14},{7,127},{8,16},... | collective-permute-start | bytes 1179656 | tf_op jit(solution)/shard_map/ppermute | solution.py:135
  201.4 10.6 %collective-permute-start.46 = (f32[4,96,128]{2,1,0:T(8,128)S(1)}, f32[4,96,128]{2,1,0:T(8,128)S(1)}, u32[]{:S(2)}, u32[]{:S(2)}) collective-permute-start(f32[4,96,128]{2,1,0:T(8,128)S(1)} %pad_maximum_fusion.31), channel_id=1, source_target_pairs={{0,2},{1,7},{2,4},{3,1},{4,6},{5,3},{6,0},{7,5},{8,10},{9,15},{10,... | collective-permute-start | bytes 589832 | tf_op jit(solution)/shard_map/ppermute | solution.py:136
  221.0 14.5 %collective-permute-start.52 = (f32[2,96,128]{2,1,0:T(8,128)S(1)}, f32[2,96,128]{2,1,0:T(8,128)S(1)}, u32[]{:S(2)}, u32[]{:S(2)}) collective-permute-start(f32[2,96,128]{2,1,0:T(8,128)S(1)} %get-tuple-element.367), channel_id=1, source_target_pairs={{0,4},{1,5},{2,6},{3,7},{4,0},{5,1},{6,2},{7,3},{8,12},{9,13},{10,... | collective-permute-start | bytes 294920 | tf_op jit(solution)/shard_map/ppermute | solution.py:137
  222.5 13.1 %collective-permute-start.51 = (f32[4,96,128]{2,1,0:T(8,128)S(1)}, f32[4,96,128]{2,1,0:T(8,128)S(1)}, u32[]{:S(2)}, u32[]{:S(2)}) collective-permute-start(f32[4,96,128]{2,1,0:T(8,128)S(1)} %pad_maximum_fusion.32), channel_id=1, source_target_pairs={{0,2},{1,7},{2,4},{3,1},{4,6},{5,3},{6,0},{7,5},{8,10},{9,15},{10,... | collective-permute-start | bytes 589832 | tf_op jit(solution)/shard_map/ppermute | solution.py:136
  223.3 12.3 %collective-permute-start.53 = (f32[8,96,128]{2,1,0:T(8,128)S(1)}, f32[8,96,128]{2,1,0:T(8,128)S(1)}, u32[]{:S(2)}, u32[]{:S(2)}) collective-permute-start(f32[8,96,128]{2,1,0:T(8,128)S(1)} %pad_maximum_fusion.11), channel_id=1, source_target_pairs={{0,8},{1,121},{2,10},{3,123},{4,12},{5,125},{6,14},{7,127},{8,16},... | collective-permute-start | bytes 1179656 | tf_op jit(solution)/shard_map/ppermute | solution.py:135
  (87 other events, 396.5 us)

commit v4 on v3

--- a/solution.py
+++ b/solution.py
@@ -160,7 +160,7 @@
     return pl.CostEstimate(flops=flops, bytes_accessed=moved, transcendentals=0)
 
 
-GROUP = 6
+GROUP = 8
 ROOM = 128
 CUT = 12
 READS = 6

time: 249 us -> 249 us (level)
    unnamed x129 -> x137, local copies, waits for them, and re-layouts: 12.3 us -> 12.4 us
  transfers between devices with their start and end apart: 55 -> 55, of which waited for: 18 -> 17; matrix products, arithmetic and copies ran while one was open for 3% -> 3% of each run, Pallas kernels for 35% -> 36%
where the time goes in v4:
time: 249 us; the launch traced here: 248 us
  Pallas kernels  134 us (54%)
  starting transfers between devices  69.1 us (28%)
  waiting for transfers between devices  23.2 us (9%)
  local copies, waits for them, and re-layouts  15.9 us (6%)
  other arithmetic  3.37 us (1%)
  between operations  2.59 us (1%)
    pallas_call x11, Pallas kernels, rim_product(): pl.pallas_call(functools.partial(rim_kernel, targets=targets, side=side,...  48.1 us
    pallas_call x11, Pallas kernels, own_product(): pl.pallas_call(functools.partial(own_kernel, own=own, targets=targets, wi...  47.5 us
    ppermute x11, starting transfers between devices, travel(): lax.ppermute(jnp.concatenate([region, pre_in[3:]], axis=0), ('region', 's...  26.5 us
    pallas_call x7, Pallas kernels, edge_tracer_part(): pl.pallas_call(functools.partial(edge_tracer_kernel, start=start, blocks=...  21 us
    ppermute x11, starting transfers between devices, travel(): across_in = lax.ppermute(across, 'sub', ACROSS)  20.4 us
    pallas_call x1, Pallas kernels, split_weights(): pl.pallas_call(split_kernel, in_specs=[SMEM] * 3 + [HBM] * 2, out_specs=[...  12.8 us
    unnamed x137, local copies, waits for them, and re-layouts  12.4 us
    ppermute x11, waiting for transfers between devices, travel(): post_in = lax.ppermute(post, 'sub', MATES)  12.3 us
  transfers between devices with their start and end apart: 55, of which 17 were waited for; matrix products, arithmetic and copies ran while one was open for 3% of the time, Pallas kernels for 36%

profile of v4, /device:TPU:1, one launch (start us, length us, event | category | flops | bytes accessed | tf_op | source)
XLA Modules:
  0.0 248.0 jit_solution(13550994497450218864)
XLA Ops:
  13.9 6.2 %collective-permute-start.4 = (f32[8,96,128]{2,1,0:T(8,128)}, f32[8,96,128]{2,1,0:T(8,128)}, u32[]{:S(2)}, u32[]{:S(2)}) collective-permute-start(f32[8,96,128]{2,1,0:T(8,128)} %pad_maximum_fusion.2), channel_id=1, source_target_pairs={{0,8},{1,121},{2,10},{3,123},{4,12},{5,125},{6,14},{7,127},{8,16},... | collective-permute-start | bytes 1179656 | tf_op jit(solution)/shard_map/ppermute | solution.py:135
  25.6 12.8 %split_weights.1 = (bf16[388,128,256]{2,1,0:T(8,128)(2,1)}, s32[128]{0:T(128)}, s32[128]{0:T(128)}, s32[1]{0:T(128)}, s32[128]{0:T(128)}, /*index=5*/s32[128]{0:T(128)}, s32[1]{0:T(128)}) custom-call(s32[108]{0:T(128)} %reshape.39.g_pattern.pattern, s32[96]{0:T(128)} %reshape.40.d_pattern.pattern, s32[230]{0:T(256)} %bitcast.35, f32[108,128,128]{2,1,0:T(8,128)} %bitcast.58, ...), custom_call_target="tpu_custom_call" | custom-call | bytes 31457280 | tf_op jit(solution)/shard_map/split_weights/pallas_call | solution.py:250
  39.8 4.8 %own_product.11.refs_2_ = f32[96,4608]{1,0:T(8,128)S(1)} custom-call(s32[108]{0:T(128)S(1)} %copy-done.47, f32[96,3072]{1,0:T(8,128)S(1)} %copy-done.1, f32[96,4608]{1,0:T(8,128)S(1)} %copy-done.6, bf16[388,128,256]{2,1,0:T(8,128)(2,1)} %get-tuple-element.192.refs_2_.refs_3_.refs_1_), custom_call_target="tpu_custom_call" | custom-call | bytes 262144 | tf_op jit(solution)/shard_map/own_product/pallas_call | solution.py:392
  48.3 4.0 %rim_product.11 = (f32[96,4608]{1,0:T(8,128)S(1)}, f32[7,96,128]{2,1,0:T(8,128)S(1)}, f32[2,96,128]{2,1,0:T(8,128)S(1)}, f32[2,96,128]{2,1,0:T(8,128)S(1)}, f32[4,96,128]{2,1,0:T(8,128)S(1)}) custom-call(s32[128]{0:T(128)S(1)} %copy-done.53, s32[128]{0:T(128)S(1)} %copy-done.54, s32[1]{0:T(128)} %get-tuple-element.208.count, s32[16]{0:T(128)S(1)} %bitcast.52, ...), custom_call_target="tpu_custom_call" | custom-call | flops 1073741824 | bytes 4194304 | tf_op jit(solution)/shard_map/rim_product/pallas_call | solution.py:482
  57.7 3.9 %own_product.12.refs_2_ = f32[96,3072]{1,0:T(8,128)S(1)} custom-call(s32[96]{0:T(128)S(1)} %copy-done.46, f32[96,4608]{1,0:T(8,128)S(1)} %get-tuple-element.351.refs_0_.refs_1_, f32[96,3072]{1,0:T(8,128)S(1)} %copy-done.1, bf16[388,128,256]{2,1,0:T(8,128)(2,1)} %get-tuple-element.192.refs_2_.refs_3_.refs_1_), custom_call_target="tpu_custom_call" | custom-call | bytes 262144 | tf_op jit(solution)/shard_map/own_product/pallas_call | solution.py:392
  68.2 4.7 %rim_product.12 = (f32[96,3072]{1,0:T(8,128)S(1)}, f32[7,96,128]{2,1,0:T(8,128)S(1)}, f32[2,96,128]{2,1,0:T(8,128)S(1)}, f32[2,96,128]{2,1,0:T(8,128)S(1)}, f32[4,96,128]{2,1,0:T(8,128)S(1)}) custom-call(s32[128]{0:T(128)S(1)} %copy-done.48, s32[128]{0:T(128)S(1)} %copy-done.49, s32[1]{0:T(128)} %get-tuple-element.205.count, s32[16]{0:T(128)S(1)} %bitcast.48, ...), custom_call_target="tpu_custom_call" | custom-call | flops 1073741824 | bytes 4194304 | tf_op jit(solution)/shard_map/rim_product/pallas_call | solution.py:482
  80.7 4.8 %own_product.13.refs_2_ = f32[96,4608]{1,0:T(8,128)S(1)} custom-call(s32[108]{0:T(128)S(1)} %copy-done.47, f32[96,3072]{1,0:T(8,128)S(1)} %get-tuple-element.260.refs_0_.refs_1_, f32[96,4608]{1,0:T(8,128)S(1)} %get-tuple-element.351.refs_0_.refs_1_, bf16[388,128,256]{2,1,0:T(8,128)(2,1)} %get-tuple-element.192.refs_2_.refs_3_.refs_1_), custom_call_target="tpu_custom_call" | custom-call | bytes 262144 | tf_op jit(solution)/shard_map/own_product/pallas_call | solution.py:392
  90.7 3.5 %rim_product.13 = (f32[96,4608]{1,0:T(8,128)S(1)}, f32[7,96,128]{2,1,0:T(8,128)S(1)}, f32[2,96,128]{2,1,0:T(8,128)S(1)}, f32[2,96,128]{2,1,0:T(8,128)S(1)}, f32[4,96,128]{2,1,0:T(8,128)S(1)}) custom-call(s32[128]{0:T(128)S(1)} %copy-done.53, s32[128]{0:T(128)S(1)} %copy-done.54, s32[1]{0:T(128)} %get-tuple-element.208.count, s32[16]{0:T(128)S(1)} %bitcast.53, ...), custom_call_target="tpu_custom_call" | custom-call | flops 1073741824 | bytes 4194304 | tf_op jit(solution)/shard_map/rim_product/pallas_call | solution.py:482
  101.0 3.9 %own_product.14.refs_2_ = f32[96,3072]{1,0:T(8,128)S(1)} custom-call(s32[96]{0:T(128)S(1)} %copy-done.46, f32[96,4608]{1,0:T(8,128)S(1)} %get-tuple-element.352.refs_0_.refs_1_, f32[96,3072]{1,0:T(8,128)S(1)} %get-tuple-element.260.refs_0_.refs_1_, bf16[388,128,256]{2,1,0:T(8,128)(2,1)} %get-tuple-element.192.refs_2_.refs_3_.refs_1_), custom_call_target="tpu_custom_call" | custom-call | bytes 262144 | tf_op jit(solution)/shard_map/own_product/pallas_call | solution.py:392
  110.0 4.7 %rim_product.14 = (f32[96,3072]{1,0:T(8,128)S(1)}, f32[7,96,128]{2,1,0:T(8,128)S(1)}, f32[2,96,128]{2,1,0:T(8,128)S(1)}, f32[2,96,128]{2,1,0:T(8,128)S(1)}, f32[4,96,128]{2,1,0:T(8,128)S(1)}) custom-call(s32[128]{0:T(128)S(1)} %copy-done.48, s32[128]{0:T(128)S(1)} %copy-done.49, s32[1]{0:T(128)} %get-tuple-element.205.count, s32[16]{0:T(128)S(1)} %bitcast.49, ...), custom_call_target="tpu_custom_call" | custom-call | flops 1073741824 | bytes 4194304 | tf_op jit(solution)/shard_map/rim_product/pallas_call | solution.py:482
  122.4 4.8 %own_product.15.refs_2_ = f32[96,4608]{1,0:T(8,128)S(1)} custom-call(s32[108]{0:T(128)S(1)} %copy-done.47, f32[96,3072]{1,0:T(8,128)S(1)} %get-tuple-element.290.refs_0_.refs_1_, f32[96,4608]{1,0:T(8,128)S(1)} %get-tuple-element.352.refs_0_.refs_1_, bf16[388,128,256]{2,1,0:T(8,128)(2,1)} %get-tuple-element.192.refs_2_.refs_3_.refs_1_), custom_call_target="tpu_custom_call" | custom-call | bytes 262144 | tf_op jit(solution)/shard_map/own_product/pallas_call | solution.py:392
  132.2 3.5 %rim_product.15 = (f32[96,4608]{1,0:T(8,128)S(1)}, f32[7,96,128]{2,1,0:T(8,128)S(1)}, f32[2,96,128]{2,1,0:T(8,128)S(1)}, f32[2,96,128]{2,1,0:T(8,128)S(1)}, f32[4,96,128]{2,1,0:T(8,128)S(1)}) custom-call(s32[128]{0:T(128)S(1)} %copy-done.53, s32[128]{0:T(128)S(1)} %copy-done.54, s32[1]{0:T(128)} %get-tuple-element.208.count, s32[16]{0:T(128)S(1)} %bitcast.54, ...), custom_call_target="tpu_custom_call" | custom-call | flops 1073741824 | bytes 4194304 | tf_op jit(solution)/shard_map/rim_product/pallas_call | solution.py:482
  142.4 4.0 %own_product.16.refs_2_ = f32[96,3072]{1,0:T(8,128)S(1)} custom-call(s32[96]{0:T(128)S(1)} %copy-done.46, f32[96,4608]{1,0:T(8,128)S(1)} %get-tuple-element.353.refs_0_.refs_1_, f32[96,3072]{1,0:T(8,128)S(1)} %get-tuple-element.290.refs_0_.refs_1_, bf16[388,128,256]{2,1,0:T(8,128)(2,1)} %get-tuple-element.192.refs_2_.refs_3_.refs_1_), custom_call_target="tpu_custom_call" | custom-call | bytes 262144 | tf_op jit(solution)/shard_map/own_product/pallas_call | solution.py:392
  151.5 4.7 %rim_product.16 = (f32[96,3072]{1,0:T(8,128)S(1)}, f32[7,96,128]{2,1,0:T(8,128)S(1)}, f32[2,96,128]{2,1,0:T(8,128)S(1)}, f32[2,96,128]{2,1,0:T(8,128)S(1)}, f32[4,96,128]{2,1,0:T(8,128)S(1)}) custom-call(s32[128]{0:T(128)S(1)} %copy-done.48, s32[128]{0:T(128)S(1)} %copy-done.49, s32[1]{0:T(128)} %get-tuple-element.205.count, s32[16]{0:T(128)S(1)} %bitcast.50, ...), custom_call_target="tpu_custom_call" | custom-call | flops 1073741824 | bytes 4194304 | tf_op jit(solution)/shard_map/rim_product/pallas_call | solution.py:482
  163.8 4.8 %own_product.17.refs_2_ = f32[96,4608]{1,0:T(8,128)S(1)} custom-call(s32[108]{0:T(128)S(1)} %copy-done.47, f32[96,3072]{1,0:T(8,128)S(1)} %get-tuple-element.320.refs_0_.refs_1_, f32[96,4608]{1,0:T(8,128)S(1)} %get-tuple-element.353.refs_0_.refs_1_, bf16[388,128,256]{2,1,0:T(8,128)(2,1)} %get-tuple-element.192.refs_2_.refs_3_.refs_1_), custom_call_target="tpu_custom_call" | custom-call | bytes 262144 | tf_op jit(solution)/shard_map/own_product/pallas_call | solution.py:392
  184.1 4.0 %own_product.18.refs_2_ = f32[96,3072]{1,0:T(8,128)S(1)} custom-call(s32[96]{0:T(128)S(1)} %copy-done.46, f32[96,4608]{1,0:T(8,128)S(1)} %get-tuple-element.354.refs_0_.refs_1_, f32[96,3072]{1,0:T(8,128)S(1)} %get-tuple-element.320.refs_0_.refs_1_, bf16[388,128,256]{2,1,0:T(8,128)(2,1)} %get-tuple-element.192.refs_2_.refs_3_.refs_1_), custom_call_target="tpu_custom_call" | custom-call | bytes 262144 | tf_op jit(solution)/shard_map/own_product/pallas_call | solution.py:392
  193.2 4.7 %rim_product.18 = (f32[96,3072]{1,0:T(8,128)S(1)}, f32[7,96,128]{2,1,0:T(8,128)S(1)}, f32[2,96,128]{2,1,0:T(8,128)S(1)}, f32[2,96,128]{2,1,0:T(8,128)S(1)}, f32[4,96,128]{2,1,0:T(8,128)S(1)}) custom-call(s32[128]{0:T(128)S(1)} %copy-done.48, s32[128]{0:T(128)S(1)} %copy-done.49, s32[1]{0:T(128)} %get-tuple-element.205.count, s32[16]{0:T(128)S(1)} %bitcast.51, ...), custom_call_target="tpu_custom_call" | custom-call | flops 1073741824 | bytes 4194304 | tf_op jit(solution)/shard_map/rim_product/pallas_call | solution.py:482
  205.5 4.7 %own_product.19.refs_2_ = f32[96,4608]{1,0:T(8,128)S(1)} custom-call(s32[108]{0:T(128)S(1)} %copy-done.47, f32[96,3072]{1,0:T(8,128)S(1)} %get-tuple-element.350.refs_0_.refs_1_, f32[96,4608]{1,0:T(8,128)S(1)} %get-tuple-element.354.refs_0_.refs_1_, bf16[388,128,256]{2,1,0:T(8,128)(2,1)} %get-tuple-element.192.refs_2_.refs_3_.refs_1_), custom_call_target="tpu_custom_call" | custom-call | bytes 262144 | tf_op jit(solution)/shard_map/own_product/pallas_call | solution.py:392
  216.0 4.8 %rim_product.19 = (f32[96,4608]{1,0:T(8,128)}, f32[7,96,128]{2,1,0:T(8,128)S(1)}, f32[2,96,128]{2,1,0:T(8,128)S(1)}, f32[2,96,128]{2,1,0:T(8,128)S(1)}, f32[4,96,128]{2,1,0:T(8,128)S(1)}) custom-call(s32[128]{0:T(128)S(1)} %copy-done.53, s32[128]{0:T(128)S(1)} %copy-done.54, s32[1]{0:T(128)} %get-tuple-element.208.count, s32[16]{0:T(128)S(1)} %bitcast.56, ...), custom_call_target="tpu_custom_call" | custom-call | flops 1073741824 | bytes 4194304 | tf_op jit(solution)/shard_map/rim_product/pallas_call | solution.py:482
  223.4 3.7 %collective-permute-start.53 = (f32[8,96,128]{2,1,0:T(8,128)S(1)}, f32[8,96,128]{2,1,0:T(8,128)S(1)}, u32[]{:S(2)}, u32[]{:S(2)}) collective-permute-start(f32[8,96,128]{2,1,0:T(8,128)S(1)} %pad_maximum_fusion.11), channel_id=1, source_target_pairs={{0,8},{1,121},{2,10},{3,123},{4,12},{5,125},{6,14},{7,127},{8,16},... | collective-permute-start | bytes 1179656 | tf_op jit(solution)/shard_map/ppermute | solution.py:135
  227.7 4.0 %own_product.20.refs_0_ = f32[96,3072]{1,0:T(8,128)S(1)} custom-call(s32[96]{0:T(128)S(1)} %copy-done.46, f32[96,4608]{1,0:T(8,128)S(1)} %copy-done.3, f32[96,3072]{1,0:T(8,128)S(1)} %get-tuple-element.350.refs_0_.refs_1_, bf16[388,128,256]{2,1,0:T(8,128)(2,1)} %get-tuple-element.192.refs_2_.refs_3_.refs_1_), custom_call_target="tpu_custom_call" | custom-call | bytes 262144 | tf_op jit(solution)/shard_map/own_product/pallas_call | solution.py:392
  231.7 4.0 %own_product.21.refs_1_ = f32[96,3072]{1,0:T(8,128)S(1)} custom-call(s32[96]{0:T(128)S(1)} %copy-done.46, f32[96,4608]{1,0:T(8,128)S(1)} %add_add_fusion.refs_0_, f32[52,96,128]{2,1,0:T(8,128)S(1)} %constant_dynamic-update-slice_fusion.1.refs_1_.refs_8_, f32[96,3072]{1,0:T(8,128)S(1)} %copy-done.2, ...), custom_call_target="tpu_custom_call" | custom-call | bytes 262144 | tf_op jit(solution)/shard_map/own_product/pallas_call | solution.py:392
  237.8 4.5 %rim_product.21 = f32[96,3072]{1,0:T(8,128)} custom-call(s32[128]{0:T(128)S(1)} %copy-done.48, s32[128]{0:T(128)S(1)} %copy-done.49, s32[1]{0:T(128)} %get-tuple-element.205.count, s32[230]{0:T(256)S(1)} %bitcast.46, f32[96,3072]{1,0:T(8,128)S(1)} %own_product.21.refs_1_, bf16[388,128,256]{2,1,0:T(8,128)(2,1)} %get-tuple-element.192.refs_2_.refs_3_.refs_1_, ...), custom_call_target="tpu_custom_call" | custom-call | flops 1073741824 | bytes 4194304 | tf_op jit(solution)/shard_map/rim_product/pallas_call | solution.py:482
  242.3 5.5 %rim_product.20 = f32[96,3072]{1,0:T(8,128)} custom-call(s32[128]{0:T(128)S(1)} %copy-done.48, s32[128]{0:T(128)S(1)} %copy-done.49, s32[1]{0:T(128)} %get-tuple-element.205.count, f32[96,3072]{1,0:T(8,128)S(1)} %own_product.20.refs_0_, bf16[388,128,256]{2,1,0:T(8,128)(2,1)} %get-tuple-element.192.refs_2_.refs_3_.refs_1_, ...), custom_call_target="tpu_custom_call" | custom-call | flops 1073741824 | bytes 4194304 | tf_op jit(solution)/shard_map/rim_product/pallas_call | solution.py:482
  (356 shorter events, 130.7 us)
Async XLA Ops:
  9.4 35.2 %collective-permute-start.3 = (f32[2,96,128]{2,1,0:T(8,128)}, f32[2,96,128]{2,1,0:T(8,128)S(1)}, u32[]{:S(2)}, u32[]{:S(2)}) collective-permute-start(f32[2,96,128]{2,1,0:T(8,128)} %get-tuple-element.201), channel_id=1, source_target_pairs={{0,4},{1,5},{2,6},{3,7},{4,0},{5,1},{6,2},{7,3},{8,12},{9,13},{10,... | collective-permute-start | bytes 294920 | tf_op jit(solution)/shard_map/ppermute | solution.py:137
  13.9 30.8 %collective-permute-start.4 = (f32[8,96,128]{2,1,0:T(8,128)}, f32[8,96,128]{2,1,0:T(8,128)}, u32[]{:S(2)}, u32[]{:S(2)}) collective-permute-start(f32[8,96,128]{2,1,0:T(8,128)} %pad_maximum_fusion.2), channel_id=1, source_target_pairs={{0,8},{1,121},{2,10},{3,123},{4,12},{5,125},{6,14},{7,127},{8,16},... | collective-permute-start | bytes 1179656 | tf_op jit(solution)/shard_map/ppermute | solution.py:135
  23.2 21.5 %collective-permute-start.2 = (f32[4,96,128]{2,1,0:T(8,128)S(1)}, f32[4,96,128]{2,1,0:T(8,128)S(1)}, u32[]{:S(2)}, u32[]{:S(2)}) collective-permute-start(f32[4,96,128]{2,1,0:T(8,128)S(1)} %pad_maximum_fusion.22), channel_id=1, source_target_pairs={{0,2},{1,7},{2,4},{3,1},{4,6},{5,3},{6,0},{7,5},{8,10},{9,15},{10,... | collective-permute-start | bytes 589832 | tf_op jit(solution)/shard_map/ppermute | solution.py:136
  25.1 27.6 %collective-permute-start.9 = (f32[16,96,128]{2,1,0:T(8,128)}, f32[16,96,128]{2,1,0:T(8,128)S(1)}, u32[]{:S(2)}, u32[]{:S(2)}) collective-permute-start(f32[16,96,128]{2,1,0:T(8,128)} %pad_maximum_fusion), channel_id=1, source_target_pairs={{0,8},{1,121},{2,10},{3,123},{4,12},{5,125},{6,14},{7,127},{8,16},... | collective-permute-start | bytes 2359304 | tf_op jit(solution)/shard_map/ppermute | solution.py:135
  74.7 14.1 %collective-permute-start.18 = (f32[8,96,128]{2,1,0:T(8,128)S(1)}, f32[8,96,128]{2,1,0:T(8,128)S(1)}, u32[]{:S(2)}, u32[]{:S(2)}) collective-permute-start(f32[8,96,128]{2,1,0:T(8,128)S(1)} %pad_maximum_fusion.4), channel_id=1, source_target_pairs={{0,8},{1,121},{2,10},{3,123},{4,12},{5,125},{6,14},{7,127},{8,16},... | collective-permute-start | bytes 1179656 | tf_op jit(solution)/shard_map/ppermute | solution.py:135
  77.3 11.4 %collective-permute-start.16 = (f32[4,96,128]{2,1,0:T(8,128)S(1)}, f32[4,96,128]{2,1,0:T(8,128)S(1)}, u32[]{:S(2)}, u32[]{:S(2)}) collective-permute-start(f32[4,96,128]{2,1,0:T(8,128)S(1)} %pad_maximum_fusion.25), channel_id=1, source_target_pairs={{0,2},{1,7},{2,4},{3,1},{4,6},{5,3},{6,0},{7,5},{8,10},{9,15},{10,... | collective-permute-start | bytes 589832 | tf_op jit(solution)/shard_map/ppermute | solution.py:136
  78.8 10.0 %collective-permute-start.17 = (f32[2,96,128]{2,1,0:T(8,128)S(1)}, f32[2,96,128]{2,1,0:T(8,128)S(1)}, u32[]{:S(2)}, u32[]{:S(2)}) collective-permute-start(f32[2,96,128]{2,1,0:T(8,128)S(1)} %get-tuple-element.251), channel_id=1, source_target_pairs={{0,4},{1,5},{2,6},{3,7},{4,0},{5,1},{6,2},{7,3},{8,12},{9,13},{10,... | collective-permute-start | bytes 294920 | tf_op jit(solution)/shard_map/ppermute | solution.py:137
  96.1 12.1 %collective-permute-start.23 = (f32[8,96,128]{2,1,0:T(8,128)S(1)}, f32[8,96,128]{2,1,0:T(8,128)S(1)}, u32[]{:S(2)}, u32[]{:S(2)}) collective-permute-start(f32[8,96,128]{2,1,0:T(8,128)S(1)} %pad_maximum_fusion.5), channel_id=1, source_target_pairs={{0,8},{1,121},{2,10},{3,123},{4,12},{5,125},{6,14},{7,127},{8,16},... | collective-permute-start | bytes 1179656 | tf_op jit(solution)/shard_map/ppermute | solution.py:135
  97.6 10.6 %collective-permute-start.21 = (f32[4,96,128]{2,1,0:T(8,128)S(1)}, f32[4,96,128]{2,1,0:T(8,128)S(1)}, u32[]{:S(2)}, u32[]{:S(2)}) collective-permute-start(f32[4,96,128]{2,1,0:T(8,128)S(1)} %pad_maximum_fusion.26), channel_id=1, source_target_pairs={{0,2},{1,7},{2,4},{3,1},{4,6},{5,3},{6,0},{7,5},{8,10},{9,15},{10,... | collective-permute-start | bytes 589832 | tf_op jit(solution)/shard_map/ppermute | solution.py:136
  116.5 13.8 %collective-permute-start.28 = (f32[8,96,128]{2,1,0:T(8,128)S(1)}, f32[8,96,128]{2,1,0:T(8,128)S(1)}, u32[]{:S(2)}, u32[]{:S(2)}) collective-permute-start(f32[8,96,128]{2,1,0:T(8,128)S(1)} %pad_maximum_fusion.6), channel_id=1, source_target_pairs={{0,8},{1,121},{2,10},{3,123},{4,12},{5,125},{6,14},{7,127},{8,16},... | collective-permute-start | bytes 1179656 | tf_op jit(solution)/shard_map/ppermute | solution.py:135
  119.1 11.2 %collective-permute-start.26 = (f32[4,96,128]{2,1,0:T(8,128)S(1)}, f32[4,96,128]{2,1,0:T(8,128)S(1)}, u32[]{:S(2)}, u32[]{:S(2)}) collective-permute-start(f32[4,96,128]{2,1,0:T(8,128)S(1)} %pad_maximum_fusion.27), channel_id=1, source_target_pairs={{0,2},{1,7},{2,4},{3,1},{4,6},{5,3},{6,0},{7,5},{8,10},{9,15},{10,... | collective-permute-start | bytes 589832 | tf_op jit(solution)/shard_map/ppermute | solution.py:136
  120.4 10.0 %collective-permute-start.27 = (f32[2,96,128]{2,1,0:T(8,128)S(1)}, f32[2,96,128]{2,1,0:T(8,128)S(1)}, u32[]{:S(2)}, u32[]{:S(2)}) collective-permute-start(f32[2,96,128]{2,1,0:T(8,128)S(1)} %get-tuple-element.281), channel_id=1, source_target_pairs={{0,4},{1,5},{2,6},{3,7},{4,0},{5,1},{6,2},{7,3},{8,12},{9,13},{10,... | collective-permute-start | bytes 294920 | tf_op jit(solution)/shard_map/ppermute | solution.py:137
  137.5 12.1 %collective-permute-start.33 = (f32[8,96,128]{2,1,0:T(8,128)S(1)}, f32[8,96,128]{2,1,0:T(8,128)S(1)}, u32[]{:S(2)}, u32[]{:S(2)}) collective-permute-start(f32[8,96,128]{2,1,0:T(8,128)S(1)} %pad_maximum_fusion.7), channel_id=1, source_target_pairs={{0,8},{1,121},{2,10},{3,123},{4,12},{5,125},{6,14},{7,127},{8,16},... | collective-permute-start | bytes 1179656 | tf_op jit(solution)/shard_map/ppermute | solution.py:135
  139.2 10.4 %collective-permute-start.31 = (f32[4,96,128]{2,1,0:T(8,128)S(1)}, f32[4,96,128]{2,1,0:T(8,128)S(1)}, u32[]{:S(2)}, u32[]{:S(2)}) collective-permute-start(f32[4,96,128]{2,1,0:T(8,128)S(1)} %pad_maximum_fusion.28), channel_id=1, source_target_pairs={{0,2},{1,7},{2,4},{3,1},{4,6},{5,3},{6,0},{7,5},{8,10},{9,15},{10,... | collective-permute-start | bytes 589832 | tf_op jit(solution)/shard_map/ppermute | solution.py:136
  158.0 13.8 %collective-permute-start.38 = (f32[8,96,128]{2,1,0:T(8,128)S(1)}, f32[8,96,128]{2,1,0:T(8,128)S(1)}, u32[]{:S(2)}, u32[]{:S(2)}) collective-permute-start(f32[8,96,128]{2,1,0:T(8,128)S(1)} %pad_maximum_fusion.8), channel_id=1, source_target_pairs={{0,8},{1,121},{2,10},{3,123},{4,12},{5,125},{6,14},{7,127},{8,16},... | collective-permute-start | bytes 1179656 | tf_op jit(solution)/shard_map/ppermute | solution.py:135
  160.6 11.2 %collective-permute-start.36 = (f32[4,96,128]{2,1,0:T(8,128)S(1)}, f32[4,96,128]{2,1,0:T(8,128)S(1)}, u32[]{:S(2)}, u32[]{:S(2)}) collective-permute-start(f32[4,96,128]{2,1,0:T(8,128)S(1)} %pad_maximum_fusion.29), channel_id=1, source_target_pairs={{0,2},{1,7},{2,4},{3,1},{4,6},{5,3},{6,0},{7,5},{8,10},{9,15},{10,... | collective-permute-start | bytes 589832 | tf_op jit(solution)/shard_map/ppermute | solution.py:136
  161.8 10.0 %collective-permute-start.37 = (f32[2,96,128]{2,1,0:T(8,128)S(1)}, f32[2,96,128]{2,1,0:T(8,128)S(1)}, u32[]{:S(2)}, u32[]{:S(2)}) collective-permute-start(f32[2,96,128]{2,1,0:T(8,128)S(1)} %get-tuple-element.311), channel_id=1, source_target_pairs={{0,4},{1,5},{2,6},{3,7},{4,0},{5,1},{6,2},{7,3},{8,12},{9,13},{10,... | collective-permute-start | bytes 294920 | tf_op jit(solution)/shard_map/ppermute | solution.py:137
  179.2 12.1 %collective-permute-start.43 = (f32[8,96,128]{2,1,0:T(8,128)S(1)}, f32[8,96,128]{2,1,0:T(8,128)S(1)}, u32[]{:S(2)}, u32[]{:S(2)}) collective-permute-start(f32[8,96,128]{2,1,0:T(8,128)S(1)} %pad_maximum_fusion.9), channel_id=1, source_target_pairs={{0,8},{1,121},{2,10},{3,123},{4,12},{5,125},{6,14},{7,127},{8,16},... | collective-permute-start | bytes 1179656 | tf_op jit(solution)/shard_map/ppermute | solution.py:135
  180.9 10.4 %collective-permute-start.41 = (f32[4,96,128]{2,1,0:T(8,128)S(1)}, f32[4,96,128]{2,1,0:T(8,128)S(1)}, u32[]{:S(2)}, u32[]{:S(2)}) collective-permute-start(f32[4,96,128]{2,1,0:T(8,128)S(1)} %pad_maximum_fusion.30), channel_id=1, source_target_pairs={{0,2},{1,7},{2,4},{3,1},{4,6},{5,3},{6,0},{7,5},{8,10},{9,15},{10,... | collective-permute-start | bytes 589832 | tf_op jit(solution)/shard_map/ppermute | solution.py:136
  199.7 12.6 %collective-permute-start.48 = (f32[8,96,128]{2,1,0:T(8,128)S(1)}, f32[8,96,128]{2,1,0:T(8,128)S(1)}, u32[]{:S(2)}, u32[]{:S(2)}) collective-permute-start(f32[8,96,128]{2,1,0:T(8,128)S(1)} %pad_maximum_fusion.10), channel_id=1, source_target_pairs={{0,8},{1,121},{2,10},{3,123},{4,12},{5,125},{6,14},{7,127},{8,16},... | collective-permute-start | bytes 1179656 | tf_op jit(solution)/shard_map/ppermute | solution.py:135
  202.3 9.9 %collective-permute-start.46 = (f32[4,96,128]{2,1,0:T(8,128)S(1)}, f32[4,96,128]{2,1,0:T(8,128)S(1)}, u32[]{:S(2)}, u32[]{:S(2)}) collective-permute-start(f32[4,96,128]{2,1,0:T(8,128)S(1)} %pad_maximum_fusion.31), channel_id=1, source_target_pairs={{0,2},{1,7},{2,4},{3,1},{4,6},{5,3},{6,0},{7,5},{8,10},{9,15},{10,... | collective-permute-start | bytes 589832 | tf_op jit(solution)/shard_map/ppermute | solution.py:136
  221.1 14.6 %collective-permute-start.52 = (f32[2,96,128]{2,1,0:T(8,128)S(1)}, f32[2,96,128]{2,1,0:T(8,128)S(1)}, u32[]{:S(2)}, u32[]{:S(2)}) collective-permute-start(f32[2,96,128]{2,1,0:T(8,128)S(1)} %get-tuple-element.367), channel_id=1, source_target_pairs={{0,4},{1,5},{2,6},{3,7},{4,0},{5,1},{6,2},{7,3},{8,12},{9,13},{10,... | collective-permute-start | bytes 294920 | tf_op jit(solution)/shard_map/ppermute | solution.py:137
  222.6 13.1 %collective-permute-start.51 = (f32[4,96,128]{2,1,0:T(8,128)S(1)}, f32[4,96,128]{2,1,0:T(8,128)S(1)}, u32[]{:S(2)}, u32[]{:S(2)}) collective-permute-start(f32[4,96,128]{2,1,0:T(8,128)S(1)} %pad_maximum_fusion.32), channel_id=1, source_target_pairs={{0,2},{1,7},{2,4},{3,1},{4,6},{5,3},{6,0},{7,5},{8,10},{9,15},{10,... | collective-permute-start | bytes 589832 | tf_op jit(solution)/shard_map/ppermute | solution.py:136
  223.4 12.3 %collective-permute-start.53 = (f32[8,96,128]{2,1,0:T(8,128)S(1)}, f32[8,96,128]{2,1,0:T(8,128)S(1)}, u32[]{:S(2)}, u32[]{:S(2)}) collective-permute-start(f32[8,96,128]{2,1,0:T(8,128)S(1)} %pad_maximum_fusion.11), channel_id=1, source_target_pairs={{0,8},{1,121},{2,10},{3,123},{4,12},{5,125},{6,14},{7,127},{8,16},... | collective-permute-start | bytes 1179656 | tf_op jit(solution)/shard_map/ppermute | solution.py:135
  (91 other events, 419.0 us)
